TPU v7x, 512 devices: a whole 4x8x8 slice. The times are simulated.
512 devices in a mesh: rows: 128 (over z, x_hi, y), grp: 4 (over x_lo, core).
Axes of the slice: x: 4 (x_hi: 2, x_lo: 2; x = x_hi * 2 + x_lo), y: 8, z: 8, core: 2. Of those that a mesh axis runs over, the one named last changes fastest.
Arguments:
- tokens: bfloat16 [512, 512, 256], P('rows', 'grp'), may hold values from -36 to 36
- norm_gain: float32 [256], replicated, may hold values from 0.1 to 1.9
- qkv_weight: bfloat16 [256, 768], replicated, may hold values from -0.375 to 0.375
- head_scale: float32 [4], replicated, may hold values from 2 to 12
- out_weight: bfloat16 [256, 256], replicated, may hold values from -0.375 to 0.375
- cotangent: bfloat16 [512, 512, 256], P('rows', 'grp'), may hold values from -6 to 6
Outputs:
- output: bfloat16 [512, 512, 256], P('rows', 'grp')
- token_grad: float32 [512, 512, 256], P('rows', 'grp')
- gain_grad: float32 [256], replicated
- qkv_grad: float32 [256, 768], replicated
- scale_grad: float32 [4], replicated
- out_grad: float32 [256, 256], replicated
All inputs are finite; a program needn't handle non-finite values.
Results may differ from a plain program's by a relative error of at most 0.011.
Values may be sent and summed in bfloat16 or wider, within the bound.
No kernel may reach another device: no remote copies, remote signals or barrier semaphores. Data moves between devices by JAX's collectives and lax.ppermute only.
A program may use at most 64 MiB of HBM per device.

v0:
```python
import math

import jax
import jax.numpy as jnp
from jax import lax
from jax.sharding import PartitionSpec as P

HEADS = 4
HEAD = 64
C = 256
WIN = 3
BR = 4
BC = 128


EPS = 1e-06


def with_halo(shard, sides, width):
    for axis, dim in sides:
        size, length = (lax.axis_size(axis), shard.shape[dim])
        up = [(i, (i + 1) % size) for i in range(size - 1)]
        down = [(j, i) for i, j in up]
        last = lax.slice_in_dim(shard, length - width, length, axis=dim)
        leading = lax.slice_in_dim(shard, 0, width, axis=dim)
        before = lax.ppermute(last, axis, up)
        after = lax.ppermute(leading, axis, down)
        shard = jnp.concatenate([before, shard, after], axis=dim)
    return shard


def own_slice(array, row_at, col_at, tile_cols):
    starts = (row_at, col_at) + (0,) * (array.ndim - 2)
    return lax.dynamic_slice(array, starts, (1, tile_cols) + array.shape[2:])[0]


def near_slice(array, row_at, col_at, span_rows, near_cols):
    starts = (row_at, col_at) + (0,) * (array.ndim - 2)
    piece = lax.dynamic_slice(array, starts, (span_rows, near_cols) + array.shape[2:])
    return piece.reshape((span_rows * near_cols,) + array.shape[2:])


def body(tokens, norm_gain, qkv_weight, head_scale, out_weight, cotangent):
    rows_total = BR * lax.axis_size("rows")
    cols_total = BC * lax.axis_size("grp")
    row_start = lax.axis_index("rows") * BR
    col_start = lax.axis_index("grp") * BC
    tok_f32 = tokens.astype(jnp.float32)
    row_inverse = lax.rsqrt(jnp.mean(tok_f32 * tok_f32, axis=-1, keepdims=True) + EPS)
    normed = (tok_f32 * row_inverse * norm_gain).astype(jnp.bfloat16)
    projected = jnp.dot(normed.reshape(-1, C), qkv_weight, preferred_element_type=jnp.float32)
    projected = projected.reshape(BR, BC, 3, HEADS, HEAD)
    query_raw = projected[:, :, 0]
    key_raw = projected[:, :, 1]
    value_raw = projected[:, :, 2]
    factor = (head_scale / HEAD)[:, None]
    query_inverse = lax.rsqrt(jnp.mean(query_raw * query_raw, axis=-1, keepdims=True) + EPS)
    key_inverse = lax.rsqrt(jnp.mean(key_raw * key_raw, axis=-1, keepdims=True) + EPS)
    query_heads = (query_raw * query_inverse * factor).astype(jnp.bfloat16)
    key_heads = (key_raw * key_inverse).astype(jnp.bfloat16)
    value_heads = value_raw.astype(jnp.bfloat16)
    grad_att = jnp.dot(cotangent.reshape(-1, C), out_weight.T, preferred_element_type=jnp.float32)
    grad_att = grad_att.astype(jnp.bfloat16).reshape(BR, BC, HEADS, HEAD)
    key_value = jnp.concatenate(
        [key_heads.reshape(BR, BC, C), value_heads.reshape(BR, BC, C)], axis=-1
    )
    kv_outer = with_halo(key_value, (("rows", 0), ("grp", 1)), WIN)
    ext_rows = row_start - WIN + jnp.arange(BR + 2 * WIN)
    ext_cols = col_start - WIN + jnp.arange(BC + 2 * WIN)
    valid_outer = (
        ((ext_rows >= 0) & (ext_rows < rows_total))[:, None]
        & ((ext_cols >= 0) & (ext_cols < cols_total))[None, :]
    ).astype(jnp.float32)
    span_rows = 2 * WIN + 1
    tile_cols = min(BC, 128)
    tile_count = BC // tile_cols
    block_count = BR * tile_count
    near_cols = tile_cols + 2 * WIN
    near_count = span_rows * near_cols
    near_index = jnp.tile(jnp.arange(near_cols), span_rows)
    offset = near_index[None, :] - jnp.arange(tile_cols)[:, None]
    band_mask = ((offset >= 0) & (offset <= 2 * WIN)).astype(jnp.float32)
    block_ids = jnp.arange(block_count, dtype=jnp.int32)

    def query_pass(block_id):
        row_at = block_id // tile_count
        col_at = block_id % tile_count * tile_cols
        q_own = own_slice(query_heads, row_at, col_at, tile_cols)
        d_own = own_slice(grad_att, row_at, col_at, tile_cols)
        near_kv = near_slice(kv_outer, row_at, col_at, span_rows, near_cols)
        k_near = near_kv[:, :C].reshape(near_count, HEADS, HEAD)
        v_near = near_kv[:, C:].reshape(near_count, HEADS, HEAD)
        allowed = band_mask * near_slice(valid_outer, row_at, col_at, span_rows, near_cols)[None, :]
        scores = jnp.einsum("qhd,khd->hqk", q_own, k_near, preferred_element_type=jnp.float32)
        exp_scores = jnp.exp(scores) * allowed[None]
        denom_sum = jnp.sum(exp_scores, axis=-1)
        attend = exp_scores / denom_sum[..., None]
        attend_b = attend.astype(jnp.bfloat16)
        attended = jnp.einsum("hqk,khd->qhd", attend_b, v_near, preferred_element_type=jnp.float32)
        grad_probs = jnp.einsum("qhd,khd->hqk", d_own, v_near, preferred_element_type=jnp.float32)
        delta_sum = jnp.sum(attend * grad_probs, axis=-1)
        grad_scores = (attend * (grad_probs - delta_sum[..., None])).astype(jnp.bfloat16)
        grad_query = jnp.einsum(
            "hqk,khd->qhd", grad_scores, k_near, preferred_element_type=jnp.float32
        )
        results = (attended.astype(jnp.bfloat16), denom_sum.T, delta_sum.T, grad_query)
        return results

    stacked = lax.map(lambda block_id: query_pass(block_id), block_ids)
    attended = stacked[0].reshape(BR, BC, C)
    denoms = stacked[1]
    deltas = stacked[2]
    grad_query = stacked[3]
    output = (
        tok_f32
        + jnp.dot(attended.reshape(-1, C), out_weight, preferred_element_type=jnp.float32).reshape(
            BR, BC, C
        )
    ).astype(jnp.bfloat16)
    query_side = jnp.concatenate(
        [query_heads.reshape(BR, BC, C), grad_att.reshape(BR, BC, C)], axis=-1
    )
    stats = jnp.concatenate([denoms, deltas], axis=-1)
    query_outer, stats_outer = (
        with_halo(query_side.astype(jnp.float32), (("rows", 0), ("grp", 1)), WIN).astype(
            query_side.dtype
        ),
        with_halo(stats, (("rows", 0), ("grp", 1)), WIN),
    )
    denom_outer = stats_outer[..., :HEADS] + (1.0 - valid_outer)[..., None]
    delta_outer = stats_outer[..., HEADS:]

    def key_pass(block_id):
        row_at = block_id // tile_count
        col_at = block_id % tile_count * tile_cols
        k_own = own_slice(key_heads, row_at, col_at, tile_cols)
        v_own = own_slice(value_heads, row_at, col_at, tile_cols)
        near_query = near_slice(query_outer, row_at, col_at, span_rows, near_cols)
        q_near = near_query[:, :C].reshape(near_count, HEADS, HEAD)
        d_near = near_query[:, C:].reshape(near_count, HEADS, HEAD)
        near_denom = near_slice(denom_outer, row_at, col_at, span_rows, near_cols).T
        near_delta = near_slice(delta_outer, row_at, col_at, span_rows, near_cols).T
        allowed = band_mask * near_slice(valid_outer, row_at, col_at, span_rows, near_cols)[None, :]
        scores = jnp.einsum("khd,qhd->hkq", k_own, q_near, preferred_element_type=jnp.float32)
        attend = jnp.exp(scores) * allowed[None] / near_denom[:, None, :]
        attend_b = attend.astype(jnp.bfloat16)
        grad_probs = jnp.einsum("qhd,khd->hkq", d_near, v_own, preferred_element_type=jnp.float32)
        grad_scores = (attend * (grad_probs - near_delta[:, None, :])).astype(jnp.bfloat16)
        key_part = jnp.einsum(
            "hkq,qhd->khd", grad_scores, q_near, preferred_element_type=jnp.float32
        ).reshape(tile_cols, C)
        value_part = jnp.einsum(
            "hkq,qhd->khd", attend_b, d_near, preferred_element_type=jnp.float32
        ).reshape(tile_cols, C)
        return jnp.concatenate([key_part, value_part], axis=-1)

    grad_core = lax.map(key_pass, block_ids)
    grad_keys = grad_core[..., :C].reshape(BR, BC, HEADS, HEAD)
    grad_values = grad_core[..., C:].reshape(BR, BC, HEADS, HEAD)
    grad_q = factor * query_inverse * grad_query - factor * query_inverse**3 * query_raw * jnp.mean(
        grad_query * query_raw, axis=-1, keepdims=True
    )
    grad_k = key_inverse * grad_keys - key_inverse**3 * key_raw * jnp.mean(
        grad_keys * key_raw, axis=-1, keepdims=True
    )
    scale_sum = jnp.sum(grad_query * query_raw * query_inverse, axis=(0, 1, 3)) / HEAD
    grad_proj = (
        jnp.stack([grad_q, grad_k, grad_values], axis=2).reshape(-1, 3 * C).astype(jnp.bfloat16)
    )
    qkv_sum = jnp.dot(normed.reshape(-1, C).T, grad_proj, preferred_element_type=jnp.float32)
    out_sum = jnp.dot(
        attended.reshape(-1, C).T, cotangent.reshape(-1, C), preferred_element_type=jnp.float32
    )
    grad_normed = jnp.dot(grad_proj, qkv_weight.T, preferred_element_type=jnp.float32).reshape(
        BR, BC, C
    )
    gain_sum = jnp.sum(grad_normed * tok_f32 * row_inverse, axis=(0, 1))
    scaled = norm_gain * grad_normed
    token_grad = (
        cotangent.astype(jnp.float32)
        + row_inverse * scaled
        - row_inverse**3 * tok_f32 * jnp.mean(scaled * tok_f32, axis=-1, keepdims=True)
    )
    gain_all, qkv_all, scale_all, out_all = lax.psum(
        (gain_sum, qkv_sum, scale_sum, out_sum), ("rows", "grp")
    )
    norm_factor = 1.0 / math.sqrt(rows_total * cols_total)
    return (
        output,
        token_grad,
        gain_all * norm_factor,
        qkv_all * norm_factor,
        scale_all * norm_factor,
        out_all * norm_factor,
    )


def solution(mesh):
    placed = (P("rows", "grp", None), P(), P(), P(), P(), P("rows", "grp", None))
    return jax.shard_map(
        body,
        mesh=mesh,
        in_specs=placed,
        out_specs=(P("rows", "grp", None), P("rows", "grp", None), P(), P(), P(), P()),
        check_vma=False,
    )
```

profile of v0, /device:TPU:1, one launch (start us, length us, event | category | flops | bytes accessed | tf_op | source)
XLA Modules:
  0.0 614.5 jit_solution(8111706163204111749)
XLA Ops:
  17.2 5.4 collective-permute-start
  29.4 4.8 collective-permute-start.4
  40.6 9.2 %collective-permute-start.3 = (bf16[10,3,512]{2,1,0:T(4,128)(2,1)S(1)}, bf16[10,3,512]{2,1,0:T(4,128)(2,1)S(1)}, u32[]{:S(2)}, u32[]{:S(2)}) collective-permute-start(bf16[10,3,512]{2,1,0:T(4,128)(2,1)S(1)} %get-tuple-element.442), channel_id=1, source_target_pairs={{1,0},{2,1},{3,2},{5,4},{6,5},{7,6},{9,8},{10,9},{11,10},{13,12},{... | collective-permute-start | bytes 92168 | tf_op jit(solution)/shard_map/ppermute | solution.py:27
  49.8 1.9 collective-permute-start.2
  54.2 2.4 collective-permute-start.7
  56.6 3.2 collective-permute-start.6
  59.8 2.6 pad_maximum_fusion.1
  62.4 72.1 %while.32 = (s32[]{:T(128)}, bf16[4,128,4,64]{1,3,2,0:T(8,128)(2,1)}, f32[4,128,4]{1,0,2:T(4,128)S(1)}, f32[4,128,4]{1,0,2:T(4,128)S(1)}, f32[4,128,4,64]{1,3,2,...) while((s32[]{:T(128)}, ...), condition=%wide.region_6.7_spmd.clone, body=%wide.region_3.6_spmd.clone.sunk | while | flops 253246720 | bytes 24003820 | solution.py:109
  72.2 2.2 fusion.127
  74.5 3.0 multiply_reduce_fusion.3
  77.5 2.9 fusion.128
  90.3 2.2 fusion.127
  92.5 3.0 multiply_reduce_fusion.3
  95.5 2.9 fusion.128
  108.3 2.2 fusion.127
  110.5 3.0 multiply_reduce_fusion.3
  113.6 2.9 fusion.128
  126.3 2.2 fusion.127
  128.6 3.0 multiply_reduce_fusion.3
  131.6 2.9 fusion.128
  135.8 1.9 fusion.39
  139.0 4.0 collective-permute-start.8
  145.0 1.9 collective-permute-start.11
  146.9 3.8 collective-permute-start.10
  153.7 60.7 %while.33 = (s32[]{:T(128)}, f32[4,128,512]{1,2,0:T(8,128)}, s32[4]{0:T(128)}, bf16[10,134,512]{2,1,0:T(8,128)(2,1)}, bf16[4,128,4,64]{1,3,2,0:T(8,128)(2,1)}, /...) while((s32[]{:T(128)}, f32[4,128,512]{1,2,0:T(8,128)}, ...), condition=%wide.region_9.10_spmd.clone, body=%wide.region_8.9_spmd.clone.sunk | while | flops 249438464 | bytes 17684252 | solution.py:157
  163.8 1.9 multiply_divide_fusion.2
  179.0 1.9 multiply_divide_fusion.2
  194.2 1.9 multiply_divide_fusion.2
  209.4 1.9 multiply_divide_fusion.2
  220.3 113.7 %all-reduce = (f32[256]{0:T(256)S(1)}, f32[4]{0:T(128)S(1)}) all-reduce(f32[256]{0:T(256)S(1)} %get-tuple-element.375, f32[4]{0:T(128)S(1)} %broadcast_multiply_fusion.8), channel_id=1, replica_groups=mesh['rows'=128,'grp'=4] {'rows','grp'}, use_global_device_ids=true, to_apply=%region_13.14 | all-reduce | flops 260 | bytes 2080 | tf_op jit(solution)/shard_map/psum | solution.py:184
  337.5 266.4 %all-reduce.4.cloned.1.call-done = (f32[256,768]{1,0:T(8,128)}, f32[256,256]{1,0:T(8,128)}) async-done(((f32[256,768]{1,0:T(8,128)}, f32[256,256]{1,0:T(8,128)}), (f32[256,768]{1,0:T(8,128)}, f32[256,256]{1,0:T(8,128)})) %all-reduce.4.cloned.1.call-update) | async-done | bytes 1048592 | tf_op jit(solution)/shard_map/psum | solution.py:184
  603.9 2.1 broadcast_multiply_fusion
  (262 shorter events, 109.9 us)
Async XLA Ops:
  7.2 18.5 %copy-start = (bf16[256,256]{1,0:T(8,128)(2,1)S(1)}, bf16[256,256]{1,0:T(8,128)(2,1)}, u32[]{:S(2)}) copy-start(bf16[256,256]{1,0:T(8,128)(2,1)} %param.14) | copy-start | bytes 393220
  7.2 596.7 %all-reduce.4.cloned.1.call-start = ((), (), s32[]{:S(2)}) async-start(), calls=%async_computation | async-start | bytes 2097152 | tf_op jit(solution)/shard_map/psum | solution.py:184
  12.3 25.9 %copy-start.1 = (f32[4,128,3,4,64]{1,4,3,2,0:T(8,128)}, f32[4,128,3,4,64]{1,4,3,2,0:T(8,128)S(1)}, u32[]{:S(2)}) copy-start(f32[4,128,3,4,64]{1,4,3,2,0:T(8,128)S(1)} %fusion.68) | copy-start | bytes 4718596
  14.4 23.8 %copy-start.13 = (f32[4,128,4]{1,2,0:T(4,128)}, f32[4,128,4]{1,2,0:T(4,128)S(1)}, u32[]{:S(2)}) copy-start(f32[4,128,4]{1,2,0:T(4,128)S(1)} %get-tuple-element.457) | copy-start | bytes 24580
  14.4 23.8 %copy-start.15 = (f32[4,128,4]{1,2,0:T(4,128)}, f32[4,128,4]{1,2,0:T(4,128)S(1)}, u32[]{:S(2)}) copy-start(f32[4,128,4]{1,2,0:T(4,128)S(1)} %get-tuple-element.461) | copy-start | bytes 24580
  14.9 10.8 %copy-start.9 = (bf16[4,128,256]{2,1,0:T(8,128)(2,1)S(1)}, bf16[4,128,256]{2,1,0:T(8,128)(2,1)}, u32[]{:S(2)}) copy-start(bf16[4,128,256]{2,1,0:T(8,128)(2,1)} %param.15) | copy-start | bytes 786436
  15.9 23.9 %collective-permute-start.1 = (bf16[3,128,512]{2,1,0:T(8,128)(2,1)}, bf16[3,128,512]{2,1,0:T(8,128)(2,1)}, u32[]{:S(2)}, u32[]{:S(2)}) collective-permute-start(bf16[3,128,512]{2,1,0:T(8,128)(2,1)} %get-tuple-element.446), channel_id=1, source_target_pairs={{4,0},{8,4},{12,8},{16,12},{20,16},{24,20},{28,24},{32,28},{36,32}... | collective-permute-start | bytes 1179656 | tf_op jit(solution)/shard_map/ppermute | solution.py:27
  17.2 22.6 %collective-permute-start = (bf16[3,128,512]{2,1,0:T(8,128)(2,1)}, bf16[3,128,512]{2,1,0:T(8,128)(2,1)}, u32[]{:S(2)}, u32[]{:S(2)}) collective-permute-start(bf16[3,128,512]{2,1,0:T(8,128)(2,1)} %get-tuple-element.445), channel_id=1, source_target_pairs={{0,4},{4,8},{8,12},{12,16},{16,20},{20,24},{24,28},{28,32},{32,36}... | collective-permute-start | bytes 1179656 | tf_op jit(solution)/shard_map/ppermute | solution.py:26
  28.1 23.6 %collective-permute-start.5 = (bf16[3,128,512]{2,1,0:T(8,128)(2,1)}, bf16[3,128,512]{2,1,0:T(8,128)(2,1)}, u32[]{:S(2)}, u32[]{:S(2)}) collective-permute-start(bf16[3,128,512]{2,1,0:T(8,128)(2,1)} %get-tuple-element.444), channel_id=1, source_target_pairs={{4,0},{8,4},{12,8},{16,12},{20,16},{24,20},{28,24},{32,28},{36,32}... | collective-permute-start | bytes 1179656 | tf_op jit(solution)/shard_map/ppermute | solution.py:27
  29.4 22.4 %collective-permute-start.4 = (bf16[3,128,512]{2,1,0:T(8,128)(2,1)}, bf16[3,128,512]{2,1,0:T(8,128)(2,1)}, u32[]{:S(2)}, u32[]{:S(2)}) collective-permute-start(bf16[3,128,512]{2,1,0:T(8,128)(2,1)} %get-tuple-element.443), channel_id=1, source_target_pairs={{0,4},{4,8},{8,12},{12,16},{16,20},{20,24},{24,28},{28,32},{32,36}... | collective-permute-start | bytes 1179656 | tf_op jit(solution)/shard_map/ppermute | solution.py:26
  40.6 19.2 %collective-permute-start.3 = (bf16[10,3,512]{2,1,0:T(4,128)(2,1)S(1)}, bf16[10,3,512]{2,1,0:T(4,128)(2,1)S(1)}, u32[]{:S(2)}, u32[]{:S(2)}) collective-permute-start(bf16[10,3,512]{2,1,0:T(4,128)(2,1)S(1)} %get-tuple-element.442), channel_id=1, source_target_pairs={{1,0},{2,1},{3,2},{5,4},{6,5},{7,6},{9,8},{10,9},{11,10},{13,12},{... | collective-permute-start | bytes 92168 | tf_op jit(solution)/shard_map/ppermute | solution.py:27
  49.8 10.0 %collective-permute-start.2 = (bf16[10,3,512]{2,1,0:T(4,128)(2,1)S(1)}, bf16[10,3,512]{2,1,0:T(4,128)(2,1)S(1)}, u32[]{:S(2)}, u32[]{:S(2)}) collective-permute-start(bf16[10,3,512]{2,1,0:T(4,128)(2,1)S(1)} %get-tuple-element.441), channel_id=1, source_target_pairs={{0,1},{1,2},{2,3},{4,5},{5,6},{6,7},{8,9},{9,10},{10,11},{12,13},{... | collective-permute-start | bytes 92168 | tf_op jit(solution)/shard_map/ppermute | solution.py:26
  54.1 8.2 %copy-start.23 = (f32[4,128,4]{1,0,2:T(4,128)S(1)}, f32[4,128,4]{1,0,2:T(4,128)}, u32[]{:S(2)}) copy-start(f32[4,128,4]{1,0,2:T(4,128)} %custom-call.2) | copy-start | bytes 24580
  54.1 8.2 %copy-start.24 = (f32[4,128,4]{1,0,2:T(4,128)S(1)}, f32[4,128,4]{1,0,2:T(4,128)}, u32[]{:S(2)}) copy-start(f32[4,128,4]{1,0,2:T(4,128)} %custom-call.3) | copy-start | bytes 24580
  54.2 96.6 %collective-permute-start.7 = (bf16[10,3,512]{2,1,0:T(4,128)(2,1)S(1)}, bf16[10,3,512]{2,1,0:T(4,128)(2,1)S(1)}, u32[]{:S(2)}, u32[]{:S(2)}) collective-permute-start(bf16[10,3,512]{2,1,0:T(4,128)(2,1)S(1)} %get-tuple-element.438), channel_id=1, source_target_pairs={{1,0},{2,1},{3,2},{5,4},{6,5},{7,6},{9,8},{10,9},{11,10},{13,12},{... | collective-permute-start | bytes 92168 | tf_op jit(solution)/shard_map/ppermute | solution.py:27
  56.6 94.2 %collective-permute-start.6 = (bf16[10,3,512]{2,1,0:T(4,128)(2,1)S(1)}, bf16[10,3,512]{2,1,0:T(4,128)(2,1)S(1)}, u32[]{:S(2)}, u32[]{:S(2)}) collective-permute-start(bf16[10,3,512]{2,1,0:T(4,128)(2,1)S(1)} %get-tuple-element.437), channel_id=1, source_target_pairs={{0,1},{1,2},{2,3},{4,5},{5,6},{6,7},{8,9},{9,10},{10,11},{12,13},{... | collective-permute-start | bytes 92168 | tf_op jit(solution)/shard_map/ppermute | solution.py:26
  62.3 73.4 %copy-start.5 = (bf16[4,128,256]{2,1,0:T(8,128)(2,1)S(1)}, bf16[4,128,256]{2,1,0:T(8,128)(2,1)}, u32[]{:S(2)}) copy-start(bf16[4,128,256]{2,1,0:T(8,128)(2,1)} %param.10) | copy-start | bytes 786436
  134.5 16.3 %copy-start.4 = (bf16[10,128,512]{2,1,0:T(8,128)(2,1)S(1)}, bf16[10,128,512]{2,1,0:T(8,128)(2,1)}, u32[]{:S(2)}) copy-start(bf16[10,128,512]{2,1,0:T(8,128)(2,1)} %copy-done.3) | copy-start | bytes 3932164
  137.7 7.2 %collective-permute-start.9 = (f32[3,128,8]{1,0,2:T(4,128)S(1)}, f32[3,128,8]{1,0,2:T(4,128)S(1)}, u32[]{:S(2)}, u32[]{:S(2)}) collective-permute-start(f32[3,128,8]{1,0,2:T(4,128)S(1)} %get-tuple-element.452), channel_id=1, source_target_pairs={{4,0},{8,4},{12,8},{16,12},{20,16},{24,20},{28,24},{32,28},{36,32}... | collective-permute-start | bytes 36872 | tf_op jit(solution)/shard_map/ppermute | solution.py:27
  139.0 5.9 collective-permute-start.8
  144.9 7.6 %copy-start.16 = (f32[10,134]{1,0:T(8,128)S(1)}, f32[10,134]{1,0:T(8,128)}, u32[]{:S(2)}) copy-start(f32[10,134]{1,0:T(8,128)} %broadcast_subtract_fusion) | copy-start | bytes 16084
  145.0 7.3 %collective-permute-start.11 = (f32[10,3,8]{1,0,2:T(8,128)S(1)}, f32[10,3,8]{1,0,2:T(8,128)S(1)}, u32[]{:S(2)}, u32[]{:S(2)}) collective-permute-start(f32[10,3,8]{1,0,2:T(8,128)S(1)} %get-tuple-element.450), channel_id=1, source_target_pairs={{1,0},{2,1},{3,2},{5,4},{6,5},{7,6},{9,8},{10,9},{11,10},{13,12},{... | collective-permute-start | bytes 2888 | tf_op jit(solution)/shard_map/ppermute | solution.py:27
  146.9 5.4 collective-permute-start.10
  214.4 2.3 copy-start.2
  214.4 3.8 copy-start.14
  214.5 3.8 copy-start.19
  216.7 1.7 copy-start.11
  216.8 1.7 copy-start.17
  216.8 1.7 copy-start.18
  218.8 115.8 %copy-start.8 = (bf16[4,128,256]{2,1,0:T(8,128)(2,1)S(1)}, bf16[4,128,256]{2,1,0:T(8,128)(2,1)}, u32[]{:S(2)}) copy-start(bf16[4,128,256]{2,1,0:T(8,128)(2,1)} %copy-done.7) | copy-start | bytes 786436
  220.3 116.1 %copy-start.10 = (bf16[4,128,256]{2,1,0:T(8,128)(2,1)S(1)}, bf16[4,128,256]{2,1,0:T(8,128)(2,1)}, u32[]{:S(2)}) copy-start(bf16[4,128,256]{2,1,0:T(8,128)(2,1)} %param.15) | copy-start | bytes 786436
  220.3 116.1 %copy-start.22 = (f32[4,128]{1,0:T(4,128)S(1)}, f32[4,128]{1,0:T(4,128)}, u32[]{:S(2)}) copy-start(f32[4,128]{1,0:T(4,128)} %get-tuple-element.458) | copy-start | bytes 6148
  (9 other events, 9.2 us)
Sparse Core Ops, SparseCore 0:
  336.0 267.8 all-reduce.3
where the time goes:
time: 618 us; the launch traced here: 614 us
  waiting for transfers between devices  266 us (43%)
  blocking collectives  114 us (18%)
  local copies, waits for them, and re-layouts  58 us (9%)
  matrix products  57.4 us (9%)
  starting transfers between devices  40.5 us (7%)
  other arithmetic  37.3 us (6%)
  loops' own time  26.5 us (4%)
  between operations  14.6 us (2%)
    psum x1, waiting for transfers between devices, body(): lax.psum((gain_sum, qkv_sum, scale_sum, out_sum), ('rows', 'grp'))  266 us
    psum x1, blocking collectives, body(): lax.psum((gain_sum, qkv_sum, scale_sum, out_sum), ('rows', 'grp'))  114 us
    ppermute x6, starting transfers between devices, with_halo(): before = lax.ppermute(last, axis, up)  23.1 us
    dynamic_slice x20, local copies, waits for them, and re-layouts, near_slice(): lax.dynamic_slice(array, starts, (span_rows, near_cols) + array.shape[2:])  19.6 us
    ppermute x6, starting transfers between devices, with_halo(): after = lax.ppermute(leading, axis, down)  17.4 us
    another operation x1, loops' own time, body(): grad_core = lax.map(key_pass, block_ids)  13.3 us
    another operation x1, loops' own time, body(): stacked = lax.map(lambda block_id: query_pass(block_id), block_ids)  13.2 us
  transfers between devices with their start and end apart: 13, of which 1 were waited for; matrix products, arithmetic and copies ran while one was open for 14% of the time, Pallas kernels for 0%

commit v1 on v0

v1 whole, which is shorter than its diff:
```python
import math

import jax
import jax.numpy as jnp
from jax import lax
from jax.experimental import pallas as pl
from jax.experimental.pallas import tpu as pltpu
from jax.sharding import Mesh, PartitionSpec as P

HEADS = 4
HEAD = 64
C = 256
WIN = 3
BR = 4
BC = 128
GRID = 512

EPS = 1e-06

PAD = 8
ER = BR + 2 * WIN
EC = BC + 2 * PAD
QC = 32
KC = 48
BLOCKS = BC // QC
NQ = BR * QC
NK = ER * KC
PAIRS = HEADS // 2
LANES = 2 * HEAD

AXES = ("z", "xh", "y", "xl", "core")
AXIS_SIZES = (8, 2, 8, 2, 2)
ROWS = ("z", "xh", "y")
GRP = ("xl", "core")
SPLIT = ("z", "y")
REST = ("xh", "xl", "core")
PARTS = 64
PART = 4 * C // PARTS
EXTRA = 16
PART_ROWS = 2 * PART + EXTRA

F32 = jnp.float32
BF16 = jnp.bfloat16


def mm(a, b, dims=((1,), (0,))):
    return lax.dot_general(a, b, (dims, ((), ())), preferred_element_type=F32)


def split_bf16(a):
    high = a.astype(BF16)
    return high, (a - high.astype(F32)).astype(BF16)


def row_stats(t):
    n = lax.rsqrt(jnp.mean(t * t, axis=-1, keepdims=True) + EPS)
    return n, t * n


def norm_grad(u, n, hat):
    return n * (u - hat * jnp.mean(u * hat, axis=-1, keepdims=True))


def kernel(
    place,
    up,
    own,
    down,
    left,
    right,
    cot,
    gain_ref,
    factor_ref,
    wqkv,
    wo,
    out,
    grad_own,
    grad_up,
    grad_down,
    grad_left,
    grad_right,
    sums,
    ext,
    normed_ext,
    k_hat,
    k_inv,
    k_b,
    v_b,
    gk,
    gv,
    normed_own,
    q_hat,
    q_inv,
    q_b,
    d_b,
    att_b,
    gq,
    acc_q,
    acc_kv,
    acc_out,
    acc_row,
    head_mean,
    base,
):
    gain = gain_ref[...]
    factor = factor_ref[...]

    lane_head = lax.broadcasted_iota(jnp.int32, (C, C), 1) // HEAD
    row_head = lax.broadcasted_iota(jnp.int32, (C, C), 0) // HEAD
    head_mean[...] = jnp.where(lane_head == row_head, 1.0 / HEAD, 0.0).astype(BF16)

    def per_head_mean(a):
        high, low = split_bf16(a)
        return mm(high, head_mean[...]) + mm(low, head_mean[...])

    own_cols = slice(PAD, PAD + BC)
    ext[0:WIN, own_cols] = up[...].astype(F32)
    ext[WIN : WIN + BR, own_cols] = own[...].astype(F32)
    ext[WIN + BR : ER, own_cols] = down[...].astype(F32)
    ext[:, 0:PAD] = left[...].astype(F32)
    ext[:, PAD + BC : EC] = right[...].astype(F32)

    gk[...] = jnp.zeros_like(gk)
    gv[...] = jnp.zeros_like(gv)
    acc_q[...] = jnp.zeros_like(acc_q)
    acc_kv[...] = jnp.zeros_like(acc_kv)
    acc_out[...] = jnp.zeros_like(acc_out)
    acc_row[...] = jnp.zeros_like(acc_row)

    @pl.loop(0, ER // 2)
    def _(i):
        rows = pl.ds(2 * i, 2)
        shape = (2, EC, C)
        _, hat = row_stats(ext[rows].reshape(2 * EC, C))
        normed = (hat * gain).astype(BF16)
        normed_ext[rows] = normed.reshape(shape)
        kv = mm(normed, wqkv[:, C:])
        k = kv[:, :C]
        inv = lax.rsqrt(per_head_mean(k * k) + EPS)
        hat_k = k * inv
        k_hat[rows] = hat_k.reshape(shape)
        k_inv[rows] = inv.reshape(shape)
        k_b[rows] = hat_k.astype(BF16).reshape(shape)
        v_b[rows] = kv[:, C:].astype(BF16).reshape(shape)

    @pl.loop(0, BR // 2)
    def _(i):
        rows = pl.ds(2 * i, 2)
        shape = (2, BC, C)
        _, hat = row_stats(own[rows].reshape(2 * BC, C).astype(F32))
        normed = (hat * gain).astype(BF16)
        normed_own[rows] = normed.reshape(shape)
        q = mm(normed, wqkv[:, :C])
        inv = lax.rsqrt(per_head_mean(q * q) + EPS)
        hat_q = q * inv
        q_hat[rows] = hat_q.reshape(shape)
        q_inv[rows] = inv.reshape(shape)
        q_b[rows] = (hat_q * factor).astype(BF16).reshape(shape)
        d = mm(cot[rows].reshape(2 * BC, C), wo[...], ((1,), (1,)))
        d_b[rows] = d.astype(BF16).reshape(shape)

    key_row = lax.broadcasted_iota(jnp.int32, (ER, KC, NQ), 0)
    key_col = lax.broadcasted_iota(jnp.int32, (ER, KC, NQ), 1)
    query = lax.broadcasted_iota(jnp.int32, (ER, KC, NQ), 2)
    row_gap = key_row - query // QC
    col_gap = key_col - query % QC - (PAD - WIN)
    in_rows = (key_row + place[0] - WIN >= 0) & (key_row + place[0] - WIN < GRID)
    near = (row_gap >= 0) & (row_gap <= 2 * WIN) & (col_gap >= 0) & (col_gap <= 2 * WIN)
    base[...] = jnp.where(near & in_rows, 1.0, 0.0)

    lane = lax.broadcasted_iota(jnp.int32, (NQ, LANES), 1)
    first = lane < HEAD
    row = lax.broadcasted_iota(jnp.int32, (LANES, NQ), 0)
    top = row < HEAD

    def both(a):
        zero = jnp.zeros_like(a)
        return jnp.concatenate([jnp.where(first, a, zero), jnp.where(first, zero, a)], axis=0)

    def own_head(a):
        return jnp.where(top, a[:, :NQ], a[:, NQ:]).T

    @pl.loop(0, BLOCKS)
    def _(b):
        q_cols = pl.ds(pl.multiple_of(b * QC, QC), QC)
        k_cols = pl.ds(pl.multiple_of(b * QC, QC), KC)
        col = lax.broadcasted_iota(jnp.int32, (ER, KC, NQ), 1) + (place[1] - PAD + b * QC)
        mask = jnp.where((col >= 0) & (col < GRID), base[...], 0.0).reshape(NK, NQ)
        mask = jnp.concatenate([mask, mask], axis=1)
        for p in range(PAIRS):
            lanes = slice(p * LANES, (p + 1) * LANES)
            k2 = k_b[:, k_cols, lanes].reshape(NK, LANES)
            v2 = v_b[:, k_cols, lanes].reshape(NK, LANES)
            q2 = both(q_b[:, q_cols, lanes].reshape(NQ, LANES))
            d2 = both(d_b[:, q_cols, lanes].reshape(NQ, LANES))
            e = jnp.exp(mm(k2, q2, ((1,), (1,)))) * mask
            attend = e * (1.0 / jnp.sum(e, axis=0, keepdims=True))
            attend_b = attend.astype(BF16)
            grad_probs = mm(v2, d2, ((1,), (1,)))
            delta = jnp.sum(attend * grad_probs, axis=0, keepdims=True)
            grad_scores = (attend * (grad_probs - delta)).astype(BF16)
            attended = own_head(mm(v2, attend_b, ((0,), (0,))))
            att_b[:, q_cols, lanes] = attended.astype(BF16).reshape(BR, QC, LANES)
            grad_query = own_head(mm(k2, grad_scores, ((0,), (0,))))
            gq[:, q_cols, lanes] = grad_query.reshape(BR, QC, LANES)
            gk[:, k_cols, lanes] += mm(grad_scores, q2).reshape(ER, KC, LANES)
            gv[:, k_cols, lanes] += mm(attend_b, d2).reshape(ER, KC, LANES)

    @pl.loop(0, BR // 2)
    def _(i):
        rows = pl.ds(2 * i, 2)
        shape = (2, BC, C)
        grad_query = gq[rows].reshape(2 * BC, C)
        hat_q = q_hat[rows].reshape(2 * BC, C)
        mean = per_head_mean(grad_query * hat_q)
        inv = q_inv[rows].reshape(2 * BC, C)
        g = (factor * inv * (grad_query - hat_q * mean)).astype(BF16)
        acc_row[0:1] += jnp.sum(mean, axis=0, keepdims=True)
        cot_b = cot[rows].reshape(2 * BC, C)
        att = att_b[rows].reshape(2 * BC, C)
        tok = own[rows].reshape(2 * BC, C).astype(F32)
        out[rows] = (tok + mm(att, wo[...])).astype(BF16).reshape(shape)
        acc_out[...] += mm(att, cot_b, ((0,), (0,)))
        acc_q[...] += mm(normed_own[rows].reshape(2 * BC, C), g, ((0,), (0,)))
        grad_normed = mm(g, wqkv[:, :C], ((1,), (1,)))
        n, hat = row_stats(tok)
        acc_row[1:2] += jnp.sum(grad_normed * hat, axis=0, keepdims=True)
        grad = cot_b.astype(F32) + norm_grad(gain * grad_normed, n, hat)
        grad_own[rows] = grad.reshape(shape)

    @pl.loop(0, ER // 2)
    def _(i):
        rows = pl.ds(2 * i, 2)
        grad_key = gk[rows].reshape(2 * EC, C)
        hat_k = k_hat[rows].reshape(2 * EC, C)
        mean = per_head_mean(grad_key * hat_k)
        g_k = k_inv[rows].reshape(2 * EC, C) * (grad_key - hat_k * mean)
        g = jnp.concatenate([g_k, gv[rows].reshape(2 * EC, C)], axis=1).astype(BF16)
        acc_kv[...] += mm(normed_ext[rows].reshape(2 * EC, C), g, ((0,), (0,)))
        grad_normed = mm(g, wqkv[:, C:], ((1,), (1,)))
        n, hat = row_stats(ext[rows].reshape(2 * EC, C))
        acc_row[1:2] += jnp.sum(grad_normed * hat, axis=0, keepdims=True)
        ext[rows] = norm_grad(gain * grad_normed, n, hat).reshape(2, EC, C)

    grad_own[...] += ext[WIN : WIN + BR, own_cols]
    grad_up[...] = ext[0:WIN].astype(BF16)
    grad_down[...] = ext[WIN + BR : ER].astype(BF16)
    grad_left[...] = ext[WIN : WIN + BR, 0:PAD]
    grad_right[...] = ext[WIN : WIN + BR, PAD + BC : EC]

    scale_high, scale_low = split_bf16(acc_row[0:1])
    gain_high, gain_low = split_bf16(acc_row[1:2])
    small = jnp.concatenate(
        [a.astype(F32)[:, h * 128 : h * 128 + 128] for a in (scale_high, scale_low, gain_high, gain_low) for h in (0, 1)]
        + [jnp.zeros((EXTRA - 8, 128), F32)],
        axis=0,
    ).astype(BF16)
    blocks = (acc_q, acc_kv, acc_kv, acc_out)
    offsets = (0, 0, C, 0)
    for part in range(PARTS):
        block, start = divmod(part * PART, C)
        ref, at = blocks[block], offsets[block]
        for h in (0, 1):
            piece = ref[start : start + PART, at + h * 128 : at + h * 128 + 128]
            sums[part, h * PART : h * PART + PART] = piece.astype(BF16)
        sums[part, 2 * PART :] = small


def run_kernel(place, up, own, down, left, right, cot, gain, factor, wqkv, wo):
    vmem = pl.BlockSpec(memory_space=pltpu.VMEM)
    shape = jax.ShapeDtypeStruct
    out_shape = (
        shape((BR, BC, C), BF16),
        shape((BR, BC, C), F32),
        shape((WIN, EC, C), BF16),
        shape((WIN, EC, C), BF16),
        shape((BR, PAD, C), F32),
        shape((BR, PAD, C), F32),
        shape((PARTS, PART_ROWS, 128), BF16),
    )
    ext_f, ext_b = pltpu.VMEM((ER, EC, C), F32), pltpu.VMEM((ER, EC, C), BF16)
    own_f, own_b = pltpu.VMEM((BR, BC, C), F32), pltpu.VMEM((BR, BC, C), BF16)
    scratch = [ext_f, ext_b, ext_f, ext_f, ext_b, ext_b, ext_f, ext_f]
    scratch += [own_b, own_f, own_f, own_b, own_b, own_b, own_f]
    scratch += [pltpu.VMEM((C, C), F32), pltpu.VMEM((C, 2 * C), F32), pltpu.VMEM((C, C), F32)]
    scratch += [pltpu.VMEM((8, C), F32), pltpu.VMEM((C, C), BF16), pltpu.VMEM((ER, KC, NQ), F32)]
    return pl.pallas_call(
        kernel,
        out_shape=out_shape,
        in_specs=[pl.BlockSpec(memory_space=pltpu.SMEM)] + [vmem] * 10,
        out_specs=[vmem] * 7,
        scratch_shapes=scratch,
        compiler_params=pltpu.CompilerParams(vmem_limit_bytes=40 * 1024 * 1024),
        cost_estimate=pl.CostEstimate(flops=6_000_000_000, bytes_accessed=6_000_000, transcendentals=1_000_000),
    )(place, up, own, down, left, right, cot, gain, factor, wqkv, wo)


def exchange(last, first, axes):
    size = math.prod(AXIS_SIZES[AXES.index(a)] for a in axes)
    forward = [(i, i + 1) for i in range(size - 1)]
    backward = [(i + 1, i) for i in range(size - 1)]
    return lax.ppermute(last, axes, forward), lax.ppermute(first, axes, backward)


def to_all(x, axes, size):
    return lax.all_to_all(jnp.broadcast_to(x[None], (size,) + x.shape), axes, 0, 0)


def reduce_sums(sums):
    part = jnp.sum(lax.all_to_all(sums, SPLIT, 0, 0).astype(F32), axis=0).astype(BF16)
    rest = 512 // PARTS
    part = jnp.sum(to_all(part, REST, rest).astype(F32), axis=0)
    small = part[2 * PART :]
    whole = to_all(part[: 2 * PART].astype(BF16), SPLIT, PARTS)
    whole = whole.reshape(4, C // PART, 2, PART, 128).transpose(0, 1, 3, 2, 4).reshape(4, C, C)
    return whole.astype(F32), small


def body(tokens, norm_gain, qkv_weight, head_scale, out_weight, cotangent):
    place = jnp.stack([lax.axis_index(ROWS) * BR, lax.axis_index(GRP) * BC]).astype(jnp.int32)
    up, down = exchange(tokens[BR - WIN :], tokens[:WIN], ROWS)
    last_cols = jnp.concatenate([a[:, BC - PAD :] for a in (up, tokens, down)], axis=0)
    first_cols = jnp.concatenate([a[:, :PAD] for a in (up, tokens, down)], axis=0)
    left, right = exchange(last_cols, first_cols, GRP)
    factor = jnp.repeat(head_scale / HEAD, HEAD)[None]
    out, grad_own, grad_up, grad_down, grad_left, grad_right, sums = run_kernel(
        place, up, tokens, down, left, right, cotangent, norm_gain[None], factor, qkv_weight, out_weight
    )
    from_up, from_down = exchange(grad_down, grad_up, ROWS)
    from_up = jnp.pad(from_up.astype(F32), ((0, BR - WIN), (0, 0), (0, 0)))
    from_down = jnp.pad(from_down.astype(F32), ((BR - WIN, 0), (0, 0), (0, 0)))
    rows_back = from_up + from_down
    from_left, from_right = exchange(
        (grad_right + rows_back[:, PAD + BC :]).astype(BF16),
        (grad_left + rows_back[:, :PAD]).astype(BF16),
        GRP,
    )
    token_grad = (
        grad_own
        + rows_back[:, PAD : PAD + BC]
        + jnp.pad(from_left.astype(F32), ((0, 0), (0, BC - PAD), (0, 0)))
        + jnp.pad(from_right.astype(F32), ((0, 0), (BC - PAD, 0), (0, 0)))
    )
    whole, small = reduce_sums(sums)
    norm_factor = 1.0 / GRID
    qkv_grad = jnp.concatenate([whole[0], whole[1], whole[2]], axis=1) * norm_factor
    small = small[:8].reshape(2, 2, C).sum(axis=1) * norm_factor
    scale_grad = small[0].reshape(HEADS, HEAD)[:, 0]
    return out, token_grad, small[1], qkv_grad, scale_grad, whole[3] * norm_factor


def solution(mesh):
    fine = Mesh(mesh.devices.reshape(AXIS_SIZES), AXES)
    tiles = P(ROWS, GRP, None)
    return jax.shard_map(
        body,
        mesh=fine,
        in_specs=(tiles, P(), P(), P(), P(), tiles),
        out_specs=(tiles, tiles, P(), P(), P(), P()),
        check_vma=False,
    )
```

time: 618 us -> 119 us (0.19)
  waiting for transfers between devices: 266 us -> 33.2 us
  blocking collectives: 114 us -> 7.66 us
  matrix products: 57.4 us -> 0 us
  local copies, waits for them, and re-layouts: 58 us -> 4.85 us
  other arithmetic: 37.3 us -> 2.39 us
  loops' own time: 26.5 us -> 0 us
  Pallas kernels: 0 us -> 15.8 us
  between operations: 14.6 us -> 0.94 us
  starting transfers between devices: 40.5 us -> 52.2 us
    psum x1 -> x0, waiting for transfers between devices: 266 us -> none  [body(): lax.psum((gain_sum, qkv_sum, scale_sum, out_sum), ('rows', 'grp'))]
    psum x1 -> x0, blocking collectives: 114 us -> none  [body(): lax.psum((gain_sum, qkv_sum, scale_sum, out_sum), ('rows', 'grp'))]
    dot_general x34 -> x0, matrix products: 57.4 us -> none  [the longest x4 11.9 us: query_pass(): jnp.einsum('qhd,khd->hqk', d_own, v_near, preferred_element_type=jnp.floa...]
    dynamic_slice x36 -> x0, local copies, waits for them, and re-layouts: 30.8 us -> none  [the longest x20 19.6 us: near_slice(): lax.dynamic_slice(array, starts, (span_rows, near_cols) + array.shape[2:])]
    all_to_all x0 -> x2, waiting for transfers between devices: none -> 26.7 us  [the longest x1 20.2 us: reduce_sums(): lax.all_to_all(sums, SPLIT, 0, 0).astype(F32)]
    another operation x2 -> x0, loops' own time: 26.5 us -> none  [the longest x1 13.3 us: body(): grad_core = lax.map(key_pass, block_ids)]
    all_to_all x0 -> x2, starting transfers between devices: none -> 26.3 us  [the longest x1 20.9 us: reduce_sums(): lax.all_to_all(sums, SPLIT, 0, 0).astype(F32)]
    pallas_call x0 -> x1, Pallas kernels: none -> 15.8 us  [run_kernel(): pl.pallas_call(kernel, out_shape=out_shape, in_specs=[pl.BlockSpec(memory...]
  transfers between devices with their start and end apart: 13 -> 10, of which waited for: 1 -> 6; matrix products, arithmetic and copies ran while one was open for 14% -> 3% of each run, Pallas kernels for 0% -> 0%
where the time goes in v1:
time: 119 us; the launch traced here: 117 us
  starting transfers between devices  52.2 us (44%)
  waiting for transfers between devices  33.2 us (28%)
  Pallas kernels  15.8 us (13%)
  blocking collectives  7.66 us (6%)
  local copies, waits for them, and re-layouts  4.85 us (4%)
  other arithmetic  2.39 us (2%)
    all_to_all x1, starting transfers between devices, reduce_sums(): lax.all_to_all(sums, SPLIT, 0, 0).astype(F32)  20.9 us
    all_to_all x1, waiting for transfers between devices, reduce_sums(): lax.all_to_all(sums, SPLIT, 0, 0).astype(F32)  20.2 us
    ppermute x4, starting transfers between devices, exchange(): lax.ppermute(last, axes, forward)  16.4 us
    pallas_call x1, Pallas kernels, run_kernel(): pl.pallas_call(kernel, out_shape=out_shape, in_specs=[pl.BlockSpec(memory...  15.8 us
    ppermute x4, starting transfers between devices, exchange(): lax.ppermute(first, axes, backward)  9.51 us
    all_to_all x1, blocking collectives, to_all(): lax.all_to_all(jnp.broadcast_to(x[None], (size,) + x.shape), axes, 0, 0)  7.66 us
    all_to_all x1, waiting for transfers between devices, to_all(): lax.all_to_all(jnp.broadcast_to(x[None], (size,) + x.shape), axes, 0, 0)  6.43 us
    all_to_all x1, starting transfers between devices, to_all(): lax.all_to_all(jnp.broadcast_to(x[None], (size,) + x.shape), axes, 0, 0)  5.4 us
  transfers between devices with their start and end apart: 10, of which 6 were waited for; matrix products, arithmetic and copies ran while one was open for 3% of the time, Pallas kernels for 0%

profile of v1, /device:TPU:1, one launch (start us, length us, event | category | flops | bytes accessed | tf_op | source)
XLA Modules:
  0.0 117.0 jit_solution(6486945403136412298)
XLA Ops:
  0.7 1.1 fusion.5
  1.8 1.4 %collective-permute-start.1 = (bf16[3,128,256]{2,1,0:T(8,128)(2,1)S(1)}, bf16[3,128,256]{2,1,0:T(8,128)(2,1)S(1)}, u32[]{:S(2)}, u32[]{:S(2)}) collective-permute-start(bf16[3,128,256]{2,1,0:T(8,128)(2,1)S(1)} %get-tuple-element.28), channel_id=1, source_target_pairs={{4,0},{8,4},{12,8},{16,12},{20,16},{24,20},{28,24},{32,28},{36,32}... | collective-permute-start | bytes 589832 | tf_op jit(solution)/shard_map/ppermute | solution.py:302
  3.2 4.7 %collective-permute-start = (bf16[3,128,256]{2,1,0:T(8,128)(2,1)S(1)}, bf16[3,128,256]{2,1,0:T(8,128)(2,1)S(1)}, u32[]{:S(2)}, u32[]{:S(2)}) collective-permute-start(bf16[3,128,256]{2,1,0:T(8,128)(2,1)S(1)} %get-tuple-element.29), channel_id=1, source_target_pairs={{0,4},{4,8},{8,12},{12,16},{16,20},{20,24},{24,28},{28,32},{32,36}... | collective-permute-start | bytes 589832 | tf_op jit(solution)/shard_map/ppermute | solution.py:302
  8.0 1.0 collective-permute-done.1.down
  9.0 1.5 %collective-permute-done.up = bf16[3,128,256]{2,1,0:T(8,128)(2,1)S(1)} collective-permute-done((bf16[3,128,256]{2,1,0:T(8,128)(2,1)S(1)}, bf16[3,128,256]{2,1,0:T(8,128)(2,1)S(1)}, u32[]{:S(2)}, u32[]{:S(2)}) %collective-permute-start) | collective-permute-done | bytes 196640 | tf_op jit(solution)/shard_map/ppermute | solution.py:302
  10.5 5.7 %collective-permute-start.2 = (bf16[10,8,256]{2,1,0:T(8,128)(2,1)S(1)}, bf16[10,8,256]{2,1,0:T(8,128)(2,1)S(1)}, u32[]{:S(2)}, u32[]{:S(2)}) collective-permute-start(bf16[10,8,256]{2,1,0:T(8,128)(2,1)S(1)} %pad_maximum_fusion), channel_id=1, source_target_pairs={{0,1},{1,2},{2,3},{4,5},{5,6},{6,7},{8,9},{9,10},{10,11},{12,13},{... | collective-permute-start | bytes 122888 | tf_op jit(solution)/shard_map/ppermute | solution.py:302
  16.2 4.9 %collective-permute-start.3 = (bf16[10,8,256]{2,1,0:T(8,128)(2,1)S(1)}, bf16[10,8,256]{2,1,0:T(8,128)(2,1)S(1)}, u32[]{:S(2)}, u32[]{:S(2)}) collective-permute-start(bf16[10,8,256]{2,1,0:T(8,128)(2,1)S(1)} %pad_maximum_fusion.1), channel_id=1, source_target_pairs={{1,0},{2,1},{3,2},{5,4},{6,5},{7,6},{9,8},{10,9},{11,10},{13,12},{... | collective-permute-start | bytes 122888 | tf_op jit(solution)/shard_map/ppermute | solution.py:302
  21.3 0.6 collective-permute-done.3.right
  22.0 15.8 %shard_map.109 = (bf16[4,128,256]{2,1,0:T(8,128)(2,1)}, f32[4,128,256]{2,1,0:T(8,128)S(1)}, bf16[3,144,256]{2,1,0:T(8,128)(2,1)S(1)}, bf16[3,144,256]{2,1,0:T(8,...) custom-call(s32[2]{0:T(128)S(1)} %pad_add_fusion.place, ...), custom_call_target="tpu_custom_call" | custom-call | flops 6000000000 | bytes 6000000 | tf_op jit(solution)/shard_map/pallas_call | solution.py:287
  37.8 20.9 %all-to-all-start = ((bf16[64,48,128]{2,1,0:T(8,128)(2,1)}), bf16[64,48,128]{2,1,0:T(8,128)(2,1)S(1)}, u32[]{:S(2)}, u32[]{:S(2)}) async-start(bf16[64,48,128]{2,1,0:T(8,128)(2,1)} %get-tuple-element.19), calls=%async_computation | async-start | bytes 1572864 | tf_op jit(solution)/shard_map/all_to_all | solution.py:310
  58.7 2.9 %collective-permute-start.4 = (bf16[3,144,256]{2,1,0:T(8,128)(2,1)S(1)}, bf16[3,144,256]{2,1,0:T(8,128)(2,1)S(1)}, u32[]{:S(2)}, u32[]{:S(2)}) collective-permute-start(bf16[3,144,256]{2,1,0:T(8,128)(2,1)S(1)} %get-tuple-element.15), channel_id=1, source_target_pairs={{0,4},{4,8},{8,12},{12,16},{16,20},{20,24},{24,28},{28,32},{32,36}... | collective-permute-start | bytes 663560 | tf_op jit(solution)/shard_map/ppermute | solution.py:302
  61.6 1.3 %collective-permute-start.5 = (bf16[3,144,256]{2,1,0:T(8,128)(2,1)S(1)}, bf16[3,144,256]{2,1,0:T(8,128)(2,1)S(1)}, u32[]{:S(2)}, u32[]{:S(2)}) collective-permute-start(bf16[3,144,256]{2,1,0:T(8,128)(2,1)S(1)} %get-tuple-element.16), channel_id=1, source_target_pairs={{4,0},{8,4},{12,8},{16,12},{20,16},{24,20},{28,24},{32,28},{36,32}... | collective-permute-start | bytes 663560 | tf_op jit(solution)/shard_map/ppermute | solution.py:302
  62.9 20.2 %all-to-all-done = bf16[64,48,128]{2,1,0:T(8,128)(2,1)S(1)} async-done(((bf16[64,48,128]{2,1,0:T(8,128)(2,1)}), bf16[64,48,128]{2,1,0:T(8,128)(2,1)S(1)}, u32[]{:S(2)}, u32[]{:S(2)}) %all-to-all-start) | async-done | bytes 786464 | tf_op jit(solution)/shard_map/all_to_all | solution.py:310
  83.2 0.1 reduce_sum.30
  83.3 7.7 %all_to_all.15 = bf16[8,48,128]{2,1,0:T(8,128)(2,1)S(1)} all-to-all(bf16[8,48,128]{2,1,0:T(8,128)(2,1)S(1)} %broadcast_in_dim.20), channel_id=1, replica_groups=mesh['z'=8,'xh'=2,'y'=8,'xl'=2,'core'=2] {'xh','xl','core'}, dimensions={0} | all-to-all | bytes 196608 | tf_op jit(solution)/shard_map/all_to_all | solution.py:306
  91.0 0.9 broadcast_in_dim.21
  91.9 5.4 %all-to-all-start.2 = ((bf16[64,32,128]{2,1,0:T(8,128)(2,1)}), bf16[64,32,128]{2,1,0:T(8,128)(2,1)S(1)}, u32[]{:S(2)}, u32[]{:S(2)}) async-start(bf16[64,32,128]{2,1,0:T(8,128)(2,1)} %broadcast_in_dim.21), calls=%async_computation.2 | async-start | bytes 1048576 | tf_op jit(solution)/shard_map/all_to_all | solution.py:306
  97.3 3.2 %collective-permute-start.6 = (bf16[4,8,256]{2,1,0:T(8,128)(2,1)S(1)}, bf16[4,8,256]{2,1,0:T(8,128)(2,1)S(1)}, u32[]{:S(2)}, u32[]{:S(2)}) collective-permute-start(bf16[4,8,256]{2,1,0:T(8,128)(2,1)S(1)} %get-tuple-element.24), channel_id=1, source_target_pairs={{0,1},{1,2},{2,3},{4,5},{5,6},{6,7},{8,9},{9,10},{10,11},{12,13},{... | collective-permute-start | bytes 49160 | tf_op jit(solution)/shard_map/ppermute | solution.py:302
  100.5 1.9 %collective-permute-start.7 = (bf16[4,8,256]{2,1,0:T(8,128)(2,1)S(1)}, bf16[4,8,256]{2,1,0:T(8,128)(2,1)S(1)}, u32[]{:S(2)}, u32[]{:S(2)}) collective-permute-start(bf16[4,8,256]{2,1,0:T(8,128)(2,1)S(1)} %get-tuple-element.25), channel_id=1, source_target_pairs={{1,0},{2,1},{3,2},{5,4},{6,5},{7,6},{9,8},{10,9},{11,10},{13,12},{... | collective-permute-start | bytes 49160 | tf_op jit(solution)/shard_map/ppermute | solution.py:302
  102.5 3.4 %collective-permute-done.7 = bf16[4,8,256]{2,1,0:T(8,128)(2,1)S(1)} collective-permute-done((bf16[4,8,256]{2,1,0:T(8,128)(2,1)S(1)}, bf16[4,8,256]{2,1,0:T(8,128)(2,1)S(1)}, u32[]{:S(2)}, u32[]{:S(2)}) %collective-permute-start.7) | collective-permute-done | bytes 16416 | tf_op jit(solution)/shard_map/ppermute | solution.py:302
  105.9 0.9 fusion.1
  106.8 0.6 slice_reduce_fusion.1
  107.4 0.6 slice_reduce_fusion
  108.1 6.4 %all-to-all-done.2 = bf16[64,32,128]{2,1,0:T(8,128)(2,1)S(1)} async-done(((bf16[64,32,128]{2,1,0:T(8,128)(2,1)}), bf16[64,32,128]{2,1,0:T(8,128)(2,1)S(1)}, u32[]{:S(2)}, u32[]{:S(2)}) %all-to-all-start.2) | async-done | bytes 524320 | tf_op jit(solution)/shard_map/all_to_all | solution.py:306
  114.5 0.1 convert_bitcast_fusion
  114.6 0.1 slice_multiply_fusion
  114.7 0.1 copy.19
  114.9 0.7 copy.28
  115.6 0.1 copy.18
  115.7 0.1 copy.17
  115.9 0.1 copy.16
  116.1 0.9 maximum_multiply_fusion
  (37 shorter events, 0.6 us)
Async XLA Ops:
  0.6 7.3 %copy-start = (bf16[4,128,256]{2,1,0:T(8,128)(2,1)S(1)}, bf16[4,128,256]{2,1,0:T(8,128)(2,1)}, u32[]{:S(2)}) copy-start(bf16[4,128,256]{2,1,0:T(8,128)(2,1)} %own.1) | copy-start | bytes 786436
  0.6 7.3 %copy-start.5 = (f32[4]{0:T(128)S(1)}, f32[4]{0:T(128)}, u32[]{:S(2)}) copy-start(f32[4]{0:T(128)} %param.9) | copy-start | bytes 52
  0.7 21.3 %copy-start.2 = (bf16[4,128,256]{2,1,0:T(8,128)(2,1)S(1)}, bf16[4,128,256]{2,1,0:T(8,128)(2,1)}, u32[]{:S(2)}) copy-start(bf16[4,128,256]{2,1,0:T(8,128)(2,1)} %cot.1) | copy-start | bytes 786436
  0.7 21.3 %copy-start.3 = (bf16[256,256]{1,0:T(8,128)(2,1)S(1)}, bf16[256,256]{1,0:T(8,128)(2,1)}, u32[]{:S(2)}) copy-start(bf16[256,256]{1,0:T(8,128)(2,1)} %wo.1) | copy-start | bytes 393220
  1.8 20.1 %copy-start.1 = (bf16[256,768]{1,0:T(8,128)(2,1)S(1)}, bf16[256,768]{1,0:T(8,128)(2,1)}, u32[]{:S(2)}) copy-start(bf16[256,768]{1,0:T(8,128)(2,1)} %wqkv.1) | copy-start | bytes 1179652
  1.8 7.2 %collective-permute-start.1 = (bf16[3,128,256]{2,1,0:T(8,128)(2,1)S(1)}, bf16[3,128,256]{2,1,0:T(8,128)(2,1)S(1)}, u32[]{:S(2)}, u32[]{:S(2)}) collective-permute-start(bf16[3,128,256]{2,1,0:T(8,128)(2,1)S(1)} %get-tuple-element.28), channel_id=1, source_target_pairs={{4,0},{8,4},{12,8},{16,12},{20,16},{24,20},{28,24},{32,28},{36,32}... | collective-permute-start | bytes 589832 | tf_op jit(solution)/shard_map/ppermute | solution.py:302
  3.2 7.3 %collective-permute-start = (bf16[3,128,256]{2,1,0:T(8,128)(2,1)S(1)}, bf16[3,128,256]{2,1,0:T(8,128)(2,1)S(1)}, u32[]{:S(2)}, u32[]{:S(2)}) collective-permute-start(bf16[3,128,256]{2,1,0:T(8,128)(2,1)S(1)} %get-tuple-element.29), channel_id=1, source_target_pairs={{0,4},{4,8},{8,12},{12,16},{16,20},{20,24},{24,28},{28,32},{32,36}... | collective-permute-start | bytes 589832 | tf_op jit(solution)/shard_map/ppermute | solution.py:302
  10.5 10.8 %collective-permute-start.2 = (bf16[10,8,256]{2,1,0:T(8,128)(2,1)S(1)}, bf16[10,8,256]{2,1,0:T(8,128)(2,1)S(1)}, u32[]{:S(2)}, u32[]{:S(2)}) collective-permute-start(bf16[10,8,256]{2,1,0:T(8,128)(2,1)S(1)} %pad_maximum_fusion), channel_id=1, source_target_pairs={{0,1},{1,2},{2,3},{4,5},{5,6},{6,7},{8,9},{9,10},{10,11},{12,13},{... | collective-permute-start | bytes 122888 | tf_op jit(solution)/shard_map/ppermute | solution.py:302
  16.2 5.7 %collective-permute-start.3 = (bf16[10,8,256]{2,1,0:T(8,128)(2,1)S(1)}, bf16[10,8,256]{2,1,0:T(8,128)(2,1)S(1)}, u32[]{:S(2)}, u32[]{:S(2)}) collective-permute-start(bf16[10,8,256]{2,1,0:T(8,128)(2,1)S(1)} %pad_maximum_fusion.1), channel_id=1, source_target_pairs={{1,0},{2,1},{3,2},{5,4},{6,5},{7,6},{9,8},{10,9},{11,10},{13,12},{... | collective-permute-start | bytes 122888 | tf_op jit(solution)/shard_map/ppermute | solution.py:302
  21.3 0.7 copy-start.4
  37.8 45.3 %all-to-all-start = ((bf16[64,48,128]{2,1,0:T(8,128)(2,1)}), bf16[64,48,128]{2,1,0:T(8,128)(2,1)S(1)}, u32[]{:S(2)}, u32[]{:S(2)}) async-start(bf16[64,48,128]{2,1,0:T(8,128)(2,1)} %get-tuple-element.19), calls=%async_computation | async-start | bytes 1572864 | tf_op jit(solution)/shard_map/all_to_all | solution.py:310
  58.7 38.6 %collective-permute-start.4 = (bf16[3,144,256]{2,1,0:T(8,128)(2,1)S(1)}, bf16[3,144,256]{2,1,0:T(8,128)(2,1)S(1)}, u32[]{:S(2)}, u32[]{:S(2)}) collective-permute-start(bf16[3,144,256]{2,1,0:T(8,128)(2,1)S(1)} %get-tuple-element.15), channel_id=1, source_target_pairs={{0,4},{4,8},{8,12},{12,16},{16,20},{20,24},{24,28},{28,32},{32,36}... | collective-permute-start | bytes 663560 | tf_op jit(solution)/shard_map/ppermute | solution.py:302
  61.6 35.7 %collective-permute-start.5 = (bf16[3,144,256]{2,1,0:T(8,128)(2,1)S(1)}, bf16[3,144,256]{2,1,0:T(8,128)(2,1)S(1)}, u32[]{:S(2)}, u32[]{:S(2)}) collective-permute-start(bf16[3,144,256]{2,1,0:T(8,128)(2,1)S(1)} %get-tuple-element.16), channel_id=1, source_target_pairs={{4,0},{8,4},{12,8},{16,12},{20,16},{24,20},{28,24},{32,28},{36,32}... | collective-permute-start | bytes 663560 | tf_op jit(solution)/shard_map/ppermute | solution.py:302
  91.9 22.6 %all-to-all-start.2 = ((bf16[64,32,128]{2,1,0:T(8,128)(2,1)}), bf16[64,32,128]{2,1,0:T(8,128)(2,1)S(1)}, u32[]{:S(2)}, u32[]{:S(2)}) async-start(bf16[64,32,128]{2,1,0:T(8,128)(2,1)} %broadcast_in_dim.21), calls=%async_computation.2 | async-start | bytes 1048576 | tf_op jit(solution)/shard_map/all_to_all | solution.py:306
  97.3 5.2 %collective-permute-start.6 = (bf16[4,8,256]{2,1,0:T(8,128)(2,1)S(1)}, bf16[4,8,256]{2,1,0:T(8,128)(2,1)S(1)}, u32[]{:S(2)}, u32[]{:S(2)}) collective-permute-start(bf16[4,8,256]{2,1,0:T(8,128)(2,1)S(1)} %get-tuple-element.24), channel_id=1, source_target_pairs={{0,1},{1,2},{2,3},{4,5},{5,6},{6,7},{8,9},{9,10},{10,11},{12,13},{... | collective-permute-start | bytes 49160 | tf_op jit(solution)/shard_map/ppermute | solution.py:302
  100.5 5.4 %collective-permute-start.7 = (bf16[4,8,256]{2,1,0:T(8,128)(2,1)S(1)}, bf16[4,8,256]{2,1,0:T(8,128)(2,1)S(1)}, u32[]{:S(2)}, u32[]{:S(2)}) collective-permute-start(bf16[4,8,256]{2,1,0:T(8,128)(2,1)S(1)} %get-tuple-element.25), channel_id=1, source_target_pairs={{1,0},{2,1},{3,2},{5,4},{6,5},{7,6},{9,8},{10,9},{11,10},{13,12},{... | collective-permute-start | bytes 49160 | tf_op jit(solution)/shard_map/ppermute | solution.py:302

commit v2 on v1

v2 whole, which is shorter than its diff:
```python
import math

import jax
import jax.numpy as jnp
from jax import lax
from jax.experimental import pallas as pl
from jax.experimental.pallas import tpu as pltpu
from jax.sharding import Mesh, PartitionSpec as P

HEADS = 4
HEAD = 64
C = 256
WIN = 3
BR = 4
BC = 128
GRID = 512

EPS = 1e-06

PAD = 8
ER = BR + 2 * WIN
EC = BC + 2 * PAD
QC = 32
KC = 48
BLOCKS = BC // QC
NQ = BR * QC
NK = ER * KC
PAIRS = HEADS // 2
LANES = 2 * HEAD

AXES = ("z", "xh", "y", "xl", "core")
AXIS_SIZES = (8, 2, 8, 2, 2)
ROWS = ("z", "xh", "y")
GRP = ("xl", "core")
SPLIT = ("z", "y")
REST = ("xh", "xl", "core")
PARTS = 64
PART = 4 * C // PARTS
EXTRA = 16
PART_ROWS = 2 * PART + EXTRA

F32 = jnp.float32
BF16 = jnp.bfloat16


def mm(a, b, dims=((1,), (0,))):
    return lax.dot_general(a, b, (dims, ((), ())), preferred_element_type=F32)


def split_bf16(a):
    high = a.astype(BF16)
    return high, (a - high.astype(F32)).astype(BF16)


def row_stats(t):
    n = lax.rsqrt(jnp.mean(t * t, axis=-1, keepdims=True) + EPS)
    return n, t * n


def norm_grad(u, n, hat):
    return n * (u - hat * jnp.mean(u * hat, axis=-1, keepdims=True))


def ones_per_head():
    lane_head = lax.broadcasted_iota(jnp.int32, (C, C), 1) // HEAD
    row_head = lax.broadcasted_iota(jnp.int32, (C, C), 0) // HEAD
    return jnp.where(lane_head == row_head, 1.0 / HEAD, 0.0).astype(BF16)


def per_head_mean(a, ones):
    high, low = split_bf16(a)
    return mm(high, ones) + mm(low, ones)


def normalise(raw, ones):
    inv = lax.rsqrt(per_head_mean(raw * raw, ones) + EPS)
    return raw * inv, inv


def widen(a, rows):
    edge = jnp.zeros((rows, PAD, C), F32)
    return jnp.concatenate([edge, a.reshape(rows, BC, C), edge], axis=1).astype(BF16)


def own_kernel(own, cot, gain, factor, wqkv, wo, q_b, d_b, normed_own, q_inv, normed_ext, k_b, v_b, k_inv, ones):
    ones[...] = ones_per_head()

    @pl.loop(0, BR // 2)
    def _(i):
        rows = pl.ds(2 * i, 2)
        shape = (2, BC, C)
        _, hat = row_stats(own[rows].reshape(2 * BC, C).astype(F32))
        scaled = hat * gain[...]
        normed = scaled.astype(BF16)
        projected = mm(normed, wqkv[...])
        q, inv = normalise(projected[:, :C], ones[...])
        k, inv_k = normalise(projected[:, C : 2 * C], ones[...])
        normed_own[rows] = normed.reshape(shape)
        q_inv[rows] = inv.reshape(shape)
        q_b[rows] = (q * factor[...]).astype(BF16).reshape(shape)
        normed_ext[rows] = widen(scaled, 2)
        k_b[rows] = widen(k, 2)
        k_inv[rows] = widen(inv_k, 2)
        v_b[rows] = widen(projected[:, 2 * C :], 2)
        d = mm(cot[rows].reshape(2 * BC, C), wo[...], ((1,), (1,)))
        d_b[rows] = d.astype(BF16).reshape(shape)


def halo_kernel(up, down, gain, wqkv, normed_ext, k_b, v_b, k_inv, ones):
    ones[...] = ones_per_head()
    for half, ref in enumerate((up, down)):
        rows = slice(half * WIN, half * WIN + WIN)
        _, hat = row_stats(ref[...].reshape(WIN * BC, C).astype(F32))
        scaled = hat * gain[...]
        projected = mm(scaled.astype(BF16), wqkv[:, C:])
        k, inv_k = normalise(projected[:, :C], ones[...])
        normed_ext[rows] = widen(scaled, WIN)
        k_b[rows] = widen(k, WIN)
        k_inv[rows] = widen(inv_k, WIN)
        v_b[rows] = widen(projected[:, C:], WIN)


def attention_kernel(
    place,
    left,
    right,
    cot,
    gain,
    factor,
    wqkv,
    q_b,
    d_b,
    normed_own,
    q_inv,
    normed_mid,
    k_mid,
    v_mid,
    k_inv_mid,
    normed_halo,
    k_halo,
    v_halo,
    k_inv_halo,
    sums,
    att_b,
    g_q,
    g_kv,
    normed_ext,
    k_b,
    v_b,
    k_inv,
    gk,
    gv,
    gq,
    acc_q,
    acc_kv,
    acc_out,
    acc_scale,
    ones,
    base,
):
    ones[...] = ones_per_head()

    edges = jnp.concatenate([left[...].astype(F32), right[...].astype(F32)], axis=0)
    _, hat = row_stats(edges.reshape(2 * ER * PAD, C))
    scaled = hat * gain[...]
    projected = mm(scaled.astype(BF16), wqkv[:, C:])
    k, inv_k = normalise(projected[:, :C], ones[...])
    for ext, mid, halo, edge in (
        (normed_ext, normed_mid, normed_halo, scaled),
        (k_b, k_mid, k_halo, k),
        (v_b, v_mid, v_halo, projected[:, C:]),
        (k_inv, k_inv_mid, k_inv_halo, inv_k),
    ):
        edge = edge.reshape(2 * ER, PAD, C)
        ext[0:WIN] = halo[0:WIN]
        ext[WIN : WIN + BR] = mid[...]
        ext[WIN + BR : ER] = halo[WIN : 2 * WIN]
        near = ext[:, 0 : 2 * PAD].astype(F32)[:, PAD:]
        ext[:, 0 : 2 * PAD] = jnp.concatenate([edge[:ER], near], axis=1).astype(BF16)
        near = ext[:, EC - 2 * PAD : EC].astype(F32)[:, :PAD]
        ext[:, EC - 2 * PAD : EC] = jnp.concatenate([near, edge[ER:]], axis=1).astype(BF16)

    gk[...] = jnp.zeros_like(gk)
    gv[...] = jnp.zeros_like(gv)

    key_row = lax.broadcasted_iota(jnp.int32, (ER, KC, NQ), 0)
    key_col = lax.broadcasted_iota(jnp.int32, (ER, KC, NQ), 1)
    query = lax.broadcasted_iota(jnp.int32, (ER, KC, NQ), 2)
    row_gap = key_row - query // QC
    col_gap = key_col - query % QC - (PAD - WIN)
    in_rows = (key_row + place[0] - WIN >= 0) & (key_row + place[0] - WIN < GRID)
    near = (row_gap >= 0) & (row_gap <= 2 * WIN) & (col_gap >= 0) & (col_gap <= 2 * WIN)
    base[...] = jnp.where(near & in_rows, 1.0, 0.0)

    first = lax.broadcasted_iota(jnp.int32, (NQ, LANES), 1) < HEAD
    top = lax.broadcasted_iota(jnp.int32, (LANES, NQ), 0) < HEAD

    def both(a):
        zero = jnp.zeros_like(a)
        return jnp.concatenate([jnp.where(first, a, zero), jnp.where(first, zero, a)], axis=0)

    def own_head(a):
        return jnp.where(top, a[:, :NQ], a[:, NQ:]).T

    @pl.loop(0, BLOCKS)
    def _(b):
        q_cols = pl.ds(pl.multiple_of(b * QC, QC), QC)
        k_cols = pl.ds(pl.multiple_of(b * QC, QC), KC)
        col = lax.broadcasted_iota(jnp.int32, (ER, KC, NQ), 1) + (place[1] - PAD + b * QC)
        mask = jnp.where((col >= 0) & (col < GRID), base[...], 0.0).reshape(NK, NQ)
        mask = jnp.concatenate([mask, mask], axis=1)
        for p in range(PAIRS):
            lanes = slice(p * LANES, (p + 1) * LANES)
            k2 = k_b[:, k_cols, lanes].reshape(NK, LANES)
            v2 = v_b[:, k_cols, lanes].reshape(NK, LANES)
            q2 = both(q_b[:, q_cols, lanes].reshape(NQ, LANES))
            d2 = both(d_b[:, q_cols, lanes].reshape(NQ, LANES))
            e = jnp.exp(mm(k2, q2, ((1,), (1,)))) * mask
            attend = e * (1.0 / jnp.sum(e, axis=0, keepdims=True))
            attend_b = attend.astype(BF16)
            grad_probs = mm(v2, d2, ((1,), (1,)))
            delta = jnp.sum(attend * grad_probs, axis=0, keepdims=True)
            grad_scores = (attend * (grad_probs - delta)).astype(BF16)
            attended = own_head(mm(v2, attend_b, ((0,), (0,))))
            att_b[:, q_cols, lanes] = attended.astype(BF16).reshape(BR, QC, LANES)
            grad_query = own_head(mm(k2, grad_scores, ((0,), (0,))))
            gq[:, q_cols, lanes] = grad_query.reshape(BR, QC, LANES)
            gk[:, k_cols, lanes] += mm(grad_scores, q2).reshape(ER, KC, LANES)
            gv[:, k_cols, lanes] += mm(attend_b, d2).reshape(ER, KC, LANES)

    inv_factor = 1.0 / factor[...]
    grad_query = gq[...].reshape(BR * BC, C)
    q_f = q_b[...].reshape(BR * BC, C).astype(F32)
    mean = per_head_mean(grad_query * q_f, ones[...]) * inv_factor
    acc_scale[...] = jnp.sum(mean, axis=0, keepdims=True)
    g = q_inv[...].reshape(BR * BC, C) * (factor[...] * grad_query - q_f * mean)
    g = g.astype(BF16)
    g_q[...] = g.reshape(BR, BC, C)
    acc_out[...] = mm(att_b[...].reshape(BR * BC, C), cot[...].reshape(BR * BC, C), ((0,), (0,)))
    acc_q[...] = mm(normed_own[...].reshape(BR * BC, C), g, ((0,), (0,)))

    @pl.loop(0, ER // 2)
    def _(i):
        rows = pl.ds(2 * i, 2)
        shape = (2, EC, C)
        grad_key = gk[rows].reshape(2 * EC, C)
        k_f = k_b[rows].reshape(2 * EC, C).astype(F32)
        mean = per_head_mean(grad_key * k_f, ones[...])
        g_k = k_inv[rows].reshape(2 * EC, C).astype(F32) * (grad_key - k_f * mean)
        g_kv[rows, :, :C] = g_k.astype(BF16).reshape(shape)
        g_kv[rows, :, C:] = gv[rows].astype(BF16)

    acc_kv[...] = mm(normed_ext[...].reshape(ER * EC, C), g_kv[...].reshape(ER * EC, 2 * C), ((0,), (0,)))

    by_feature = (
        wqkv[:, :C].astype(F32) * acc_q[...]
        + wqkv[:, C : 2 * C].astype(F32) * acc_kv[:, :C]
        + wqkv[:, 2 * C :].astype(F32) * acc_kv[:, C:]
    )
    high, low = split_bf16(by_feature)
    every = jnp.ones((8, C), BF16)
    gain_sum = mm(every, high, ((1,), (1,))) + mm(every, low, ((1,), (1,)))
    gain_sum = gain_sum[0:1] / gain[...]

    small = [part.astype(F32) for a in (acc_scale[...], gain_sum) for part in split_bf16(a)]
    small = [a[:, h * 128 : h * 128 + 128] for a in small for h in (0, 1)]
    small = jnp.concatenate(small + [jnp.zeros((EXTRA - 8, 128), F32)], axis=0).astype(BF16)
    blocks = (acc_q, acc_kv, acc_kv, acc_out)
    offsets = (0, 0, C, 0)
    for part in range(PARTS):
        block, start = divmod(part * PART, C)
        ref, at = blocks[block], offsets[block]
        for h in (0, 1):
            piece = ref[start : start + PART, at + h * 128 : at + h * 128 + 128]
            sums[part, h * PART : h * PART + PART] = piece.astype(BF16)
        sums[part, 2 * PART :] = small


def token_kernel(
    up,
    own,
    down,
    left,
    right,
    cot,
    gain,
    wqkv,
    wo,
    att_b,
    g_q,
    g_kv,
    out,
    grad_own,
    grad_up,
    grad_down,
    grad_left,
    grad_right,
    ext,
):
    own_cols = slice(PAD, PAD + BC)
    ext[0:WIN, own_cols] = up[...].astype(F32)
    ext[WIN : WIN + BR, own_cols] = own[...].astype(F32)
    ext[WIN + BR : ER, own_cols] = down[...].astype(F32)
    ext[:, 0:PAD] = left[...].astype(F32)
    ext[:, PAD + BC : EC] = right[...].astype(F32)

    @pl.loop(0, ER // 2)
    def _(i):
        rows = pl.ds(2 * i, 2)
        grad_normed = mm(g_kv[rows].reshape(2 * EC, 2 * C), wqkv[:, C:], ((1,), (1,)))
        n, hat = row_stats(ext[rows].reshape(2 * EC, C))
        ext[rows] = norm_grad(gain[...] * grad_normed, n, hat).reshape(2, EC, C)

    grad_up[...] = ext[0:WIN].astype(BF16)
    grad_down[...] = ext[WIN + BR : ER].astype(BF16)
    grad_left[...] = ext[WIN : WIN + BR, 0:PAD]
    grad_right[...] = ext[WIN : WIN + BR, PAD + BC : EC]

    @pl.loop(0, BR // 2)
    def _(i):
        rows = pl.ds(2 * i, 2)
        shape = (2, BC, C)
        tok = own[rows].reshape(2 * BC, C).astype(F32)
        att = att_b[rows].reshape(2 * BC, C)
        out[rows] = (tok + mm(att, wo[...])).astype(BF16).reshape(shape)
        grad_normed = mm(g_q[rows].reshape(2 * BC, C), wqkv[:, :C], ((1,), (1,)))
        n, hat = row_stats(tok)
        grad = cot[rows].reshape(2 * BC, C).astype(F32) + norm_grad(gain[...] * grad_normed, n, hat)
        grad_own[rows] = grad.reshape(shape) + ext[pl.ds(WIN + 2 * i, 2), own_cols]


def call(fn, out_shape, scratch, megabytes, microseconds, *args):
    vmem = pl.BlockSpec(memory_space=pltpu.VMEM)
    smem = pl.BlockSpec(memory_space=pltpu.SMEM)
    return pl.pallas_call(
        fn,
        out_shape=tuple(jax.ShapeDtypeStruct(s, d) for s, d in out_shape),
        in_specs=[smem if a.dtype == jnp.int32 else vmem for a in args],
        out_specs=tuple(vmem for _ in out_shape),
        scratch_shapes=[pltpu.VMEM(s, d) for s, d in scratch],
        compiler_params=pltpu.CompilerParams(vmem_limit_bytes=megabytes * 1024 * 1024),
        cost_estimate=pl.CostEstimate(flops=microseconds * 1_000_000_000, bytes_accessed=1_000_000, transcendentals=0),
    )(*args)


OWN = (BR, BC, C)
EXT = (ER, EC, C)
ONES = ((C, C), BF16)


def run_own(tokens, cotangent, gain, factor, wqkv, wo):
    mid = ((BR, EC, C), BF16)
    outs = [(OWN, BF16), (OWN, BF16), (OWN, BF16), (OWN, F32), mid, mid, mid, mid]
    return call(own_kernel, outs, [ONES], 12, 3, tokens, cotangent, gain, factor, wqkv, wo)


def run_halo(up, down, gain, wqkv):
    halo = ((2 * WIN, EC, C), BF16)
    return call(halo_kernel, [halo] * 4, [ONES], 12, 3, up, down, gain, wqkv)


def run_attention(place, left, right, cot, gain, factor, wqkv, own, halo):
    outs = [((PARTS, PART_ROWS, 128), BF16), (OWN, BF16), (OWN, BF16), ((ER, EC, 2 * C), BF16)]
    scratch = [(EXT, BF16)] * 4 + [(EXT, F32)] * 2 + [(OWN, F32)]
    scratch += [((C, C), F32), ((C, 2 * C), F32), ((C, C), F32), ((1, C), F32), ONES, ((ER, KC, NQ), F32)]
    return call(attention_kernel, outs, scratch, 28, 9, place, left, right, cot, gain, factor, wqkv, *own, *halo)


def run_tokens(up, own, down, left, right, cot, gain, wqkv, wo, att_b, g_q, g_kv):
    halo = ((WIN, EC, C), BF16)
    edge = ((BR, PAD, C), F32)
    outs = [(OWN, BF16), (OWN, F32), halo, halo, edge, edge]
    return call(token_kernel, outs, [(EXT, F32)], 16, 4, up, own, down, left, right, cot, gain, wqkv, wo, att_b, g_q, g_kv)


def exchange(last, first, axes):
    size = math.prod(AXIS_SIZES[AXES.index(a)] for a in axes)
    forward = [(i, i + 1) for i in range(size - 1)]
    backward = [(i + 1, i) for i in range(size - 1)]
    return lax.ppermute(last, axes, forward), lax.ppermute(first, axes, backward)


def to_all(x, axes, size):
    return lax.all_to_all(jnp.broadcast_to(x[None], (size,) + x.shape), axes, 0, 0)


def reduce_sums(sums):
    part = jnp.sum(lax.all_to_all(sums, SPLIT, 0, 0).astype(F32), axis=0).astype(BF16)
    rest = 512 // PARTS
    part = jnp.sum(to_all(part, REST, rest).astype(F32), axis=0)
    small = part[2 * PART :]
    whole = to_all(part[: 2 * PART].astype(BF16), SPLIT, PARTS)
    whole = whole.reshape(4, C // PART, 2, PART, 128).transpose(0, 1, 3, 2, 4).reshape(4, C, C)
    return whole.astype(F32), small


def body(tokens, norm_gain, qkv_weight, head_scale, out_weight, cotangent):
    place = jnp.stack([lax.axis_index(ROWS) * BR, lax.axis_index(GRP) * BC]).astype(jnp.int32)
    gain = norm_gain[None]
    factor = jnp.repeat(head_scale / HEAD, HEAD)[None]
    up, down = exchange(tokens[BR - WIN :], tokens[:WIN], ROWS)
    own = run_own(tokens, cotangent, gain, factor, qkv_weight, out_weight)
    last_cols = jnp.concatenate([a[:, BC - PAD :] for a in (up, tokens, down)], axis=0)
    first_cols = jnp.concatenate([a[:, :PAD] for a in (up, tokens, down)], axis=0)
    left, right = exchange(last_cols, first_cols, GRP)
    halo = run_halo(up, down, gain, qkv_weight)
    sums, att_b, g_q, g_kv = run_attention(place, left, right, cotangent, gain, factor, qkv_weight, own, halo)
    out, grad_own, grad_up, grad_down, grad_left, grad_right = run_tokens(
        up, tokens, down, left, right, cotangent, gain, qkv_weight, out_weight, att_b, g_q, g_kv
    )
    from_up, from_down = exchange(grad_down, grad_up, ROWS)
    from_up = jnp.pad(from_up.astype(F32), ((0, BR - WIN), (0, 0), (0, 0)))
    from_down = jnp.pad(from_down.astype(F32), ((BR - WIN, 0), (0, 0), (0, 0)))
    rows_back = from_up + from_down
    from_left, from_right = exchange(
        (grad_right + rows_back[:, PAD + BC :]).astype(BF16),
        (grad_left + rows_back[:, :PAD]).astype(BF16),
        GRP,
    )
    token_grad = (
        grad_own
        + rows_back[:, PAD : PAD + BC]
        + jnp.pad(from_left.astype(F32), ((0, 0), (0, BC - PAD), (0, 0)))
        + jnp.pad(from_right.astype(F32), ((0, 0), (BC - PAD, 0), (0, 0)))
    )
    whole, small = reduce_sums(sums)
    norm_factor = 1.0 / GRID
    qkv_grad = jnp.concatenate([whole[0], whole[1], whole[2]], axis=1) * norm_factor
    small = small[:8].reshape(2, 2, C).sum(axis=1) * norm_factor
    scale_grad = small[0].reshape(HEADS, HEAD)[:, 0]
    return out, token_grad, small[1], qkv_grad, scale_grad, whole[3] * norm_factor


def solution(mesh):
    fine = Mesh(mesh.devices.reshape(AXIS_SIZES), AXES)
    tiles = P(ROWS, GRP, None)
    return jax.shard_map(
        body,
        mesh=fine,
        in_specs=(tiles, P(), P(), P(), P(), tiles),
        out_specs=(tiles, tiles, P(), P(), P(), P()),
        check_vma=False,
    )
```

time: 119 us -> 117 us (0.983)
  the two profiles are of different devices: /device:TPU:1 before, /device:TPU:8 now
where the time goes in v2:
time: 117 us; the launch traced here: 116 us
  starting transfers between devices  44.5 us (38%)
  waiting for transfers between devices  27.8 us (24%)
  Pallas kernels  15.3 us (13%)
  blocking collectives  12 us (10%)
  local copies, waits for them, and re-layouts  11.7 us (10%)
  other arithmetic  4.18 us (4%)
    all_to_all x1, starting transfers between devices, reduce_sums(): lax.all_to_all(sums, SPLIT, 0, 0).astype(F32)  17 us
    pallas_call x4, Pallas kernels, call(): pl.pallas_call(fn, out_shape=tuple((jax.ShapeDtypeStruct(s, d) for s, d i...  15.3 us
    ppermute x4, starting transfers between devices, exchange(): lax.ppermute(first, axes, backward)  12.9 us
    all_to_all x1, waiting for transfers between devices, reduce_sums(): lax.all_to_all(sums, SPLIT, 0, 0).astype(F32)  12.4 us
    all_to_all x1, blocking collectives, to_all(): lax.all_to_all(jnp.broadcast_to(x[None], (size,) + x.shape), axes, 0, 0)  12 us
    all_to_all x1, waiting for transfers between devices, to_all(): lax.all_to_all(jnp.broadcast_to(x[None], (size,) + x.shape), axes, 0, 0)  11.8 us
    ppermute x4, starting transfers between devices, exchange(): lax.ppermute(last, axes, forward)  7.87 us
    unnamed x26, local copies, waits for them, and re-layouts  7.74 us
  transfers between devices with their start and end apart: 10, of which 4 were waited for; matrix products, arithmetic and copies ran while one was open for 5% of the time, Pallas kernels for 4%

profile of v2, /device:TPU:8, one launch (start us, length us, event | category | flops | bytes accessed | tf_op | source)
XLA Modules:
  0.0 116.4 jit_solution(3135689335996075910)
XLA Ops:
  0.6 1.1 fusion.5
  1.7 7.7 %collective-permute-start.1 = (bf16[3,128,256]{2,1,0:T(8,128)(2,1)S(1)}, bf16[3,128,256]{2,1,0:T(8,128)(2,1)S(1)}, u32[]{:S(2)}, u32[]{:S(2)}) collective-permute-start(bf16[3,128,256]{2,1,0:T(8,128)(2,1)S(1)} %get-tuple-element.58), channel_id=1, source_target_pairs={{4,0},{8,4},{12,8},{16,12},{20,16},{24,20},{28,24},{32,28},{36,32}... | collective-permute-start | bytes 589832 | tf_op jit(solution)/shard_map/ppermute | solution.py:380
  9.4 1.9 %collective-permute-start = (bf16[3,128,256]{2,1,0:T(8,128)(2,1)S(1)}, bf16[3,128,256]{2,1,0:T(8,128)(2,1)S(1)}, u32[]{:S(2)}, u32[]{:S(2)}) collective-permute-start(bf16[3,128,256]{2,1,0:T(8,128)(2,1)S(1)} %get-tuple-element.59), channel_id=1, source_target_pairs={{0,4},{4,8},{8,12},{12,16},{16,20},{20,24},{24,28},{28,32},{32,36}... | collective-permute-start | bytes 589832 | tf_op jit(solution)/shard_map/ppermute | solution.py:380
  12.3 0.9 copy-done
  13.2 1.0 copy-done.2
  14.2 0.9 copy-done.4
  15.2 0.9 copy-done.6
  16.1 0.7 copy-done.8
  16.7 1.2 shard_map.109
  18.0 1.3 %collective-permute-start.2 = (bf16[10,8,256]{2,1,0:T(8,128)(2,1)S(1)}, bf16[10,8,256]{2,1,0:T(8,128)(2,1)S(1)}, u32[]{:S(2)}, u32[]{:S(2)}) collective-permute-start(bf16[10,8,256]{2,1,0:T(8,128)(2,1)S(1)} %pad_maximum_fusion), channel_id=1, source_target_pairs={{0,1},{1,2},{2,3},{4,5},{5,6},{6,7},{8,9},{9,10},{10,11},{12,13},{... | collective-permute-start | bytes 122888 | tf_op jit(solution)/shard_map/ppermute | solution.py:380
  19.3 1.4 %collective-permute-start.3 = (bf16[10,8,256]{2,1,0:T(8,128)(2,1)S(1)}, bf16[10,8,256]{2,1,0:T(8,128)(2,1)S(1)}, u32[]{:S(2)}, u32[]{:S(2)}) collective-permute-start(bf16[10,8,256]{2,1,0:T(8,128)(2,1)S(1)} %pad_maximum_fusion.1), channel_id=1, source_target_pairs={{1,0},{2,1},{3,2},{5,4},{6,5},{7,6},{9,8},{10,9},{11,10},{13,12},{... | collective-permute-start | bytes 122888 | tf_op jit(solution)/shard_map/ppermute | solution.py:380
  20.8 0.8 shard_map.110
  21.5 1.0 collective-permute-done.3.right
  22.6 10.1 %shard_map.111 = (bf16[64,48,128]{2,1,0:T(8,128)(2,1)}, bf16[4,128,256]{2,1,0:T(8,128)(2,1)S(1)}, bf16[4,128,256]{2,1,0:T(8,128)(2,1)S(1)}, bf16[10,144,512]{2,1,0:T(8,128)(2,1)S(1)}) custom-call(s32[2]{0:T(128)S(1)} %pad_add_fusion.place, bf16[10,8,256]{2,1,0:T(8,128)(2,1)S(1)} %collective-permute-done.2.left, ...), custom_call_target="tpu_custom_call" | custom-call | flops 8999999488 | bytes 1000000 | tf_op jit(solution)/shard_map/pallas_call | solution.py:335
  32.7 1.1 copy-done.10
  33.8 17.0 %all-to-all-start = ((bf16[64,48,128]{2,1,0:T(8,128)(2,1)}), bf16[64,48,128]{2,1,0:T(8,128)(2,1)}, u32[]{:S(2)}, u32[]{:S(2)}) async-start(bf16[64,48,128]{2,1,0:T(8,128)(2,1)} %get-tuple-element.49), calls=%async_computation | async-start | bytes 1572864 | tf_op jit(solution)/shard_map/all_to_all | solution.py:388
  50.9 1.4 %copy-done.11 = bf16[10,144,512]{2,1,0:T(8,128)(2,1)S(1)} copy-done((bf16[10,144,512]{2,1,0:T(8,128)(2,1)S(1)}, bf16[10,144,512]{2,1,0:T(8,128)(2,1)}, u32[]{:S(2)}) %copy-start.11) | copy-done | bytes 1474584
  52.3 3.2 %shard_map.112 = (bf16[4,128,256]{2,1,0:T(8,128)(2,1)}, f32[4,128,256]{2,1,0:T(8,128)S(1)}, bf16[3,144,256]{2,1,0:T(8,128)(2,1)S(1)}, bf16[3,144,256]{2,1,0:T(8,...) custom-call(bf16[3,128,256]{2,1,0:T(8,128)(2,1)S(1)} %collective-permute-done.up, ...), custom_call_target="tpu_custom_call" | custom-call | flops 4000000000 | bytes 1000000 | tf_op jit(solution)/shard_map/pallas_call | solution.py:335
  55.5 3.4 %collective-permute-start.4 = (bf16[3,144,256]{2,1,0:T(8,128)(2,1)S(1)}, bf16[3,144,256]{2,1,0:T(8,128)(2,1)S(1)}, u32[]{:S(2)}, u32[]{:S(2)}) collective-permute-start(bf16[3,144,256]{2,1,0:T(8,128)(2,1)S(1)} %get-tuple-element.45), channel_id=1, source_target_pairs={{0,4},{4,8},{8,12},{12,16},{16,20},{20,24},{24,28},{28,32},{32,36}... | collective-permute-start | bytes 663560 | tf_op jit(solution)/shard_map/ppermute | solution.py:380
  58.9 2.5 %collective-permute-start.5 = (bf16[3,144,256]{2,1,0:T(8,128)(2,1)S(1)}, bf16[3,144,256]{2,1,0:T(8,128)(2,1)S(1)}, u32[]{:S(2)}, u32[]{:S(2)}) collective-permute-start(bf16[3,144,256]{2,1,0:T(8,128)(2,1)S(1)} %get-tuple-element.46), channel_id=1, source_target_pairs={{4,0},{8,4},{12,8},{16,12},{20,16},{24,20},{28,24},{32,28},{36,32}... | collective-permute-start | bytes 663560 | tf_op jit(solution)/shard_map/ppermute | solution.py:380
  61.3 12.4 %all-to-all-done = bf16[64,48,128]{2,1,0:T(8,128)(2,1)} async-done(((bf16[64,48,128]{2,1,0:T(8,128)(2,1)}), bf16[64,48,128]{2,1,0:T(8,128)(2,1)}, u32[]{:S(2)}, u32[]{:S(2)}) %all-to-all-start) | async-done | bytes 786464 | tf_op jit(solution)/shard_map/all_to_all | solution.py:388
  73.7 1.3 %reduce_sum.30 = bf16[48,128]{1,0:T(8,128)(2,1)S(1)} reduce(bf16[64,48,128]{2,1,0:T(8,128)(2,1)} %all-to-all-done, bf16[]{:T(256)} %constant.41.clone.1), dimensions={0}, to_apply=%region_0.1 | reduce | flops 387072 | bytes 798722 | tf_op jit(solution)/shard_map/reduce_sum | solution.py:388
  75.0 12.0 %all_to_all.15 = bf16[8,48,128]{2,1,0:T(8,128)(2,1)S(1)} all-to-all(bf16[8,48,128]{2,1,0:T(8,128)(2,1)S(1)} %broadcast_in_dim.20), channel_id=1, replica_groups=mesh['z'=8,'xh'=2,'y'=8,'xl'=2,'core'=2] {'xh','xl','core'}, dimensions={0} | all-to-all | bytes 196608 | tf_op jit(solution)/shard_map/all_to_all | solution.py:384
  87.1 0.9 broadcast_in_dim.21
  88.0 6.7 %all-to-all-start.2 = ((bf16[64,32,128]{2,1,0:T(8,128)(2,1)}), bf16[64,32,128]{2,1,0:T(8,128)(2,1)S(1)}, u32[]{:S(2)}, u32[]{:S(2)}) async-start(bf16[64,32,128]{2,1,0:T(8,128)(2,1)} %broadcast_in_dim.21), calls=%async_computation.2 | async-start | bytes 1048576 | tf_op jit(solution)/shard_map/all_to_all | solution.py:384
  94.7 1.3 %collective-permute-start.6 = (bf16[4,8,256]{2,1,0:T(8,128)(2,1)S(1)}, bf16[4,8,256]{2,1,0:T(8,128)(2,1)S(1)}, u32[]{:S(2)}, u32[]{:S(2)}) collective-permute-start(bf16[4,8,256]{2,1,0:T(8,128)(2,1)S(1)} %get-tuple-element.54), channel_id=1, source_target_pairs={{0,1},{1,2},{2,3},{4,5},{5,6},{6,7},{8,9},{9,10},{10,11},{12,13},{... | collective-permute-start | bytes 49160 | tf_op jit(solution)/shard_map/ppermute | solution.py:380
  96.0 1.3 %collective-permute-start.7 = (bf16[4,8,256]{2,1,0:T(8,128)(2,1)S(1)}, bf16[4,8,256]{2,1,0:T(8,128)(2,1)S(1)}, u32[]{:S(2)}, u32[]{:S(2)}) collective-permute-start(bf16[4,8,256]{2,1,0:T(8,128)(2,1)S(1)} %get-tuple-element.55), channel_id=1, source_target_pairs={{1,0},{2,1},{3,2},{5,4},{6,5},{7,6},{9,8},{10,9},{11,10},{13,12},{... | collective-permute-start | bytes 49160 | tf_op jit(solution)/shard_map/ppermute | solution.py:380
  97.3 2.5 %collective-permute-done.7 = bf16[4,8,256]{2,1,0:T(8,128)(2,1)S(1)} collective-permute-done((bf16[4,8,256]{2,1,0:T(8,128)(2,1)S(1)}, bf16[4,8,256]{2,1,0:T(8,128)(2,1)S(1)}, u32[]{:S(2)}, u32[]{:S(2)}) %collective-permute-start.7) | collective-permute-done | bytes 16416 | tf_op jit(solution)/shard_map/ppermute | solution.py:380
  99.8 0.9 fusion.1
  102.0 11.8 %all-to-all-done.2 = bf16[64,32,128]{2,1,0:T(8,128)(2,1)S(1)} async-done(((bf16[64,32,128]{2,1,0:T(8,128)(2,1)}), bf16[64,32,128]{2,1,0:T(8,128)(2,1)S(1)}, u32[]{:S(2)}, u32[]{:S(2)}) %all-to-all-start.2) | async-done | bytes 524320 | tf_op jit(solution)/shard_map/all_to_all | solution.py:384
  114.3 0.7 copy.28
  115.5 0.9 maximum_multiply_fusion
  (52 shorter events, 3.2 us)
Async XLA Ops:
  1.7 16.2 %collective-permute-start.1 = (bf16[3,128,256]{2,1,0:T(8,128)(2,1)S(1)}, bf16[3,128,256]{2,1,0:T(8,128)(2,1)S(1)}, u32[]{:S(2)}, u32[]{:S(2)}) collective-permute-start(bf16[3,128,256]{2,1,0:T(8,128)(2,1)S(1)} %get-tuple-element.58), channel_id=1, source_target_pairs={{4,0},{8,4},{12,8},{16,12},{20,16},{24,20},{28,24},{32,28},{36,32}... | collective-permute-start | bytes 589832 | tf_op jit(solution)/shard_map/ppermute | solution.py:380
  9.4 8.5 %collective-permute-start = (bf16[3,128,256]{2,1,0:T(8,128)(2,1)S(1)}, bf16[3,128,256]{2,1,0:T(8,128)(2,1)S(1)}, u32[]{:S(2)}, u32[]{:S(2)}) collective-permute-start(bf16[3,128,256]{2,1,0:T(8,128)(2,1)S(1)} %get-tuple-element.59), channel_id=1, source_target_pairs={{0,4},{4,8},{8,12},{12,16},{16,20},{20,24},{24,28},{28,32},{32,36}... | collective-permute-start | bytes 589832 | tf_op jit(solution)/shard_map/ppermute | solution.py:380
  12.3 0.9 copy-start
  13.2 1.0 copy-start.2
  14.2 0.9 copy-start.4
  15.2 0.9 copy-start.6
  16.1 0.7 copy-start.8
  16.7 4.0 %copy-start.3 = (bf16[256,768]{1,0:T(8,128)(2,1)S(1)}, bf16[256,768]{1,0:T(8,128)(2,1)}, u32[]{:S(2)}) copy-start(bf16[256,768]{1,0:T(8,128)(2,1)} %wqkv.7) | copy-start | bytes 1179652
  18.0 3.6 %collective-permute-start.2 = (bf16[10,8,256]{2,1,0:T(8,128)(2,1)S(1)}, bf16[10,8,256]{2,1,0:T(8,128)(2,1)S(1)}, u32[]{:S(2)}, u32[]{:S(2)}) collective-permute-start(bf16[10,8,256]{2,1,0:T(8,128)(2,1)S(1)} %pad_maximum_fusion), channel_id=1, source_target_pairs={{0,1},{1,2},{2,3},{4,5},{5,6},{6,7},{8,9},{9,10},{10,11},{12,13},{... | collective-permute-start | bytes 122888 | tf_op jit(solution)/shard_map/ppermute | solution.py:380
  19.3 3.3 %copy-start.5 = (bf16[4,128,256]{2,1,0:T(8,128)(2,1)S(1)}, bf16[4,128,256]{2,1,0:T(8,128)(2,1)}, u32[]{:S(2)}) copy-start(bf16[4,128,256]{2,1,0:T(8,128)(2,1)} %cot.5) | copy-start | bytes 786436
  19.3 3.3 %copy-start.9 = (f32[256]{0:T(256)S(1)}, f32[256]{0:T(256)}, u32[]{:S(2)}) copy-start(f32[256]{0:T(256)} %param.7) | copy-start | bytes 3076
  19.3 3.2 %collective-permute-start.3 = (bf16[10,8,256]{2,1,0:T(8,128)(2,1)S(1)}, bf16[10,8,256]{2,1,0:T(8,128)(2,1)S(1)}, u32[]{:S(2)}, u32[]{:S(2)}) collective-permute-start(bf16[10,8,256]{2,1,0:T(8,128)(2,1)S(1)} %pad_maximum_fusion.1), channel_id=1, source_target_pairs={{1,0},{2,1},{3,2},{5,4},{6,5},{7,6},{9,8},{10,9},{11,10},{13,12},{... | collective-permute-start | bytes 122888 | tf_op jit(solution)/shard_map/ppermute | solution.py:380
  32.7 1.1 copy-start.10
  33.8 17.1 %copy-start.1 = (bf16[4,128,256]{2,1,0:T(8,128)(2,1)S(1)}, bf16[4,128,256]{2,1,0:T(8,128)(2,1)}, u32[]{:S(2)}) copy-start(bf16[4,128,256]{2,1,0:T(8,128)(2,1)} %own.3) | copy-start | bytes 786436
  33.8 17.1 %copy-start.7 = (bf16[256,256]{1,0:T(8,128)(2,1)S(1)}, bf16[256,256]{1,0:T(8,128)(2,1)}, u32[]{:S(2)}) copy-start(bf16[256,256]{1,0:T(8,128)(2,1)} %wo.3) | copy-start | bytes 393220
  33.8 39.9 %all-to-all-start = ((bf16[64,48,128]{2,1,0:T(8,128)(2,1)}), bf16[64,48,128]{2,1,0:T(8,128)(2,1)}, u32[]{:S(2)}, u32[]{:S(2)}) async-start(bf16[64,48,128]{2,1,0:T(8,128)(2,1)} %get-tuple-element.49), calls=%async_computation | async-start | bytes 1572864 | tf_op jit(solution)/shard_map/all_to_all | solution.py:388
  50.9 1.4 %copy-start.11 = (bf16[10,144,512]{2,1,0:T(8,128)(2,1)S(1)}, bf16[10,144,512]{2,1,0:T(8,128)(2,1)}, u32[]{:S(2)}) copy-start(bf16[10,144,512]{2,1,0:T(8,128)(2,1)} %copy-done.10) | copy-start | bytes 4423684
  55.5 39.1 %collective-permute-start.4 = (bf16[3,144,256]{2,1,0:T(8,128)(2,1)S(1)}, bf16[3,144,256]{2,1,0:T(8,128)(2,1)S(1)}, u32[]{:S(2)}, u32[]{:S(2)}) collective-permute-start(bf16[3,144,256]{2,1,0:T(8,128)(2,1)S(1)} %get-tuple-element.45), channel_id=1, source_target_pairs={{0,4},{4,8},{8,12},{12,16},{16,20},{20,24},{24,28},{28,32},{32,36}... | collective-permute-start | bytes 663560 | tf_op jit(solution)/shard_map/ppermute | solution.py:380
  58.9 35.8 %collective-permute-start.5 = (bf16[3,144,256]{2,1,0:T(8,128)(2,1)S(1)}, bf16[3,144,256]{2,1,0:T(8,128)(2,1)S(1)}, u32[]{:S(2)}, u32[]{:S(2)}) collective-permute-start(bf16[3,144,256]{2,1,0:T(8,128)(2,1)S(1)} %get-tuple-element.46), channel_id=1, source_target_pairs={{4,0},{8,4},{12,8},{16,12},{20,16},{24,20},{28,24},{32,28},{36,32}... | collective-permute-start | bytes 663560 | tf_op jit(solution)/shard_map/ppermute | solution.py:380
  88.0 25.9 %all-to-all-start.2 = ((bf16[64,32,128]{2,1,0:T(8,128)(2,1)}), bf16[64,32,128]{2,1,0:T(8,128)(2,1)S(1)}, u32[]{:S(2)}, u32[]{:S(2)}) async-start(bf16[64,32,128]{2,1,0:T(8,128)(2,1)} %broadcast_in_dim.21), calls=%async_computation.2 | async-start | bytes 1048576 | tf_op jit(solution)/shard_map/all_to_all | solution.py:384
  94.7 2.7 %collective-permute-start.6 = (bf16[4,8,256]{2,1,0:T(8,128)(2,1)S(1)}, bf16[4,8,256]{2,1,0:T(8,128)(2,1)S(1)}, u32[]{:S(2)}, u32[]{:S(2)}) collective-permute-start(bf16[4,8,256]{2,1,0:T(8,128)(2,1)S(1)} %get-tuple-element.54), channel_id=1, source_target_pairs={{0,1},{1,2},{2,3},{4,5},{5,6},{6,7},{8,9},{9,10},{10,11},{12,13},{... | collective-permute-start | bytes 49160 | tf_op jit(solution)/shard_map/ppermute | solution.py:380
  96.0 3.9 %collective-permute-start.7 = (bf16[4,8,256]{2,1,0:T(8,128)(2,1)S(1)}, bf16[4,8,256]{2,1,0:T(8,128)(2,1)S(1)}, u32[]{:S(2)}, u32[]{:S(2)}) collective-permute-start(bf16[4,8,256]{2,1,0:T(8,128)(2,1)S(1)} %get-tuple-element.55), channel_id=1, source_target_pairs={{1,0},{2,1},{3,2},{5,4},{6,5},{7,6},{9,8},{10,9},{11,10},{13,12},{... | collective-permute-start | bytes 49160 | tf_op jit(solution)/shard_map/ppermute | solution.py:380

commit v3 on v2

--- a/solution.py
+++ b/solution.py
@@ -32,12 +32,13 @@
 AXIS_SIZES = (8, 2, 8, 2, 2)
 ROWS = ("z", "xh", "y")
 GRP = ("xl", "core")
-SPLIT = ("z", "y")
-REST = ("xh", "xl", "core")
-PARTS = 64
-PART = 4 * C // PARTS
-EXTRA = 16
-PART_ROWS = 2 * PART + EXTRA
+SPLIT = ("z", "xh", "xl")
+REST = ("y",)
+PARTS = 32
+RESTS = 8
+HALF = 2 * C
+PART = HALF // PARTS
+EXTRA = 8
 
 F32 = jnp.float32
 BF16 = jnp.bfloat16
@@ -140,10 +141,11 @@
     k_halo,
     v_halo,
     k_inv_halo,
-    sums,
+    keep,
+    send,
     att_b,
     g_q,
-    g_kv,
+    g_kv_out,
     normed_ext,
     k_b,
     v_b,
@@ -151,12 +153,11 @@
     gk,
     gv,
     gq,
-    acc_q,
-    acc_kv,
-    acc_out,
-    acc_scale,
+    g_kv,
+    acc,
     ones,
     base,
+    copied,
 ):
     ones[...] = ones_per_head()
 
@@ -232,12 +233,12 @@
     grad_query = gq[...].reshape(BR * BC, C)
     q_f = q_b[...].reshape(BR * BC, C).astype(F32)
     mean = per_head_mean(grad_query * q_f, ones[...]) * inv_factor
-    acc_scale[...] = jnp.sum(mean, axis=0, keepdims=True)
+    scale_sum = jnp.sum(mean, axis=0, keepdims=True)
     g = q_inv[...].reshape(BR * BC, C) * (factor[...] * grad_query - q_f * mean)
     g = g.astype(BF16)
     g_q[...] = g.reshape(BR, BC, C)
-    acc_out[...] = mm(att_b[...].reshape(BR * BC, C), cot[...].reshape(BR * BC, C), ((0,), (0,)))
-    acc_q[...] = mm(normed_own[...].reshape(BR * BC, C), g, ((0,), (0,)))
+    acc[3 * C :] = mm(att_b[...].reshape(BR * BC, C), cot[...].reshape(BR * BC, C), ((0,), (0,)))
+    acc[:C] = mm(normed_own[...].reshape(BR * BC, C), g, ((0,), (0,)))
 
     @pl.loop(0, ER // 2)
     def _(i):
@@ -250,30 +251,34 @@
         g_kv[rows, :, :C] = g_k.astype(BF16).reshape(shape)
         g_kv[rows, :, C:] = gv[rows].astype(BF16)
 
-    acc_kv[...] = mm(normed_ext[...].reshape(ER * EC, C), g_kv[...].reshape(ER * EC, 2 * C), ((0,), (0,)))
+    copy = pltpu.make_async_copy(g_kv, g_kv_out, copied)
+    copy.start()
+    acc_kv = mm(normed_ext[...].reshape(ER * EC, C), g_kv[...].reshape(ER * EC, 2 * C), ((0,), (0,)))
+    acc[C : 2 * C] = acc_kv[:, :C]
+    acc[2 * C : 3 * C] = acc_kv[:, C:]
 
     by_feature = (
-        wqkv[:, :C].astype(F32) * acc_q[...]
-        + wqkv[:, C : 2 * C].astype(F32) * acc_kv[:, :C]
-        + wqkv[:, 2 * C :].astype(F32) * acc_kv[:, C:]
+        wqkv[:, :C].astype(F32) * acc[:C]
+        + wqkv[:, C : 2 * C].astype(F32) * acc[C : 2 * C]
+        + wqkv[:, 2 * C :].astype(F32) * acc[2 * C : 3 * C]
     )
     high, low = split_bf16(by_feature)
     every = jnp.ones((8, C), BF16)
     gain_sum = mm(every, high, ((1,), (1,))) + mm(every, low, ((1,), (1,)))
     gain_sum = gain_sum[0:1] / gain[...]
 
-    small = [part.astype(F32) for a in (acc_scale[...], gain_sum) for part in split_bf16(a)]
-    small = [a[:, h * 128 : h * 128 + 128] for a in small for h in (0, 1)]
-    small = jnp.concatenate(small + [jnp.zeros((EXTRA - 8, 128), F32)], axis=0).astype(BF16)
-    blocks = (acc_q, acc_kv, acc_kv, acc_out)
-    offsets = (0, 0, C, 0)
-    for part in range(PARTS):
-        block, start = divmod(part * PART, C)
-        ref, at = blocks[block], offsets[block]
-        for h in (0, 1):
-            piece = ref[start : start + PART, at + h * 128 : at + h * 128 + 128]
-            sums[part, h * PART : h * PART + PART] = piece.astype(BF16)
-        sums[part, 2 * PART :] = small
+    for ref, half in ((keep, place[2]), (send, 1 - place[2])):
+        for part in range(PARTS):
+            rows = pl.ds(pl.multiple_of(half * HALF + part * PART, PART), PART)
+            for h in (0, 1):
+                piece = acc[rows, h * 128 : h * 128 + 128]
+                ref[part, h * PART : h * PART + PART] = piece.astype(ref.dtype)
+    small = [part.astype(F32) for part in split_bf16(jnp.concatenate([scale_sum, gain_sum], axis=0))]
+    small = [a[i : i + 1, h * 128 : h * 128 + 128] for a in small for i in (0, 1) for h in (0, 1)]
+    small = jnp.concatenate(small + [jnp.zeros((2 * PART - EXTRA, 128), F32)], axis=0)
+    keep[PARTS] = small
+    send[PARTS] = small.astype(BF16)
+    copy.wait()
 
 
 def token_kernel(
@@ -329,15 +334,37 @@
         grad_own[rows] = grad.reshape(shape) + ext[pl.ds(WIN + 2 * i, 2), own_cols]
 
 
-def call(fn, out_shape, scratch, megabytes, microseconds, *args):
+def result_kernel(place, mine, other, qkv, out):
+    def write(halves):
+        for block in range(4):
+            half = halves[block // 2]
+            for part in range(C // PART):
+                rows = slice(part * PART, part * PART + PART)
+                for h in (0, 1):
+                    piece = half[block % 2 * (C // PART) + part, h * PART : h * PART + PART].astype(F32) / GRID
+                    if block < 3:
+                        qkv[rows, block * C + h * 128 : block * C + h * 128 + 128] = piece
+                    else:
+                        out[rows, h * 128 : h * 128 + 128] = piece
+
+    @pl.when(place[2] == 0)
+    def _():
+        write((mine, other))
+
+    @pl.when(place[2] == 1)
+    def _():
+        write((other, mine))
+
+
+def call(fn, out_shape, scratch, megabytes, microseconds, *args, in_hbm=()):
     vmem = pl.BlockSpec(memory_space=pltpu.VMEM)
     smem = pl.BlockSpec(memory_space=pltpu.SMEM)
     return pl.pallas_call(
         fn,
         out_shape=tuple(jax.ShapeDtypeStruct(s, d) for s, d in out_shape),
         in_specs=[smem if a.dtype == jnp.int32 else vmem for a in args],
-        out_specs=tuple(vmem for _ in out_shape),
-        scratch_shapes=[pltpu.VMEM(s, d) for s, d in scratch],
+        out_specs=tuple(pl.BlockSpec(memory_space=pltpu.HBM) if i in in_hbm else vmem for i in range(len(out_shape))),
+        scratch_shapes=[pltpu.VMEM(s, d) for s, d in scratch] + [pltpu.SemaphoreType.DMA for _ in in_hbm],
         compiler_params=pltpu.CompilerParams(vmem_limit_bytes=megabytes * 1024 * 1024),
         cost_estimate=pl.CostEstimate(flops=microseconds * 1_000_000_000, bytes_accessed=1_000_000, transcendentals=0),
     )(*args)
@@ -360,10 +387,17 @@
 
 
 def run_attention(place, left, right, cot, gain, factor, wqkv, own, halo):
-    outs = [((PARTS, PART_ROWS, 128), BF16), (OWN, BF16), (OWN, BF16), ((ER, EC, 2 * C), BF16)]
-    scratch = [(EXT, BF16)] * 4 + [(EXT, F32)] * 2 + [(OWN, F32)]
-    scratch += [((C, C), F32), ((C, 2 * C), F32), ((C, C), F32), ((1, C), F32), ONES, ((ER, KC, NQ), F32)]
-    return call(attention_kernel, outs, scratch, 28, 9, place, left, right, cot, gain, factor, wqkv, *own, *halo)
+    half = (PARTS + 1, 2 * PART, 128)
+    g_kv = ((ER, EC, 2 * C), BF16)
+    outs = [(half, F32), (half, BF16), (OWN, BF16), (OWN, BF16), g_kv]
+    scratch = [(EXT, BF16)] * 4 + [(EXT, F32)] * 2 + [(OWN, F32), g_kv]
+    scratch += [((4 * C, C), F32), ONES, ((ER, KC, NQ), F32)]
+    args = (place, left, right, cot, gain, factor, wqkv, *own, *halo)
+    return call(attention_kernel, outs, scratch, 28, 9, *args, in_hbm=(4,))
+
+
+def run_result(place, mine, other):
+    return call(result_kernel, [((C, 3 * C), F32), ((C, C), F32)], [], 8, 1, place, mine, other)
 
 
 def run_tokens(up, own, down, left, right, cot, gain, wqkv, wo, att_b, g_q, g_kv):
@@ -384,18 +418,27 @@
     return lax.all_to_all(jnp.broadcast_to(x[None], (size,) + x.shape), axes, 0, 0)
 
 
-def reduce_sums(sums):
-    part = jnp.sum(lax.all_to_all(sums, SPLIT, 0, 0).astype(F32), axis=0).astype(BF16)
-    rest = 512 // PARTS
-    part = jnp.sum(to_all(part, REST, rest).astype(F32), axis=0)
-    small = part[2 * PART :]
-    whole = to_all(part[: 2 * PART].astype(BF16), SPLIT, PARTS)
-    whole = whole.reshape(4, C // PART, 2, PART, 128).transpose(0, 1, 3, 2, 4).reshape(4, C, C)
-    return whole.astype(F32), small
+def resplit(small):
+    total = small[: EXTRA // 2] + small[EXTRA // 2 :]
+    high = lax.reduce_precision(total, 8, 7)
+    return jnp.concatenate([high, total - high], axis=0)
+
+
+def reduce_sums(keep, send):
+    swap = [(0, 1), (1, 0)]
+    chip = keep + lax.ppermute(send, "core", swap).astype(F32)
+    small = jnp.broadcast_to(resplit(chip[PARTS, :EXTRA])[None], (PARTS, EXTRA, 128))
+    parts = jnp.concatenate([chip[:PARTS], small], axis=1).astype(BF16)
+    part = jnp.sum(lax.all_to_all(parts, SPLIT, 0, 0).astype(F32), axis=0)
+    part = jnp.concatenate([part[: 2 * PART], resplit(part[2 * PART :])], axis=0).astype(BF16)
+    part = jnp.sum(to_all(part, REST, RESTS).astype(F32), axis=0)
+    mine = to_all(part[: 2 * PART].astype(BF16), SPLIT, PARTS)
+    other = lax.ppermute(mine, "core", swap)
+    return mine, other, part[2 * PART :]
 
 
 def body(tokens, norm_gain, qkv_weight, head_scale, out_weight, cotangent):
-    place = jnp.stack([lax.axis_index(ROWS) * BR, lax.axis_index(GRP) * BC]).astype(jnp.int32)
+    place = jnp.stack([lax.axis_index(ROWS) * BR, lax.axis_index(GRP) * BC, lax.axis_index("core")]).astype(jnp.int32)
     gain = norm_gain[None]
     factor = jnp.repeat(head_scale / HEAD, HEAD)[None]
     up, down = exchange(tokens[BR - WIN :], tokens[:WIN], ROWS)
@@ -404,7 +447,7 @@
     first_cols = jnp.concatenate([a[:, :PAD] for a in (up, tokens, down)], axis=0)
     left, right = exchange(last_cols, first_cols, GRP)
     halo = run_halo(up, down, gain, qkv_weight)
-    sums, att_b, g_q, g_kv = run_attention(place, left, right, cotangent, gain, factor, qkv_weight, own, halo)
+    keep, send, att_b, g_q, g_kv = run_attention(place, left, right, cotangent, gain, factor, qkv_weight, own, halo)
     out, grad_own, grad_up, grad_down, grad_left, grad_right = run_tokens(
         up, tokens, down, left, right, cotangent, gain, qkv_weight, out_weight, att_b, g_q, g_kv
     )
@@ -423,12 +466,10 @@
         + jnp.pad(from_left.astype(F32), ((0, 0), (0, BC - PAD), (0, 0)))
         + jnp.pad(from_right.astype(F32), ((0, 0), (BC - PAD, 0), (0, 0)))
     )
-    whole, small = reduce_sums(sums)
-    norm_factor = 1.0 / GRID
-    qkv_grad = jnp.concatenate([whole[0], whole[1], whole[2]], axis=1) * norm_factor
-    small = small[:8].reshape(2, 2, C).sum(axis=1) * norm_factor
-    scale_grad = small[0].reshape(HEADS, HEAD)[:, 0]
-    return out, token_grad, small[1], qkv_grad, scale_grad, whole[3] * norm_factor
+    mine, other, small = reduce_sums(keep, send)
+    qkv_grad, out_grad = run_result(place, mine, other)
+    small = (small[: EXTRA // 2] + small[EXTRA // 2 :]).reshape(2, C) / GRID
+    return out, token_grad, small[1], qkv_grad, small[0].reshape(HEADS, HEAD)[:, 0], out_grad
 
 
 def solution(mesh):

time: 117 us -> 113 us (0.966)
  the two profiles are of different devices: /device:TPU:8 before, /device:TPU:1 now
where the time goes in v3:
time: 113 us; the launch traced here: 112 us
  starting transfers between devices  63.5 us (56%)
  waiting for transfers between devices  17.8 us (16%)
  Pallas kernels  16.4 us (15%)
  local copies, waits for them, and re-layouts  11 us (10%)
  other arithmetic  2.63 us (2%)
    all_to_all x1, starting transfers between devices, reduce_sums(): part = jnp.sum(lax.all_to_all(parts, SPLIT, 0, 0).astype(F32), axis=0)  17.1 us
    pallas_call x5, Pallas kernels, call(): pl.pallas_call(fn, out_shape=tuple((jax.ShapeDtypeStruct(s, d) for s, d i...  16.4 us
    ppermute x4, starting transfers between devices, exchange(): lax.ppermute(last, axes, forward)  14.5 us
    all_to_all x2, starting transfers between devices, to_all(): lax.all_to_all(jnp.broadcast_to(x[None], (size,) + x.shape), axes, 0, 0)  13.7 us
    all_to_all x2, waiting for transfers between devices, to_all(): lax.all_to_all(jnp.broadcast_to(x[None], (size,) + x.shape), axes, 0, 0)  10.8 us
    ppermute x4, starting transfers between devices, exchange(): lax.ppermute(first, axes, backward)  10.2 us
    unnamed x24, local copies, waits for them, and re-layouts  7.01 us
    all_to_all x1, waiting for transfers between devices, reduce_sums(): part = jnp.sum(lax.all_to_all(parts, SPLIT, 0, 0).astype(F32), axis=0)  5.75 us
  transfers between devices with their start and end apart: 13, of which 5 were waited for; matrix products, arithmetic and copies ran while one was open for 4% of the time, Pallas kernels for 5%

profile of v3, /device:TPU:1, one launch (start us, length us, event | category | flops | bytes accessed | tf_op | source)
XLA Modules:
  0.0 112.2 jit_solution(17229300801480755504)
XLA Ops:
  0.6 1.1 fusion.9
  1.7 1.3 %collective-permute-start.1 = (bf16[3,128,256]{2,1,0:T(8,128)(2,1)S(1)}, bf16[3,128,256]{2,1,0:T(8,128)(2,1)S(1)}, u32[]{:S(2)}, u32[]{:S(2)}) collective-permute-start(bf16[3,128,256]{2,1,0:T(8,128)(2,1)S(1)} %get-tuple-element.62), channel_id=1, source_target_pairs={{4,0},{8,4},{12,8},{16,12},{20,16},{24,20},{28,24},{32,28},{36,32}... | collective-permute-start | bytes 589832 | tf_op jit(solution)/shard_map/ppermute | solution.py:414
  3.0 4.7 %collective-permute-start = (bf16[3,128,256]{2,1,0:T(8,128)(2,1)S(1)}, bf16[3,128,256]{2,1,0:T(8,128)(2,1)S(1)}, u32[]{:S(2)}, u32[]{:S(2)}) collective-permute-start(bf16[3,128,256]{2,1,0:T(8,128)(2,1)S(1)} %get-tuple-element.63), channel_id=1, source_target_pairs={{0,4},{4,8},{8,12},{12,16},{16,20},{20,24},{24,28},{28,32},{32,36}... | collective-permute-start | bytes 589832 | tf_op jit(solution)/shard_map/ppermute | solution.py:414
  8.6 0.9 copy-done
  9.5 1.0 copy-done.2
  10.5 0.9 copy-done.4
  11.5 0.9 copy-done.6
  13.0 1.2 %shard_map.109 = (bf16[4,128,256]{2,1,0:T(8,128)(2,1)S(1)}, bf16[4,128,256]{2,1,0:T(8,128)(2,1)S(1)}, bf16[4,128,256]{2,1,0:T(8,128)(2,1)S(1)}, f32[4,128,256]{2...) custom-call(bf16[4,128,256]{2,1,0:T(8,128)(2,1)S(1)} %copy-done, ...), custom_call_target="tpu_custom_call" | custom-call | flops 3000000000 | bytes 1000000 | tf_op jit(solution)/shard_map/pallas_call | solution.py:362
  14.3 4.4 %collective-permute-start.2 = (bf16[10,8,256]{2,1,0:T(8,128)(2,1)S(1)}, bf16[10,8,256]{2,1,0:T(8,128)(2,1)S(1)}, u32[]{:S(2)}, u32[]{:S(2)}) collective-permute-start(bf16[10,8,256]{2,1,0:T(8,128)(2,1)S(1)} %pad_maximum_fusion.1), channel_id=1, source_target_pairs={{0,1},{1,2},{2,3},{4,5},{5,6},{6,7},{8,9},{9,10},{10,11},{12,13},{... | collective-permute-start | bytes 122888 | tf_op jit(solution)/shard_map/ppermute | solution.py:414
  18.7 5.7 %collective-permute-start.3 = (bf16[10,8,256]{2,1,0:T(8,128)(2,1)S(1)}, bf16[10,8,256]{2,1,0:T(8,128)(2,1)S(1)}, u32[]{:S(2)}, u32[]{:S(2)}) collective-permute-start(bf16[10,8,256]{2,1,0:T(8,128)(2,1)S(1)} %pad_maximum_fusion.2), channel_id=1, source_target_pairs={{1,0},{2,1},{3,2},{5,4},{6,5},{7,6},{9,8},{10,9},{11,10},{13,12},{... | collective-permute-start | bytes 122888 | tf_op jit(solution)/shard_map/ppermute | solution.py:414
  24.4 0.8 shard_map.110
  25.3 9.6 %shard_map.111 = (f32[33,32,128]{2,1,0:T(8,128)S(1)}, bf16[33,32,128]{2,1,0:T(8,128)(2,1)S(1)}, bf16[4,128,256]{2,1,0:T(8,128)(2,1)S(1)}, bf16[4,128,256]{2,1,0:T(8,128)(2,1)S(1)}, bf16[10,144,512]{2,1,0:T(8,128)(2,1)S(1)}) custom-call(s32[3]{0:T(128)S(1)} %pad_add_fusion.place, bf16[10,8,256]{2,1,0:T(8,128)(2,1)S(1)} %collective-permute-done.2.left, ...), custom_call_target="tpu_custom_call" | custom-call | flops 8999999488 | bytes 1000000 | tf_op jit(solution)/shard_map/pallas_call | solution.py:362
  34.9 1.1 %copy-done.10 = bf16[10,144,512]{2,1,0:T(8,128)(2,1)} copy-done((bf16[10,144,512]{2,1,0:T(8,128)(2,1)}, bf16[10,144,512]{2,1,0:T(8,128)(2,1)S(1)}, u32[]{:S(2)}) %copy-start.10) | copy-done | bytes 1474584
  36.1 2.2 %collective-permute-start.8 = (bf16[33,32,128]{2,1,0:T(8,128)(2,1)S(1)}, bf16[33,32,128]{2,1,0:T(8,128)(2,1)S(1)}, u32[]{:S(2)}, u32[]{:S(2)}) collective-permute-start(bf16[33,32,128]{2,1,0:T(8,128)(2,1)S(1)} %get-tuple-element.53), channel_id=1, source_target_pairs={{0,1},{1,0},{2,3},{3,2},{4,5},{5,4},{6,7},{7,6},{8,9},{9,8},{10,11... | collective-permute-start | bytes 811016 | tf_op jit(solution)/shard_map/ppermute | solution.py:429
  38.3 1.2 %collective-permute-done.8 = bf16[33,32,128]{2,1,0:T(8,128)(2,1)S(1)} collective-permute-done((bf16[33,32,128]{2,1,0:T(8,128)(2,1)S(1)}, bf16[33,32,128]{2,1,0:T(8,128)(2,1)S(1)}, u32[]{:S(2)}, u32[]{:S(2)}) %collective-permute-start.8) | collective-permute-done | bytes 270368 | tf_op jit(solution)/shard_map/ppermute | solution.py:429
  39.7 0.8 pad_maximum_fusion
  40.4 17.1 %all-to-all-start = ((bf16[32,40,128]{2,1,0:T(8,128)(2,1)}), bf16[32,40,128]{2,1,0:T(8,128)(2,1)S(1)}, u32[]{:S(2)}, u32[]{:S(2)}) async-start(bf16[32,40,128]{2,1,0:T(8,128)(2,1)} %pad_maximum_fusion), calls=%async_computation | async-start | bytes 655360 | tf_op jit(solution)/shard_map/all_to_all | solution.py:432
  57.6 1.4 %copy-done.11 = bf16[10,144,512]{2,1,0:T(8,128)(2,1)S(1)} copy-done((bf16[10,144,512]{2,1,0:T(8,128)(2,1)S(1)}, bf16[10,144,512]{2,1,0:T(8,128)(2,1)}, u32[]{:S(2)}) %copy-start.11) | copy-done | bytes 1474584
  59.0 3.2 %shard_map.112 = (bf16[4,128,256]{2,1,0:T(8,128)(2,1)}, f32[4,128,256]{2,1,0:T(8,128)S(1)}, bf16[3,144,256]{2,1,0:T(8,128)(2,1)S(1)}, bf16[3,144,256]{2,1,0:T(8,...) custom-call(bf16[3,128,256]{2,1,0:T(8,128)(2,1)S(1)} %collective-permute-done.up, ...), custom_call_target="tpu_custom_call" | custom-call | flops 4000000000 | bytes 1000000 | tf_op jit(solution)/shard_map/pallas_call | solution.py:362
  62.2 1.3 %collective-permute-start.4 = (bf16[3,144,256]{2,1,0:T(8,128)(2,1)S(1)}, bf16[3,144,256]{2,1,0:T(8,128)(2,1)S(1)}, u32[]{:S(2)}, u32[]{:S(2)}) collective-permute-start(bf16[3,144,256]{2,1,0:T(8,128)(2,1)S(1)} %get-tuple-element.48), channel_id=1, source_target_pairs={{0,4},{4,8},{8,12},{12,16},{16,20},{20,24},{24,28},{28,32},{32,36}... | collective-permute-start | bytes 663560 | tf_op jit(solution)/shard_map/ppermute | solution.py:414
  63.5 1.3 %collective-permute-start.5 = (bf16[3,144,256]{2,1,0:T(8,128)(2,1)S(1)}, bf16[3,144,256]{2,1,0:T(8,128)(2,1)S(1)}, u32[]{:S(2)}, u32[]{:S(2)}) collective-permute-start(bf16[3,144,256]{2,1,0:T(8,128)(2,1)S(1)} %get-tuple-element.49), channel_id=1, source_target_pairs={{4,0},{8,4},{12,8},{16,12},{20,16},{24,20},{28,24},{32,28},{36,32}... | collective-permute-start | bytes 663560 | tf_op jit(solution)/shard_map/ppermute | solution.py:414
  64.8 5.7 %all-to-all-done = bf16[32,40,128]{2,1,0:T(8,128)(2,1)S(1)} async-done(((bf16[32,40,128]{2,1,0:T(8,128)(2,1)}), bf16[32,40,128]{2,1,0:T(8,128)(2,1)S(1)}, u32[]{:S(2)}, u32[]{:S(2)}) %all-to-all-start) | async-done | bytes 327712 | tf_op jit(solution)/shard_map/all_to_all | solution.py:432
  71.3 3.4 %all-to-all-start.1 = ((bf16[8,40,128]{2,1,0:T(8,128)(2,1)}), bf16[8,40,128]{2,1,0:T(8,128)(2,1)S(1)}, u32[]{:S(2)}, u32[]{:S(2)}) async-start(bf16[8,40,128]{2,1,0:T(8,128)(2,1)} %broadcast_in_dim.13), calls=%async_computation.1 | async-start | bytes 163840 | tf_op jit(solution)/shard_map/all_to_all | solution.py:418
  74.7 4.2 %collective-permute-start.6 = (bf16[4,8,256]{2,1,0:T(8,128)(2,1)S(1)}, bf16[4,8,256]{2,1,0:T(8,128)(2,1)S(1)}, u32[]{:S(2)}, u32[]{:S(2)}) collective-permute-start(bf16[4,8,256]{2,1,0:T(8,128)(2,1)S(1)} %get-tuple-element.58), channel_id=1, source_target_pairs={{0,1},{1,2},{2,3},{4,5},{5,6},{6,7},{8,9},{9,10},{10,11},{12,13},{... | collective-permute-start | bytes 49160 | tf_op jit(solution)/shard_map/ppermute | solution.py:414
  78.9 1.9 %collective-permute-start.7 = (bf16[4,8,256]{2,1,0:T(8,128)(2,1)S(1)}, bf16[4,8,256]{2,1,0:T(8,128)(2,1)S(1)}, u32[]{:S(2)}, u32[]{:S(2)}) collective-permute-start(bf16[4,8,256]{2,1,0:T(8,128)(2,1)S(1)} %get-tuple-element.59), channel_id=1, source_target_pairs={{1,0},{2,1},{3,2},{5,4},{6,5},{7,6},{9,8},{10,9},{11,10},{13,12},{... | collective-permute-start | bytes 49160 | tf_op jit(solution)/shard_map/ppermute | solution.py:414
  80.8 1.2 %all-to-all-done.1 = bf16[8,40,128]{2,1,0:T(8,128)(2,1)S(1)} async-done(((bf16[8,40,128]{2,1,0:T(8,128)(2,1)}), bf16[8,40,128]{2,1,0:T(8,128)(2,1)S(1)}, u32[]{:S(2)}, u32[]{:S(2)}) %all-to-all-start.1) | async-done | bytes 81952 | tf_op jit(solution)/shard_map/all_to_all | solution.py:418
  82.0 0.7 broadcast_in_dim.28
  82.8 10.3 %all-to-all-start.2 = ((bf16[32,32,128]{2,1,0:T(8,128)(2,1)}), bf16[32,32,128]{2,1,0:T(8,128)(2,1)S(1)}, u32[]{:S(2)}, u32[]{:S(2)}) async-start(bf16[32,32,128]{2,1,0:T(8,128)(2,1)} %broadcast_in_dim.28), calls=%async_computation.2 | async-start | bytes 524288 | tf_op jit(solution)/shard_map/all_to_all | solution.py:418
  93.2 0.9 fusion.1
  94.1 9.5 %all-to-all-done.2.mine = bf16[32,32,128]{2,1,0:T(8,128)(2,1)S(1)} async-done(((bf16[32,32,128]{2,1,0:T(8,128)(2,1)}), bf16[32,32,128]{2,1,0:T(8,128)(2,1)S(1)}, u32[]{:S(2)}, u32[]{:S(2)}) %all-to-all-start.2) | async-done | bytes 262176 | tf_op jit(solution)/shard_map/all_to_all | solution.py:418
  103.6 5.7 %collective-permute-start.9 = (bf16[32,32,128]{2,1,0:T(8,128)(2,1)S(1)}, bf16[32,32,128]{2,1,0:T(8,128)(2,1)S(1)}, u32[]{:S(2)}, u32[]{:S(2)}) collective-permute-start(bf16[32,32,128]{2,1,0:T(8,128)(2,1)S(1)} %all-to-all-done.2.mine), channel_id=1, source_target_pairs={{0,1},{1,0},{2,3},{3,2},{4,5},{5,4},{6,7},{7,6},{8,9},{9,8},{10,11... | collective-permute-start | bytes 786440 | tf_op jit(solution)/shard_map/ppermute | solution.py:436
  110.7 1.6 %shard_map.113 = (f32[256,768]{1,0:T(8,128)}, f32[256,256]{1,0:T(8,128)}) custom-call(s32[3]{0:T(128)S(1)} %pad_add_fusion.place, bf16[32,32,128]{2,1,0:T(8,128)(2,1)S(1)} %all-to-all-done.2.mine, bf16[32,32,128]{2,1,0:T(8,128)(2,1)S(1)} %collective-permute-done.9.other), custom_call_target="tpu_custom_call" | custom-call | flops 1000000000 | bytes 1000000 | tf_op jit(solution)/shard_map/pallas_call | solution.py:362
  (54 shorter events, 3.9 us)
Async XLA Ops:
  1.7 12.5 %collective-permute-start.1 = (bf16[3,128,256]{2,1,0:T(8,128)(2,1)S(1)}, bf16[3,128,256]{2,1,0:T(8,128)(2,1)S(1)}, u32[]{:S(2)}, u32[]{:S(2)}) collective-permute-start(bf16[3,128,256]{2,1,0:T(8,128)(2,1)S(1)} %get-tuple-element.62), channel_id=1, source_target_pairs={{4,0},{8,4},{12,8},{16,12},{20,16},{24,20},{28,24},{32,28},{36,32}... | collective-permute-start | bytes 589832 | tf_op jit(solution)/shard_map/ppermute | solution.py:414
  3.0 11.3 %collective-permute-start = (bf16[3,128,256]{2,1,0:T(8,128)(2,1)S(1)}, bf16[3,128,256]{2,1,0:T(8,128)(2,1)S(1)}, u32[]{:S(2)}, u32[]{:S(2)}) collective-permute-start(bf16[3,128,256]{2,1,0:T(8,128)(2,1)S(1)} %get-tuple-element.63), channel_id=1, source_target_pairs={{0,4},{4,8},{8,12},{12,16},{16,20},{20,24},{24,28},{28,32},{32,36}... | collective-permute-start | bytes 589832 | tf_op jit(solution)/shard_map/ppermute | solution.py:414
  8.6 1.0 copy-start
  9.5 1.0 copy-start.2
  10.5 0.9 copy-start.4
  11.5 0.9 copy-start.6
  12.4 0.7 copy-start.8
  13.0 11.4 %copy-start.3 = (bf16[256,768]{1,0:T(8,128)(2,1)S(1)}, bf16[256,768]{1,0:T(8,128)(2,1)}, u32[]{:S(2)}) copy-start(bf16[256,768]{1,0:T(8,128)(2,1)} %wqkv.7) | copy-start | bytes 1179652
  14.3 10.9 %collective-permute-start.2 = (bf16[10,8,256]{2,1,0:T(8,128)(2,1)S(1)}, bf16[10,8,256]{2,1,0:T(8,128)(2,1)S(1)}, u32[]{:S(2)}, u32[]{:S(2)}) collective-permute-start(bf16[10,8,256]{2,1,0:T(8,128)(2,1)S(1)} %pad_maximum_fusion.1), channel_id=1, source_target_pairs={{0,1},{1,2},{2,3},{4,5},{5,6},{6,7},{8,9},{9,10},{10,11},{12,13},{... | collective-permute-start | bytes 122888 | tf_op jit(solution)/shard_map/ppermute | solution.py:414
  18.7 6.6 %copy-start.5 = (bf16[4,128,256]{2,1,0:T(8,128)(2,1)S(1)}, bf16[4,128,256]{2,1,0:T(8,128)(2,1)}, u32[]{:S(2)}) copy-start(bf16[4,128,256]{2,1,0:T(8,128)(2,1)} %cot.5) | copy-start | bytes 786436
  18.7 6.6 %copy-start.9 = (f32[256]{0:T(256)S(1)}, f32[256]{0:T(256)}, u32[]{:S(2)}) copy-start(f32[256]{0:T(256)} %param.7) | copy-start | bytes 3076
  18.7 6.6 %collective-permute-start.3 = (bf16[10,8,256]{2,1,0:T(8,128)(2,1)S(1)}, bf16[10,8,256]{2,1,0:T(8,128)(2,1)S(1)}, u32[]{:S(2)}, u32[]{:S(2)}) collective-permute-start(bf16[10,8,256]{2,1,0:T(8,128)(2,1)S(1)} %pad_maximum_fusion.2), channel_id=1, source_target_pairs={{1,0},{2,1},{3,2},{5,4},{6,5},{7,6},{9,8},{10,9},{11,10},{13,12},{... | collective-permute-start | bytes 122888 | tf_op jit(solution)/shard_map/ppermute | solution.py:414
  34.9 1.2 %copy-start.10 = (bf16[10,144,512]{2,1,0:T(8,128)(2,1)}, bf16[10,144,512]{2,1,0:T(8,128)(2,1)S(1)}, u32[]{:S(2)}) copy-start(bf16[10,144,512]{2,1,0:T(8,128)(2,1)S(1)} %get-tuple-element.45.g_kv) | copy-start | bytes 4423684
  36.1 3.4 %collective-permute-start.8 = (bf16[33,32,128]{2,1,0:T(8,128)(2,1)S(1)}, bf16[33,32,128]{2,1,0:T(8,128)(2,1)S(1)}, u32[]{:S(2)}, u32[]{:S(2)}) collective-permute-start(bf16[33,32,128]{2,1,0:T(8,128)(2,1)S(1)} %get-tuple-element.53), channel_id=1, source_target_pairs={{0,1},{1,0},{2,3},{3,2},{4,5},{5,4},{6,7},{7,6},{8,9},{9,8},{10,11... | collective-permute-start | bytes 811016 | tf_op jit(solution)/shard_map/ppermute | solution.py:429
  39.5 18.1 %copy-start.1 = (bf16[4,128,256]{2,1,0:T(8,128)(2,1)S(1)}, bf16[4,128,256]{2,1,0:T(8,128)(2,1)}, u32[]{:S(2)}) copy-start(bf16[4,128,256]{2,1,0:T(8,128)(2,1)} %own.3) | copy-start | bytes 786436
  39.5 18.1 %copy-start.7 = (bf16[256,256]{1,0:T(8,128)(2,1)S(1)}, bf16[256,256]{1,0:T(8,128)(2,1)}, u32[]{:S(2)}) copy-start(bf16[256,256]{1,0:T(8,128)(2,1)} %wo.3) | copy-start | bytes 393220
  40.4 30.1 %all-to-all-start = ((bf16[32,40,128]{2,1,0:T(8,128)(2,1)}), bf16[32,40,128]{2,1,0:T(8,128)(2,1)S(1)}, u32[]{:S(2)}, u32[]{:S(2)}) async-start(bf16[32,40,128]{2,1,0:T(8,128)(2,1)} %pad_maximum_fusion), calls=%async_computation | async-start | bytes 655360 | tf_op jit(solution)/shard_map/all_to_all | solution.py:432
  57.6 1.4 %copy-start.11 = (bf16[10,144,512]{2,1,0:T(8,128)(2,1)S(1)}, bf16[10,144,512]{2,1,0:T(8,128)(2,1)}, u32[]{:S(2)}) copy-start(bf16[10,144,512]{2,1,0:T(8,128)(2,1)} %copy-done.10) | copy-start | bytes 4423684
  62.2 12.5 %collective-permute-start.4 = (bf16[3,144,256]{2,1,0:T(8,128)(2,1)S(1)}, bf16[3,144,256]{2,1,0:T(8,128)(2,1)S(1)}, u32[]{:S(2)}, u32[]{:S(2)}) collective-permute-start(bf16[3,144,256]{2,1,0:T(8,128)(2,1)S(1)} %get-tuple-element.48), channel_id=1, source_target_pairs={{0,4},{4,8},{8,12},{12,16},{16,20},{20,24},{24,28},{28,32},{32,36}... | collective-permute-start | bytes 663560 | tf_op jit(solution)/shard_map/ppermute | solution.py:414
  63.5 11.2 %collective-permute-start.5 = (bf16[3,144,256]{2,1,0:T(8,128)(2,1)S(1)}, bf16[3,144,256]{2,1,0:T(8,128)(2,1)S(1)}, u32[]{:S(2)}, u32[]{:S(2)}) collective-permute-start(bf16[3,144,256]{2,1,0:T(8,128)(2,1)S(1)} %get-tuple-element.49), channel_id=1, source_target_pairs={{4,0},{8,4},{12,8},{16,12},{20,16},{24,20},{28,24},{32,28},{36,32}... | collective-permute-start | bytes 663560 | tf_op jit(solution)/shard_map/ppermute | solution.py:414
  71.3 10.7 %all-to-all-start.1 = ((bf16[8,40,128]{2,1,0:T(8,128)(2,1)}), bf16[8,40,128]{2,1,0:T(8,128)(2,1)S(1)}, u32[]{:S(2)}, u32[]{:S(2)}) async-start(bf16[8,40,128]{2,1,0:T(8,128)(2,1)} %broadcast_in_dim.13), calls=%async_computation.1 | async-start | bytes 163840 | tf_op jit(solution)/shard_map/all_to_all | solution.py:418
  74.7 18.5 %collective-permute-start.6 = (bf16[4,8,256]{2,1,0:T(8,128)(2,1)S(1)}, bf16[4,8,256]{2,1,0:T(8,128)(2,1)S(1)}, u32[]{:S(2)}, u32[]{:S(2)}) collective-permute-start(bf16[4,8,256]{2,1,0:T(8,128)(2,1)S(1)} %get-tuple-element.58), channel_id=1, source_target_pairs={{0,1},{1,2},{2,3},{4,5},{5,6},{6,7},{8,9},{9,10},{10,11},{12,13},{... | collective-permute-start | bytes 49160 | tf_op jit(solution)/shard_map/ppermute | solution.py:414
  78.9 14.3 %collective-permute-start.7 = (bf16[4,8,256]{2,1,0:T(8,128)(2,1)S(1)}, bf16[4,8,256]{2,1,0:T(8,128)(2,1)S(1)}, u32[]{:S(2)}, u32[]{:S(2)}) collective-permute-start(bf16[4,8,256]{2,1,0:T(8,128)(2,1)S(1)} %get-tuple-element.59), channel_id=1, source_target_pairs={{1,0},{2,1},{3,2},{5,4},{6,5},{7,6},{9,8},{10,9},{11,10},{13,12},{... | collective-permute-start | bytes 49160 | tf_op jit(solution)/shard_map/ppermute | solution.py:414
  82.8 20.8 %all-to-all-start.2 = ((bf16[32,32,128]{2,1,0:T(8,128)(2,1)}), bf16[32,32,128]{2,1,0:T(8,128)(2,1)S(1)}, u32[]{:S(2)}, u32[]{:S(2)}) async-start(bf16[32,32,128]{2,1,0:T(8,128)(2,1)} %broadcast_in_dim.28), calls=%async_computation.2 | async-start | bytes 524288 | tf_op jit(solution)/shard_map/all_to_all | solution.py:418
  103.6 7.0 %collective-permute-start.9 = (bf16[32,32,128]{2,1,0:T(8,128)(2,1)S(1)}, bf16[32,32,128]{2,1,0:T(8,128)(2,1)S(1)}, u32[]{:S(2)}, u32[]{:S(2)}) collective-permute-start(bf16[32,32,128]{2,1,0:T(8,128)(2,1)S(1)} %all-to-all-done.2.mine), channel_id=1, source_target_pairs={{0,1},{1,0},{2,3},{3,2},{4,5},{5,4},{6,7},{7,6},{8,9},{9,8},{10,11... | collective-permute-start | bytes 786440 | tf_op jit(solution)/shard_map/ppermute | solution.py:436

commit v4 on v3

v4 whole, which is shorter than its diff:
```python
import math

import jax
import jax.numpy as jnp
from jax import lax
from jax.experimental import pallas as pl
from jax.experimental.pallas import tpu as pltpu
from jax.sharding import Mesh, PartitionSpec as P

HEADS = 4
HEAD = 64
C = 256
WIN = 3
BR = 4
BC = 128
GRID = 512

EPS = 1e-06

PAD = 8
ER = BR + 2 * WIN
EC = BC + 2 * PAD
QC = 32
KC = 48
BLOCKS = BC // QC
NQ = BR * QC
NK = ER * KC
PAIRS = HEADS // 2
LANES = 2 * HEAD

AXES = ("z", "xh", "y", "xl", "core")
AXIS_SIZES = (8, 2, 8, 2, 2)
ROWS = ("z", "xh", "y")
GRP = ("xl", "core")
SPLIT = ("z", "xh", "xl")
REST = ("y",)
PARTS = 32
RESTS = 8
HALF = 2 * C
PART = HALF // PARTS
EXTRA = 8

F32 = jnp.float32
BF16 = jnp.bfloat16


def mm(a, b, dims=((1,), (0,))):
    return lax.dot_general(a, b, (dims, ((), ())), preferred_element_type=F32)


def split_bf16(a):
    high = a.astype(BF16)
    return high, (a - high.astype(F32)).astype(BF16)


def row_stats(t):
    n = lax.rsqrt(jnp.mean(t * t, axis=-1, keepdims=True) + EPS)
    return n, t * n


def norm_grad(u, n, hat):
    return n * (u - hat * jnp.mean(u * hat, axis=-1, keepdims=True))


def ones_per_head():
    lane_head = lax.broadcasted_iota(jnp.int32, (C, C), 1) // HEAD
    row_head = lax.broadcasted_iota(jnp.int32, (C, C), 0) // HEAD
    return jnp.where(lane_head == row_head, 1.0 / HEAD, 0.0).astype(BF16)


def per_head_mean(a, ones):
    high, low = split_bf16(a)
    return mm(high, ones) + mm(low, ones)


def normalise(raw, ones):
    inv = lax.rsqrt(per_head_mean(raw * raw, ones) + EPS)
    return raw * inv, inv


def widen(a, rows):
    edge = jnp.zeros((rows, PAD, C), F32)
    return jnp.concatenate([edge, a.reshape(rows, BC, C), edge], axis=1).astype(BF16)


def own_kernel(
    place, own, cot, gain, factor, wqkv, wo, q_b, d_b, normed_own, q_inv, near_mask, normed_ext, k_b, v_b, k_inv, ones
):
    ones[...] = ones_per_head()

    key_row = lax.broadcasted_iota(jnp.int32, (ER, KC, NQ), 0)
    key_col = lax.broadcasted_iota(jnp.int32, (ER, KC, NQ), 1)
    query = lax.broadcasted_iota(jnp.int32, (ER, KC, NQ), 2)
    row_gap = key_row - query // QC
    col_gap = key_col - query % QC - (PAD - WIN)
    in_rows = (key_row + place[0] - WIN >= 0) & (key_row + place[0] - WIN < GRID)
    near = (row_gap >= 0) & (row_gap <= 2 * WIN) & (col_gap >= 0) & (col_gap <= 2 * WIN)
    near_mask[...] = jnp.where(near & in_rows, 1.0, 0.0)

    @pl.loop(0, BR // 2)
    def _(i):
        rows = pl.ds(2 * i, 2)
        shape = (2, BC, C)
        _, hat = row_stats(own[rows].reshape(2 * BC, C).astype(F32))
        scaled = hat * gain[...]
        normed = scaled.astype(BF16)
        projected = mm(normed, wqkv[...])
        q, inv = normalise(projected[:, :C], ones[...])
        k, inv_k = normalise(projected[:, C : 2 * C], ones[...])
        normed_own[rows] = normed.reshape(shape)
        q_inv[rows] = inv.reshape(shape)
        q_b[rows] = (q * factor[...]).astype(BF16).reshape(shape)
        normed_ext[rows] = widen(scaled, 2)
        k_b[rows] = widen(k, 2)
        k_inv[rows] = widen(inv_k, 2)
        v_b[rows] = widen(projected[:, 2 * C :], 2)
        d = mm(cot[rows].reshape(2 * BC, C), wo[...], ((1,), (1,)))
        d_b[rows] = d.astype(BF16).reshape(shape)


def halo_kernel(place, from_a, from_b, gain, wqkv, normed_ext, k_b, v_b, k_inv, ones):
    ones[...] = ones_per_head()
    for ref, at in ((from_a, place[3]), (from_b, 1 - place[3])):
        rows = pl.ds(at * WIN, WIN)
        _, hat = row_stats(ref[...].reshape(WIN * BC, C).astype(F32))
        scaled = hat * gain[...]
        projected = mm(scaled.astype(BF16), wqkv[:, C:])
        k, inv_k = normalise(projected[:, :C], ones[...])
        normed_ext[rows] = widen(scaled, WIN)
        k_b[rows] = widen(k, WIN)
        k_inv[rows] = widen(inv_k, WIN)
        v_b[rows] = widen(projected[:, C:], WIN)


def attention_kernel(
    place,
    from_a,
    from_b,
    cot,
    gain,
    factor,
    wqkv,
    q_b,
    d_b,
    normed_own,
    q_inv,
    near_mask,
    normed_mid,
    k_mid,
    v_mid,
    k_inv_mid,
    normed_halo,
    k_halo,
    v_halo,
    k_inv_halo,
    keep,
    send,
    att_b,
    g_q,
    g_kv_own,
    to_a,
    to_b,
    normed_ext,
    k_b,
    v_b,
    k_inv,
    gk,
    gv,
    gq,
    g_kv,
    acc,
    ones,
):
    ones[...] = ones_per_head()

    odd = place[4] == 1
    left = jnp.where(odd, from_b[...].astype(F32), from_a[...].astype(F32))
    right = jnp.where(odd, from_a[...].astype(F32), from_b[...].astype(F32))
    edges = jnp.concatenate([left, right], axis=0)
    _, hat = row_stats(edges.reshape(2 * ER * PAD, C))
    scaled = hat * gain[...]
    projected = mm(scaled.astype(BF16), wqkv[:, C:])
    k, inv_k = normalise(projected[:, :C], ones[...])
    for ext, mid, halo, edge in (
        (normed_ext, normed_mid, normed_halo, scaled),
        (k_b, k_mid, k_halo, k),
        (v_b, v_mid, v_halo, projected[:, C:]),
        (k_inv, k_inv_mid, k_inv_halo, inv_k),
    ):
        edge = edge.reshape(2 * ER, PAD, C)
        ext[0:WIN] = halo[0:WIN]
        ext[WIN : WIN + BR] = mid[...]
        ext[WIN + BR : ER] = halo[WIN : 2 * WIN]
        near = ext[:, 0 : 2 * PAD].astype(F32)[:, PAD:]
        ext[:, 0 : 2 * PAD] = jnp.concatenate([edge[:ER], near], axis=1).astype(BF16)
        near = ext[:, EC - 2 * PAD : EC].astype(F32)[:, :PAD]
        ext[:, EC - 2 * PAD : EC] = jnp.concatenate([near, edge[ER:]], axis=1).astype(BF16)

    gk[...] = jnp.zeros_like(gk)
    gv[...] = jnp.zeros_like(gv)

    first = lax.broadcasted_iota(jnp.int32, (NQ, LANES), 1) < HEAD
    top = lax.broadcasted_iota(jnp.int32, (LANES, NQ), 0) < HEAD

    def both(a):
        zero = jnp.zeros_like(a)
        return jnp.concatenate([jnp.where(first, a, zero), jnp.where(first, zero, a)], axis=0)

    def own_head(a):
        return jnp.where(top, a[:, :NQ], a[:, NQ:]).T

    @pl.loop(0, BLOCKS, unroll=BLOCKS)
    def _(b):
        q_cols = pl.ds(pl.multiple_of(b * QC, QC), QC)
        k_cols = pl.ds(pl.multiple_of(b * QC, QC), KC)
        col = lax.broadcasted_iota(jnp.int32, (ER, KC, NQ), 1) + (place[1] - PAD + b * QC)
        mask = jnp.where((col >= 0) & (col < GRID), near_mask[...], 0.0).reshape(NK, NQ)
        mask = jnp.concatenate([mask, mask], axis=1)
        for p in range(PAIRS):
            lanes = slice(p * LANES, (p + 1) * LANES)
            k2 = k_b[:, k_cols, lanes].reshape(NK, LANES)
            v2 = v_b[:, k_cols, lanes].reshape(NK, LANES)
            q2 = both(q_b[:, q_cols, lanes].reshape(NQ, LANES))
            d2 = both(d_b[:, q_cols, lanes].reshape(NQ, LANES))
            e = jnp.exp(mm(k2, q2, ((1,), (1,)))) * mask
            attend = e * (1.0 / jnp.sum(e, axis=0, keepdims=True))
            attend_b = attend.astype(BF16)
            grad_probs = mm(v2, d2, ((1,), (1,)))
            delta = jnp.sum(attend * grad_probs, axis=0, keepdims=True)
            grad_scores = (attend * (grad_probs - delta)).astype(BF16)
            attended = own_head(mm(v2, attend_b, ((0,), (0,))))
            att_b[:, q_cols, lanes] = attended.astype(BF16).reshape(BR, QC, LANES)
            grad_query = own_head(mm(k2, grad_scores, ((0,), (0,))))
            gq[:, q_cols, lanes] = grad_query.reshape(BR, QC, LANES)
            gk[:, k_cols, lanes] += mm(grad_scores, q2).reshape(ER, KC, LANES)
            gv[:, k_cols, lanes] += mm(attend_b, d2).reshape(ER, KC, LANES)

    inv_factor = 1.0 / factor[...]
    grad_query = gq[...].reshape(BR * BC, C)
    q_f = q_b[...].reshape(BR * BC, C).astype(F32)
    mean = per_head_mean(grad_query * q_f, ones[...]) * inv_factor
    scale_sum = jnp.sum(mean, axis=0, keepdims=True)
    g = q_inv[...].reshape(BR * BC, C) * (factor[...] * grad_query - q_f * mean)
    g = g.astype(BF16)
    g_q[...] = g.reshape(BR, BC, C)
    acc[3 * C :] = mm(att_b[...].reshape(BR * BC, C), cot[...].reshape(BR * BC, C), ((0,), (0,)))
    acc[:C] = mm(normed_own[...].reshape(BR * BC, C), g, ((0,), (0,)))

    @pl.loop(0, ER // 2, unroll=ER // 2)
    def _(i):
        rows = pl.ds(2 * i, 2)
        shape = (2, EC, C)
        grad_key = gk[rows].reshape(2 * EC, C)
        k_f = k_b[rows].reshape(2 * EC, C).astype(F32)
        mean = per_head_mean(grad_key * k_f, ones[...])
        g_k = k_inv[rows].reshape(2 * EC, C).astype(F32) * (grad_key - k_f * mean)
        g_kv[rows, :, :C] = g_k.astype(BF16).reshape(shape)
        g_kv[rows, :, C:] = gv[rows].astype(BF16)

    g_kv_own[...] = g_kv[WIN : WIN + BR]
    for ref, at in ((to_a, place[3]), (to_b, 1 - place[3])):
        g = g_kv[pl.ds(at * (WIN + BR), WIN)].reshape(WIN * EC, 2 * C)
        ref[...] = mm(g, wqkv[:, C:], ((1,), (1,))).astype(BF16).reshape(WIN, EC, C)

    acc_kv = mm(normed_ext[...].reshape(ER * EC, C), g_kv[...].reshape(ER * EC, 2 * C), ((0,), (0,)))
    acc[C : 2 * C] = acc_kv[:, :C]
    acc[2 * C : 3 * C] = acc_kv[:, C:]

    by_feature = (
        wqkv[:, :C].astype(F32) * acc[:C]
        + wqkv[:, C : 2 * C].astype(F32) * acc[C : 2 * C]
        + wqkv[:, 2 * C :].astype(F32) * acc[2 * C : 3 * C]
    )
    high, low = split_bf16(by_feature)
    every = jnp.ones((8, C), BF16)
    gain_sum = mm(every, high, ((1,), (1,))) + mm(every, low, ((1,), (1,)))
    gain_sum = gain_sum[0:1] / gain[...]

    for ref, half in ((keep, place[2]), (send, 1 - place[2])):
        for part in range(PARTS):
            rows = pl.ds(pl.multiple_of(half * HALF + part * PART, PART), PART)
            for h in (0, 1):
                piece = acc[rows, h * 128 : h * 128 + 128]
                ref[part, h * PART : h * PART + PART] = piece.astype(ref.dtype)
    small = [part.astype(F32) for part in split_bf16(jnp.concatenate([scale_sum, gain_sum], axis=0))]
    small = [a[i : i + 1, h * 128 : h * 128 + 128] for a in small for i in (0, 1) for h in (0, 1)]
    small = jnp.concatenate(small + [jnp.zeros((2 * PART - EXTRA, 128), F32)], axis=0)
    keep[PARTS] = small
    send[PARTS] = small.astype(BF16)


def own_grad_kernel(
    place, own, wqkv, wo, att_b, g_q, g_kv_own, from_a, from_b, out, grad_normed, to_a, to_b, total
):
    total[...] = mm(g_kv_own[...].reshape(BR * EC, 2 * C), wqkv[:, C:], ((1,), (1,))).reshape(BR, EC, C)
    total[pl.ds(place[3], WIN)] += from_a[...].astype(F32)
    total[pl.ds(1 - place[3], WIN)] += from_b[...].astype(F32)
    left = total[:, :PAD]
    right = total[:, PAD + BC :]
    odd = place[4] == 1
    to_a[...] = jnp.where(odd, right, left).astype(BF16)
    to_b[...] = jnp.where(odd, left, right).astype(BF16)
    by_query = mm(g_q[...].reshape(BR * BC, C), wqkv[:, :C], ((1,), (1,)))
    grad_normed[...] = by_query.reshape(OWN) + total[:, PAD : PAD + BC]
    projected = mm(att_b[...].reshape(BR * BC, C), wo[...])
    out[...] = (own[...].astype(F32) + projected.reshape(OWN)).astype(BF16)


def token_kernel(place, own, cot, gain, grad_normed, from_a, from_b, token_grad, total):
    odd = place[4] == 1
    total[...] = grad_normed[...]
    total[:, :PAD] += jnp.where(odd, from_b[...].astype(F32), from_a[...].astype(F32))
    total[:, BC - PAD :] += jnp.where(odd, from_a[...].astype(F32), from_b[...].astype(F32))
    n, hat = row_stats(own[...].reshape(BR * BC, C).astype(F32))
    grad = norm_grad(gain[...] * total[...].reshape(BR * BC, C), n, hat)
    token_grad[...] = cot[...].astype(F32) + grad.reshape(OWN)


def edge_kernel(place, rows_a, rows_b, own, to_a, to_b, last, first):
    parts = ((rows_a, place[3] * (WIN + BR)), (rows_b, (1 - place[3]) * (WIN + BR)), (own, WIN))
    for ref, at in parts:
        rows = pl.ds(at, ref.shape[0])
        last[rows] = ref[:, BC - 2 * PAD :].astype(F32)[:, PAD:]
        first[rows] = ref[:, : 2 * PAD].astype(F32)[:, :PAD]
    odd = place[4] == 1
    to_a[...] = jnp.where(odd, last[...], first[...]).astype(BF16)
    to_b[...] = jnp.where(odd, first[...], last[...]).astype(BF16)


def resplit(small):
    total = small[: EXTRA // 2] + small[EXTRA // 2 :]
    high, low = split_bf16(total)
    return jnp.concatenate([high.astype(F32), low.astype(F32)], axis=0)


def chip_kernel(keep, received, parts):
    total = keep[:PARTS] + received[:PARTS].astype(F32)
    small = resplit((keep[PARTS] + received[PARTS].astype(F32))[:EXTRA])
    small = jnp.broadcast_to(small[None], (PARTS, EXTRA, 128))
    parts[...] = jnp.concatenate([total, small], axis=1).astype(BF16)


def part_kernel(parts, copies):
    part = jnp.sum(parts[...].astype(F32), axis=0)
    part = jnp.concatenate([part[: 2 * PART], resplit(part[2 * PART :])], axis=0)
    copies[...] = jnp.broadcast_to(part[None], copies.shape).astype(BF16)


def whole_kernel(parts, copies, small):
    part = jnp.sum(parts[...].astype(F32), axis=0)
    copies[...] = jnp.broadcast_to(part[None, : 2 * PART], copies.shape).astype(BF16)
    last = part[2 * PART :]
    small[...] = (last[: EXTRA // 2] + last[EXTRA // 2 :]) / GRID


def result_kernel(place, mine, other, qkv, out):
    def write(halves):
        for block in range(4):
            half = halves[block // 2]
            for part in range(C // PART):
                rows = slice(part * PART, part * PART + PART)
                for h in (0, 1):
                    piece = half[block % 2 * (C // PART) + part, h * PART : h * PART + PART].astype(F32) / GRID
                    if block < 3:
                        qkv[rows, block * C + h * 128 : block * C + h * 128 + 128] = piece
                    else:
                        out[rows, h * 128 : h * 128 + 128] = piece

    @pl.when(place[2] == 0)
    def _():
        write((mine, other))

    @pl.when(place[2] == 1)
    def _():
        write((other, mine))


def call(fn, out_shape, scratch, megabytes, microseconds, *args):
    vmem = pl.BlockSpec(memory_space=pltpu.VMEM)
    smem = pl.BlockSpec(memory_space=pltpu.SMEM)
    return pl.pallas_call(
        fn,
        out_shape=tuple(jax.ShapeDtypeStruct(s, d) for s, d in out_shape),
        in_specs=[smem if a.dtype == jnp.int32 else vmem for a in args],
        out_specs=tuple(vmem for _ in out_shape),
        scratch_shapes=[pltpu.VMEM(s, d) for s, d in scratch],
        compiler_params=pltpu.CompilerParams(vmem_limit_bytes=megabytes * 1024 * 1024),
        cost_estimate=pl.CostEstimate(flops=microseconds * 1_000_000_000, bytes_accessed=1_000_000, transcendentals=0),
    )(*args)


OWN = (BR, BC, C)
EXT = (ER, EC, C)
ONES = ((C, C), BF16)


def run_own(place, tokens, cotangent, gain, factor, wqkv, wo):
    mid = ((BR, EC, C), BF16)
    outs = [(OWN, BF16), (OWN, BF16), (OWN, BF16), (OWN, F32), ((ER, KC, NQ), F32), mid, mid, mid, mid]
    return call(own_kernel, outs, [ONES], 12, 3, place, tokens, cotangent, gain, factor, wqkv, wo)


def run_halo(place, from_a, from_b, gain, wqkv):
    halo = ((2 * WIN, EC, C), BF16)
    return call(halo_kernel, [halo] * 4, [ONES], 12, 3, place, from_a, from_b, gain, wqkv)


def run_attention(place, from_a, from_b, cot, gain, factor, wqkv, own, halo):
    half = (PARTS + 1, 2 * PART, 128)
    to_rows = ((WIN, EC, C), BF16)
    outs = [(half, F32), (half, BF16), (OWN, BF16), (OWN, BF16), ((BR, EC, 2 * C), BF16), to_rows, to_rows]
    scratch = [(EXT, BF16)] * 4 + [(EXT, F32)] * 2 + [(OWN, F32), ((ER, EC, 2 * C), BF16)]
    scratch += [((4 * C, C), F32), ONES]
    return call(attention_kernel, outs, scratch, 28, 9, place, from_a, from_b, cot, gain, factor, wqkv, *own, *halo)


def run_own_grad(place, own, wqkv, wo, att_b, g_q, g_kv_own, from_a, from_b):
    to_cols = ((BR, PAD, C), BF16)
    outs = [(OWN, BF16), (OWN, F32), to_cols, to_cols]
    scratch = [((BR, EC, C), F32)]
    return call(own_grad_kernel, outs, scratch, 12, 3, place, own, wqkv, wo, att_b, g_q, g_kv_own, from_a, from_b)


def run_tokens(place, own, cot, gain, grad_normed, from_a, from_b):
    return call(token_kernel, [(OWN, F32)], [(OWN, F32)], 12, 2, place, own, cot, gain, grad_normed, from_a, from_b)[0]


def run_result(place, mine, other):
    return call(result_kernel, [((C, 3 * C), F32), ((C, C), F32)], [], 8, 1, place, mine, other)


def swap(a, b, axes):
    size = math.prod(AXIS_SIZES[AXES.index(axis)] for axis in axes)
    pairs = [[(i, i + 1) for i in range(at, size - 1, 2)] for at in (1, 0)]
    pairs = [[*some, *((j, i) for i, j in some)] for some in pairs]
    return lax.ppermute(a, axes, pairs[0]), lax.ppermute(b, axes, pairs[1])


def body(tokens, norm_gain, qkv_weight, head_scale, out_weight, cotangent):
    row, col = lax.axis_index(ROWS), lax.axis_index(GRP)
    odd_row, odd_col = row % 2, col % 2
    place = jnp.stack([row * BR, col * BC, lax.axis_index("core"), odd_row, odd_col]).astype(jnp.int32)
    gain = norm_gain[None]
    factor = jnp.repeat(head_scale / HEAD, HEAD)[None]
    cores = [(0, 1), (1, 0)]

    rows_a, rows_b = swap(
        lax.dynamic_slice_in_dim(tokens, odd_row, WIN, 0), lax.dynamic_slice_in_dim(tokens, 1 - odd_row, WIN, 0), ROWS
    )
    own = run_own(place, tokens, cotangent, gain, factor, qkv_weight, out_weight)
    edges = [((ER, PAD, C), BF16)] * 2
    cols_a, cols_b = call(edge_kernel, edges, [((ER, PAD, C), F32)] * 2, 8, 1, place, rows_a, rows_b, tokens)
    cols_a, cols_b = swap(cols_a, cols_b, GRP)
    halo = run_halo(place, rows_a, rows_b, gain, qkv_weight)
    keep, send, att_b, g_q, g_kv_own, rows_a, rows_b = run_attention(
        place, cols_a, cols_b, cotangent, gain, factor, qkv_weight, own, halo
    )

    received = lax.ppermute(send, "core", cores)
    rows = 2 * PART + EXTRA
    (parts,) = call(chip_kernel, [((PARTS, rows, 128), BF16)], [], 8, 1, keep, received)
    parts, rows_a, rows_b = lax.optimization_barrier((parts, rows_a, rows_b))
    parts = lax.all_to_all(parts, SPLIT, 0, 0)
    rows_a, rows_b = swap(rows_a, rows_b, ROWS)
    (copies,) = call(part_kernel, [((RESTS, rows, 128), BF16)], [], 8, 1, parts)
    copies, att_b, g_kv_own = lax.optimization_barrier((copies, att_b, g_kv_own))
    parts = lax.all_to_all(copies, REST, 0, 0)
    out, grad_normed, cols_a, cols_b = run_own_grad(
        place, tokens, qkv_weight, out_weight, att_b, g_q, g_kv_own, rows_a, rows_b
    )
    copies, small = call(whole_kernel, [((PARTS, 2 * PART, 128), BF16), ((EXTRA // 2, 128), F32)], [], 8, 1, parts)
    copies, cols_a, cols_b = lax.optimization_barrier((copies, cols_a, cols_b))
    mine = lax.all_to_all(copies, SPLIT, 0, 0)
    cols_a, cols_b = swap(cols_a, cols_b, GRP)
    token_grad = run_tokens(place, tokens, cotangent, gain, grad_normed, cols_a, cols_b)
    other = lax.ppermute(mine, "core", cores)
    qkv_grad, out_grad = run_result(place, mine, other)
    small = small.reshape(2, C)
    return out, token_grad, small[1], qkv_grad, small[0].reshape(HEADS, HEAD)[:, 0], out_grad


def solution(mesh):
    fine = Mesh(mesh.devices.reshape(AXIS_SIZES), AXES)
    tiles = P(ROWS, GRP, None)
    return jax.shard_map(
        body,
        mesh=fine,
        in_specs=(tiles, P(), P(), P(), P(), tiles),
        out_specs=(tiles, tiles, P(), P(), P(), P()),
        check_vma=False,
    )
```

time: 113 us -> 108 us (0.956)
  local copies, waits for them, and re-layouts: 11 us -> 5.84 us
  other arithmetic: 2.63 us -> 0.01 us
  Pallas kernels: 16.4 us -> 18.3 us
    unnamed x24 -> x19, local copies, waits for them, and re-layouts: 7.01 us -> 3.83 us
    pallas_call x5 -> x10, Pallas kernels: 16.4 us -> 18.3 us  [call(): pl.pallas_call(fn, out_shape=tuple((jax.ShapeDtypeStruct(s, d) for s, d i...]
    broadcast_in_dim x3 -> x0, local copies, waits for them, and re-layouts: 1.39 us -> none  [the longest x2 1.38 us: to_all(): jnp.broadcast_to(x[None], (size,) + x.shape)]
    ppermute x10, starting transfers between devices: 32.7 us -> 33.9 us  [the longest x8 24.9 us: swap(): return (lax.ppermute(a, axes, pairs[0]), lax.ppermute(b, axes, pairs[1]))]
  transfers between devices with their start and end apart: 13 -> 13, of which waited for: 5 -> 4; matrix products, arithmetic and copies ran while one was open for 4% -> 1% of each run, Pallas kernels for 5% -> 7%
where the time goes in v4:
time: 108 us; the launch traced here: 107 us
  starting transfers between devices  64.3 us (60%)
  Pallas kernels  18.3 us (17%)
  waiting for transfers between devices  17.4 us (16%)
  local copies, waits for them, and re-layouts  5.84 us (5%)
    ppermute x8, starting transfers between devices, swap(): return (lax.ppermute(a, axes, pairs[0]), lax.ppermute(b, axes, pairs[1]))  24.9 us
    pallas_call x10, Pallas kernels, call(): pl.pallas_call(fn, out_shape=tuple((jax.ShapeDtypeStruct(s, d) for s, d i...  18.3 us
    all_to_all x1, starting transfers between devices, body(): parts = lax.all_to_all(parts, SPLIT, 0, 0)  17.5 us
    all_to_all x1, waiting for transfers between devices, body(): parts = lax.all_to_all(parts, SPLIT, 0, 0)  10.2 us
    all_to_all x1, starting transfers between devices, body(): mine = lax.all_to_all(copies, SPLIT, 0, 0)  7.51 us
    ppermute x1, starting transfers between devices, body(): other = lax.ppermute(mine, 'core', cores)  7.06 us
    all_to_all x1, starting transfers between devices, body(): parts = lax.all_to_all(copies, REST, 0, 0)  5.46 us
    all_to_all x1, waiting for transfers between devices, body(): parts = lax.all_to_all(copies, REST, 0, 0)  4.64 us
  transfers between devices with their start and end apart: 13, of which 4 were waited for; matrix products, arithmetic and copies ran while one was open for 1% of the time, Pallas kernels for 7%

profile of v4, /device:TPU:1, one launch (start us, length us, event | category | flops | bytes accessed | tf_op | source)
XLA Modules:
  0.0 106.8 jit_solution(357167405796877224)
XLA Ops:
  0.7 1.1 %constant_dynamic-slice_fusion = (bf16[3,128,256]{2,1,0:T(8,128)(2,1)S(1)}, bf16[3,128,256]{2,1,0:T(8,128)(2,1)S(1)}) fusion(bf16[4,128,256]{2,1,0:T(8,128)(2,1)} %own.7, s32[]{:T(128)S(6)} %select_n.20, s32[]{:T(128)S(6)} %select_n.19), kind=kLoop, calls=%fused_computation.1 | loop fusion | bytes 786440 | tf_op jit(solution)/shard_map/dynamic_slice | solution.py:448
  1.8 4.0 %collective-permute-start.1 = (bf16[3,128,256]{2,1,0:T(8,128)(2,1)S(1)}, bf16[3,128,256]{2,1,0:T(8,128)(2,1)S(1)}, u32[]{:S(2)}, u32[]{:S(2)}) collective-permute-start(bf16[3,128,256]{2,1,0:T(8,128)(2,1)S(1)} %get-tuple-element.84), channel_id=1, source_target_pairs={{0,4},{8,12},{16,20},{24,28},{32,36},{40,44},{48,52},{56,60},{64,6... | collective-permute-start | bytes 589832 | tf_op jit(solution)/shard_map/ppermute | solution.py:436
  5.9 0.7 collective-permute-start
  6.6 0.6 copy-done.8
  7.5 0.7 copy-done.5
  8.1 0.9 copy-done.2
  9.1 1.7 %shard_map.110 = (bf16[4,128,256]{2,1,0:T(8,128)(2,1)S(1)}, bf16[4,128,256]{2,1,0:T(8,128)(2,1)S(1)}, bf16[4,128,256]{2,1,0:T(8,128)(2,1)S(1)}, f32[4,128,256]{2...) custom-call(s32[5]{0:T(128)S(1)} %stack.23.place, ...), custom_call_target="tpu_custom_call" | custom-call | flops 3000000000 | bytes 1000000 | tf_op jit(solution)/shard_map/pallas_call | solution.py:381
  11.4 4.0 %collective-permute-start.2 = (bf16[10,8,256]{2,1,0:T(8,128)(2,1)S(1)}, bf16[10,8,256]{2,1,0:T(8,128)(2,1)S(1)}, u32[]{:S(2)}, u32[]{:S(2)}) collective-permute-start(bf16[10,8,256]{2,1,0:T(8,128)(2,1)S(1)} %get-tuple-element.45), channel_id=1, source_target_pairs={{1,2},{2,1},{5,6},{6,5},{9,10},{10,9},{13,14},{14,13},{17,18},{18,... | collective-permute-start | bytes 122888 | tf_op jit(solution)/shard_map/ppermute | solution.py:436
  15.4 4.0 %collective-permute-start.3 = (bf16[10,8,256]{2,1,0:T(8,128)(2,1)S(1)}, bf16[10,8,256]{2,1,0:T(8,128)(2,1)S(1)}, u32[]{:S(2)}, u32[]{:S(2)}) collective-permute-start(bf16[10,8,256]{2,1,0:T(8,128)(2,1)S(1)} %get-tuple-element.46), channel_id=1, source_target_pairs={{0,1},{2,3},{1,0},{3,2},{4,5},{6,7},{5,4},{7,6},{8,9},{10,11},{9,8... | collective-permute-start | bytes 122888 | tf_op jit(solution)/shard_map/ppermute | solution.py:436
  19.4 1.3 %shard_map.111 = (bf16[6,144,256]{2,1,0:T(8,128)(2,1)S(1)}, bf16[6,144,256]{2,1,0:T(8,128)(2,1)S(1)}, bf16[6,144,256]{2,1,0:T(8,128)(2,1)S(1)}, bf16[6,144,256]{2,1,0:T(8,128)(2,1)S(1)}) custom-call(s32[5]{0:T(128)S(1)} %stack.23.place, bf16[3,128,256]{2,1,0:T(8,128)(2,1)S(1)} %collective-permute-done.rows_a.from_a, ...), custom_call_target="tpu_custom_call" | custom-call | flops 3000000000 | bytes 1000000 | tf_op jit(solution)/shard_map/pallas_call | solution.py:381
  20.7 7.5 %shard_map.112 = (f32[33,32,128]{2,1,0:T(8,128)S(1)}, bf16[33,32,128]{2,1,0:T(8,128)(2,1)S(1)}, bf16[4,128,256]{2,1,0:T(8,128)(2,1)S(1)}, bf16[4,128,256]{2,1,0:...) custom-call(s32[5]{0:T(128)S(1)} %stack.23.place, ...), custom_call_target="tpu_custom_call" | custom-call | flops 8999999488 | bytes 1000000 | tf_op jit(solution)/shard_map/pallas_call | solution.py:381
  28.3 1.9 %collective-permute-start.4 = (bf16[33,32,128]{2,1,0:T(8,128)(2,1)S(1)}, bf16[33,32,128]{2,1,0:T(8,128)(2,1)S(1)}, u32[]{:S(2)}, u32[]{:S(2)}) collective-permute-start(bf16[33,32,128]{2,1,0:T(8,128)(2,1)S(1)} %get-tuple-element.61), channel_id=1, source_target_pairs={{0,1},{1,0},{2,3},{3,2},{4,5},{5,4},{6,7},{7,6},{8,9},{9,8},{10,11... | collective-permute-start | bytes 811016 | tf_op jit(solution)/shard_map/ppermute | solution.py:459
  30.2 1.5 %collective-permute-done.4.received = bf16[33,32,128]{2,1,0:T(8,128)(2,1)S(1)} collective-permute-done((bf16[33,32,128]{2,1,0:T(8,128)(2,1)S(1)}, bf16[33,32,128]{2,1,0:T(8,128)(2,1)S(1)}, u32[]{:S(2)}, u32[]{:S(2)}) %collective-permute-start.4) | collective-permute-done | bytes 270368 | tf_op jit(solution)/shard_map/ppermute | solution.py:459
  31.7 0.8 shard_map.113
  32.5 17.5 %all-to-all-start = ((bf16[32,40,128]{2,1,0:T(8,128)(2,1)}), bf16[32,40,128]{2,1,0:T(8,128)(2,1)S(1)}, u32[]{:S(2)}, u32[]{:S(2)}) async-start(bf16[32,40,128]{2,1,0:T(8,128)(2,1)} %shard_map.113), calls=%async_computation | async-start | bytes 655360 | tf_op jit(solution)/shard_map/all_to_all | solution.py:463
  50.0 0.7 collective-permute-start.5
  50.7 2.1 %collective-permute-start.6 = (bf16[3,144,256]{2,1,0:T(8,128)(2,1)S(1)}, bf16[3,144,256]{2,1,0:T(8,128)(2,1)S(1)}, u32[]{:S(2)}, u32[]{:S(2)}) collective-permute-start(bf16[3,144,256]{2,1,0:T(8,128)(2,1)S(1)} %get-tuple-element.71), channel_id=1, source_target_pairs={{0,4},{8,12},{16,20},{24,28},{32,36},{40,44},{48,52},{56,60},{64,6... | collective-permute-start | bytes 663560 | tf_op jit(solution)/shard_map/ppermute | solution.py:436
  52.8 10.2 %all-to-all-done.parts = bf16[32,40,128]{2,1,0:T(8,128)(2,1)S(1)} async-done(((bf16[32,40,128]{2,1,0:T(8,128)(2,1)}), bf16[32,40,128]{2,1,0:T(8,128)(2,1)S(1)}, u32[]{:S(2)}, u32[]{:S(2)}) %all-to-all-start) | async-done | bytes 327712 | tf_op jit(solution)/shard_map/all_to_all | solution.py:463
  63.1 0.7 shard_map.114
  63.8 5.5 %all-to-all-start.1 = ((bf16[8,40,128]{2,1,0:T(8,128)(2,1)}), bf16[8,40,128]{2,1,0:T(8,128)(2,1)S(1)}, u32[]{:S(2)}, u32[]{:S(2)}) async-start(bf16[8,40,128]{2,1,0:T(8,128)(2,1)} %shard_map.114), calls=%async_computation.1 | async-start | bytes 163840 | tf_op jit(solution)/shard_map/all_to_all | solution.py:467
  69.3 0.9 copy-done.7
  70.2 1.8 %shard_map.115 = (bf16[4,128,256]{2,1,0:T(8,128)(2,1)}, f32[4,128,256]{2,1,0:T(8,128)S(1)}, bf16[4,8,256]{2,1,0:T(8,128)(2,1)S(1)}, bf16[4,8,256]{2,1,0:T(8,128)(2,1)S(1)}) custom-call(s32[5]{0:T(128)S(1)} %stack.23.place, bf16[4,128,256]{2,1,0:T(8,128)(2,1)S(1)} %copy-done, bf16[256,768]{1,0:T(8,128)(2,1)S(1)} %copy-done.1, bf16[256,256]{1,0:T(8,128)(2,1)S(1)} %copy-done.4, ...), custom_call_target="tpu_custom_call" | custom-call | flops 3000000000 | bytes 1000000 | tf_op jit(solution)/shard_map/pallas_call | solution.py:381
  72.0 4.6 %all-to-all-done.1.parts = bf16[8,40,128]{2,1,0:T(8,128)(2,1)S(1)} async-done(((bf16[8,40,128]{2,1,0:T(8,128)(2,1)}), bf16[8,40,128]{2,1,0:T(8,128)(2,1)S(1)}, u32[]{:S(2)}, u32[]{:S(2)}) %all-to-all-start.1) | async-done | bytes 81952 | tf_op jit(solution)/shard_map/all_to_all | solution.py:467
  76.6 0.7 shard_map.116
  77.4 7.5 %all-to-all-start.2 = ((bf16[32,32,128]{2,1,0:T(8,128)(2,1)}), bf16[32,32,128]{2,1,0:T(8,128)(2,1)S(1)}, u32[]{:S(2)}, u32[]{:S(2)}) async-start(bf16[32,32,128]{2,1,0:T(8,128)(2,1)} %get-tuple-element.81), calls=%async_computation.2 | async-start | bytes 524288 | tf_op jit(solution)/shard_map/all_to_all | solution.py:473
  84.9 7.5 %collective-permute-start.7 = (bf16[4,8,256]{2,1,0:T(8,128)(2,1)S(1)}, bf16[4,8,256]{2,1,0:T(8,128)(2,1)S(1)}, u32[]{:S(2)}, u32[]{:S(2)}) collective-permute-start(bf16[4,8,256]{2,1,0:T(8,128)(2,1)S(1)} %get-tuple-element.78), channel_id=1, source_target_pairs={{1,2},{2,1},{5,6},{6,5},{9,10},{10,9},{13,14},{14,13},{17,18},{18,... | collective-permute-start | bytes 49160 | tf_op jit(solution)/shard_map/ppermute | solution.py:436
  92.4 1.9 %collective-permute-start.8 = (bf16[4,8,256]{2,1,0:T(8,128)(2,1)S(1)}, bf16[4,8,256]{2,1,0:T(8,128)(2,1)S(1)}, u32[]{:S(2)}, u32[]{:S(2)}) collective-permute-start(bf16[4,8,256]{2,1,0:T(8,128)(2,1)S(1)} %get-tuple-element.79), channel_id=1, source_target_pairs={{0,1},{2,3},{1,0},{3,2},{4,5},{6,7},{5,4},{7,6},{8,9},{10,11},{9,8... | collective-permute-start | bytes 49160 | tf_op jit(solution)/shard_map/ppermute | solution.py:436
  94.3 1.0 all-to-all-done.2.mine
  95.3 7.1 %collective-permute-start.9 = (bf16[32,32,128]{2,1,0:T(8,128)(2,1)S(1)}, bf16[32,32,128]{2,1,0:T(8,128)(2,1)S(1)}, u32[]{:S(2)}, u32[]{:S(2)}) collective-permute-start(bf16[32,32,128]{2,1,0:T(8,128)(2,1)S(1)} %all-to-all-done.2.mine), channel_id=1, source_target_pairs={{0,1},{1,0},{2,3},{3,2},{4,5},{5,4},{6,7},{7,6},{8,9},{9,8},{10,11... | collective-permute-start | bytes 786440 | tf_op jit(solution)/shard_map/ppermute | solution.py:476
  103.0 0.6 copy.13
  103.6 1.6 %shard_map.117 = f32[4,128,256]{2,1,0:T(8,128)} custom-call(s32[5]{0:T(128)S(1)} %stack.23.place, bf16[4,128,256]{2,1,0:T(8,128)(2,1)S(1)} %copy-done, bf16[4,128,256]{2,1,0:T(8,128)(2,1)S(1)} %copy-done.3, f32[1,256]{1,0:T(1,128)S(1)} %bitcast.13, f32[4,128,256]{2,1,0:T(8,128)S(1)} %get-tuple-element.73.grad_normed, ...), custom_call_target="tpu_custom_call" | custom-call | flops 2000000000 | bytes 1000000 | tf_op jit(solution)/shard_map/pallas_call | solution.py:381
  105.2 1.6 %shard_map.118 = (f32[256,768]{1,0:T(8,128)}, f32[256,256]{1,0:T(8,128)}) custom-call(s32[5]{0:T(128)S(1)} %stack.23.place, bf16[32,32,128]{2,1,0:T(8,128)(2,1)S(1)} %all-to-all-done.2.mine, bf16[32,32,128]{2,1,0:T(8,128)(2,1)S(1)} %collective-permute-done.9.other), custom_call_target="tpu_custom_call" | custom-call | flops 1000000000 | bytes 1000000 | tf_op jit(solution)/shard_map/pallas_call | solution.py:381
  (30 shorter events, 1.5 us)
Async XLA Ops:
  0.7 6.8 %copy-start = (bf16[4,128,256]{2,1,0:T(8,128)(2,1)S(1)}, bf16[4,128,256]{2,1,0:T(8,128)(2,1)}, u32[]{:S(2)}) copy-start(bf16[4,128,256]{2,1,0:T(8,128)(2,1)} %own.7) | copy-start | bytes 786436
  0.7 6.8 %copy-start.1 = (bf16[256,768]{1,0:T(8,128)(2,1)S(1)}, bf16[256,768]{1,0:T(8,128)(2,1)}, u32[]{:S(2)}) copy-start(bf16[256,768]{1,0:T(8,128)(2,1)} %wqkv.7) | copy-start | bytes 1179652
  0.7 6.8 %copy-start.4 = (bf16[256,256]{1,0:T(8,128)(2,1)S(1)}, bf16[256,256]{1,0:T(8,128)(2,1)}, u32[]{:S(2)}) copy-start(bf16[256,256]{1,0:T(8,128)(2,1)} %wo.3) | copy-start | bytes 393220
  1.8 9.0 %collective-permute-start.1 = (bf16[3,128,256]{2,1,0:T(8,128)(2,1)S(1)}, bf16[3,128,256]{2,1,0:T(8,128)(2,1)S(1)}, u32[]{:S(2)}, u32[]{:S(2)}) collective-permute-start(bf16[3,128,256]{2,1,0:T(8,128)(2,1)S(1)} %get-tuple-element.84), channel_id=1, source_target_pairs={{0,4},{8,12},{16,20},{24,28},{32,36},{40,44},{48,52},{56,60},{64,6... | collective-permute-start | bytes 589832 | tf_op jit(solution)/shard_map/ppermute | solution.py:436
  5.9 5.0 %collective-permute-start = (bf16[3,128,256]{2,1,0:T(8,128)(2,1)S(1)}, bf16[3,128,256]{2,1,0:T(8,128)(2,1)S(1)}, u32[]{:S(2)}, u32[]{:S(2)}) collective-permute-start(bf16[3,128,256]{2,1,0:T(8,128)(2,1)S(1)} %get-tuple-element.85), channel_id=1, source_target_pairs={{4,8},{12,16},{20,24},{28,32},{36,40},{44,48},{52,56},{60,64},{68,... | collective-permute-start | bytes 589832 | tf_op jit(solution)/shard_map/ppermute | solution.py:436
  6.5 0.7 copy-start.8
  7.4 0.7 copy-start.5
  8.1 0.9 copy-start.2
  11.4 9.3 %collective-permute-start.2 = (bf16[10,8,256]{2,1,0:T(8,128)(2,1)S(1)}, bf16[10,8,256]{2,1,0:T(8,128)(2,1)S(1)}, u32[]{:S(2)}, u32[]{:S(2)}) collective-permute-start(bf16[10,8,256]{2,1,0:T(8,128)(2,1)S(1)} %get-tuple-element.45), channel_id=1, source_target_pairs={{1,2},{2,1},{5,6},{6,5},{9,10},{10,9},{13,14},{14,13},{17,18},{18,... | collective-permute-start | bytes 122888 | tf_op jit(solution)/shard_map/ppermute | solution.py:436
  15.4 5.3 %collective-permute-start.3 = (bf16[10,8,256]{2,1,0:T(8,128)(2,1)S(1)}, bf16[10,8,256]{2,1,0:T(8,128)(2,1)S(1)}, u32[]{:S(2)}, u32[]{:S(2)}) collective-permute-start(bf16[10,8,256]{2,1,0:T(8,128)(2,1)S(1)} %get-tuple-element.46), channel_id=1, source_target_pairs={{0,1},{2,3},{1,0},{3,2},{4,5},{6,7},{5,4},{7,6},{8,9},{10,11},{9,8... | collective-permute-start | bytes 122888 | tf_op jit(solution)/shard_map/ppermute | solution.py:436
  28.3 4.2 %copy-start.6 = (bf16[4,128,256]{2,1,0:T(8,128)(2,1)}, bf16[4,128,256]{2,1,0:T(8,128)(2,1)S(1)}, u32[]{:S(2)}) copy-start(bf16[4,128,256]{2,1,0:T(8,128)(2,1)S(1)} %get-tuple-element.68.g_q) | copy-start | bytes 786436
  28.3 3.4 %collective-permute-start.4 = (bf16[33,32,128]{2,1,0:T(8,128)(2,1)S(1)}, bf16[33,32,128]{2,1,0:T(8,128)(2,1)S(1)}, u32[]{:S(2)}, u32[]{:S(2)}) collective-permute-start(bf16[33,32,128]{2,1,0:T(8,128)(2,1)S(1)} %get-tuple-element.61), channel_id=1, source_target_pairs={{0,1},{1,0},{2,3},{3,2},{4,5},{5,4},{6,7},{7,6},{8,9},{9,8},{10,11... | collective-permute-start | bytes 811016 | tf_op jit(solution)/shard_map/ppermute | solution.py:459
  32.5 30.6 %all-to-all-start = ((bf16[32,40,128]{2,1,0:T(8,128)(2,1)}), bf16[32,40,128]{2,1,0:T(8,128)(2,1)S(1)}, u32[]{:S(2)}, u32[]{:S(2)}) async-start(bf16[32,40,128]{2,1,0:T(8,128)(2,1)} %shard_map.113), calls=%async_computation | async-start | bytes 655360 | tf_op jit(solution)/shard_map/all_to_all | solution.py:463
  50.0 19.2 %collective-permute-start.5 = (bf16[3,144,256]{2,1,0:T(8,128)(2,1)S(1)}, bf16[3,144,256]{2,1,0:T(8,128)(2,1)S(1)}, u32[]{:S(2)}, u32[]{:S(2)}) collective-permute-start(bf16[3,144,256]{2,1,0:T(8,128)(2,1)S(1)} %get-tuple-element.70), channel_id=1, source_target_pairs={{4,8},{12,16},{20,24},{28,32},{36,40},{44,48},{52,56},{60,64},{68,... | collective-permute-start | bytes 663560 | tf_op jit(solution)/shard_map/ppermute | solution.py:436
  50.7 18.5 %collective-permute-start.6 = (bf16[3,144,256]{2,1,0:T(8,128)(2,1)S(1)}, bf16[3,144,256]{2,1,0:T(8,128)(2,1)S(1)}, u32[]{:S(2)}, u32[]{:S(2)}) collective-permute-start(bf16[3,144,256]{2,1,0:T(8,128)(2,1)S(1)} %get-tuple-element.71), channel_id=1, source_target_pairs={{0,4},{8,12},{16,20},{24,28},{32,36},{40,44},{48,52},{56,60},{64,6... | collective-permute-start | bytes 663560 | tf_op jit(solution)/shard_map/ppermute | solution.py:436
  63.8 12.9 %all-to-all-start.1 = ((bf16[8,40,128]{2,1,0:T(8,128)(2,1)}), bf16[8,40,128]{2,1,0:T(8,128)(2,1)S(1)}, u32[]{:S(2)}, u32[]{:S(2)}) async-start(bf16[8,40,128]{2,1,0:T(8,128)(2,1)} %shard_map.114), calls=%async_computation.1 | async-start | bytes 163840 | tf_op jit(solution)/shard_map/all_to_all | solution.py:467
  69.3 1.0 copy-start.7
  77.4 26.2 %copy-start.3 = (bf16[4,128,256]{2,1,0:T(8,128)(2,1)S(1)}, bf16[4,128,256]{2,1,0:T(8,128)(2,1)}, u32[]{:S(2)}) copy-start(bf16[4,128,256]{2,1,0:T(8,128)(2,1)} %cot.5) | copy-start | bytes 786436
  77.4 17.9 %all-to-all-start.2 = ((bf16[32,32,128]{2,1,0:T(8,128)(2,1)}), bf16[32,32,128]{2,1,0:T(8,128)(2,1)S(1)}, u32[]{:S(2)}, u32[]{:S(2)}) async-start(bf16[32,32,128]{2,1,0:T(8,128)(2,1)} %get-tuple-element.81), calls=%async_computation.2 | async-start | bytes 524288 | tf_op jit(solution)/shard_map/all_to_all | solution.py:473
  84.9 18.7 %collective-permute-start.7 = (bf16[4,8,256]{2,1,0:T(8,128)(2,1)S(1)}, bf16[4,8,256]{2,1,0:T(8,128)(2,1)S(1)}, u32[]{:S(2)}, u32[]{:S(2)}) collective-permute-start(bf16[4,8,256]{2,1,0:T(8,128)(2,1)S(1)} %get-tuple-element.78), channel_id=1, source_target_pairs={{1,2},{2,1},{5,6},{6,5},{9,10},{10,9},{13,14},{14,13},{17,18},{18,... | collective-permute-start | bytes 49160 | tf_op jit(solution)/shard_map/ppermute | solution.py:436
  92.4 11.3 %collective-permute-start.8 = (bf16[4,8,256]{2,1,0:T(8,128)(2,1)S(1)}, bf16[4,8,256]{2,1,0:T(8,128)(2,1)S(1)}, u32[]{:S(2)}, u32[]{:S(2)}) collective-permute-start(bf16[4,8,256]{2,1,0:T(8,128)(2,1)S(1)} %get-tuple-element.79), channel_id=1, source_target_pairs={{0,1},{2,3},{1,0},{3,2},{4,5},{6,7},{5,4},{7,6},{8,9},{10,11},{9,8... | collective-permute-start | bytes 49160 | tf_op jit(solution)/shard_map/ppermute | solution.py:436
  95.3 9.9 %collective-permute-start.9 = (bf16[32,32,128]{2,1,0:T(8,128)(2,1)S(1)}, bf16[32,32,128]{2,1,0:T(8,128)(2,1)S(1)}, u32[]{:S(2)}, u32[]{:S(2)}) collective-permute-start(bf16[32,32,128]{2,1,0:T(8,128)(2,1)S(1)} %all-to-all-done.2.mine), channel_id=1, source_target_pairs={{0,1},{1,0},{2,3},{3,2},{4,5},{5,4},{6,7},{7,6},{8,9},{9,8},{10,11... | collective-permute-start | bytes 786440 | tf_op jit(solution)/shard_map/ppermute | solution.py:476

commit v5 on v4

--- a/solution.py
+++ b/solution.py
@@ -69,8 +69,7 @@
 
 
 def per_head_mean(a, ones):
-    high, low = split_bf16(a)
-    return mm(high, ones) + mm(low, ones)
+    return mm(a.astype(BF16), ones)
 
 
 def normalise(raw, ones):
@@ -118,18 +117,16 @@
         d_b[rows] = d.astype(BF16).reshape(shape)
 
 
-def halo_kernel(place, from_a, from_b, gain, wqkv, normed_ext, k_b, v_b, k_inv, ones):
+def halo_kernel(rows, gain, wqkv, normed_ext, k_b, v_b, k_inv, ones):
     ones[...] = ones_per_head()
-    for ref, at in ((from_a, place[3]), (from_b, 1 - place[3])):
-        rows = pl.ds(at * WIN, WIN)
-        _, hat = row_stats(ref[...].reshape(WIN * BC, C).astype(F32))
-        scaled = hat * gain[...]
-        projected = mm(scaled.astype(BF16), wqkv[:, C:])
-        k, inv_k = normalise(projected[:, :C], ones[...])
-        normed_ext[rows] = widen(scaled, WIN)
-        k_b[rows] = widen(k, WIN)
-        k_inv[rows] = widen(inv_k, WIN)
-        v_b[rows] = widen(projected[:, C:], WIN)
+    _, hat = row_stats(rows[...].reshape(WIN * BC, C).astype(F32))
+    scaled = hat * gain[...]
+    projected = mm(scaled.astype(BF16), wqkv[:, C:])
+    k, inv_k = normalise(projected[:, :C], ones[...])
+    normed_ext[...] = widen(scaled, WIN)
+    k_b[...] = widen(k, WIN)
+    k_inv[...] = widen(inv_k, WIN)
+    v_b[...] = widen(projected[:, C:], WIN)
 
 
 def attention_kernel(
@@ -149,10 +146,14 @@
     k_mid,
     v_mid,
     k_inv_mid,
-    normed_halo,
-    k_halo,
-    v_halo,
-    k_inv_halo,
+    normed_a,
+    k_a,
+    v_a,
+    k_inv_a,
+    normed_b,
+    k_from_b,
+    v_from_b,
+    k_inv_b,
     keep,
     send,
     att_b,
@@ -181,16 +182,16 @@
     scaled = hat * gain[...]
     projected = mm(scaled.astype(BF16), wqkv[:, C:])
     k, inv_k = normalise(projected[:, :C], ones[...])
-    for ext, mid, halo, edge in (
-        (normed_ext, normed_mid, normed_halo, scaled),
-        (k_b, k_mid, k_halo, k),
-        (v_b, v_mid, v_halo, projected[:, C:]),
-        (k_inv, k_inv_mid, k_inv_halo, inv_k),
+    for ext, mid, halo_a, halo_b, edge in (
+        (normed_ext, normed_mid, normed_a, normed_b, scaled),
+        (k_b, k_mid, k_a, k_from_b, k),
+        (v_b, v_mid, v_a, v_from_b, projected[:, C:]),
+        (k_inv, k_inv_mid, k_inv_a, k_inv_b, inv_k),
     ):
         edge = edge.reshape(2 * ER, PAD, C)
-        ext[0:WIN] = halo[0:WIN]
+        ext[pl.ds(place[3] * (WIN + BR), WIN)] = halo_a[...]
+        ext[pl.ds((1 - place[3]) * (WIN + BR), WIN)] = halo_b[...]
         ext[WIN : WIN + BR] = mid[...]
-        ext[WIN + BR : ER] = halo[WIN : 2 * WIN]
         near = ext[:, 0 : 2 * PAD].astype(F32)[:, PAD:]
         ext[:, 0 : 2 * PAD] = jnp.concatenate([edge[:ER], near], axis=1).astype(BF16)
         near = ext[:, EC - 2 * PAD : EC].astype(F32)[:, :PAD]
@@ -400,9 +401,9 @@
     return call(own_kernel, outs, [ONES], 12, 3, place, tokens, cotangent, gain, factor, wqkv, wo)
 
 
-def run_halo(place, from_a, from_b, gain, wqkv):
-    halo = ((2 * WIN, EC, C), BF16)
-    return call(halo_kernel, [halo] * 4, [ONES], 12, 3, place, from_a, from_b, gain, wqkv)
+def run_halo(rows, gain, wqkv):
+    halo = ((WIN, EC, C), BF16)
+    return call(halo_kernel, [halo] * 4, [ONES], 12, 1, rows, gain, wqkv)
 
 
 def run_attention(place, from_a, from_b, cot, gain, factor, wqkv, own, halo):
@@ -433,7 +434,8 @@
     size = math.prod(AXIS_SIZES[AXES.index(axis)] for axis in axes)
     pairs = [[(i, i + 1) for i in range(at, size - 1, 2)] for at in (1, 0)]
     pairs = [[*some, *((j, i) for i, j in some)] for some in pairs]
-    return lax.ppermute(a, axes, pairs[0]), lax.ppermute(b, axes, pairs[1])
+    b = lax.ppermute(b, axes, pairs[1])
+    return lax.ppermute(a, axes, pairs[0]), b
 
 
 def body(tokens, norm_gain, qkv_weight, head_scale, out_weight, cotangent):
@@ -451,7 +453,7 @@
     edges = [((ER, PAD, C), BF16)] * 2
     cols_a, cols_b = call(edge_kernel, edges, [((ER, PAD, C), F32)] * 2, 8, 1, place, rows_a, rows_b, tokens)
     cols_a, cols_b = swap(cols_a, cols_b, GRP)
-    halo = run_halo(place, rows_a, rows_b, gain, qkv_weight)
+    halo = (*run_halo(rows_a, gain, qkv_weight), *run_halo(rows_b, gain, qkv_weight))
     keep, send, att_b, g_q, g_kv_own, rows_a, rows_b = run_attention(
         place, cols_a, cols_b, cotangent, gain, factor, qkv_weight, own, halo
     )
@@ -471,12 +473,14 @@
     copies, small = call(whole_kernel, [((PARTS, 2 * PART, 128), BF16), ((EXTRA // 2, 128), F32)], [], 8, 1, parts)
     copies, cols_a, cols_b = lax.optimization_barrier((copies, cols_a, cols_b))
     mine = lax.all_to_all(copies, SPLIT, 0, 0)
+    small = small.reshape(2, C)
+    scale_grad, gain_grad = small[0].reshape(HEADS, HEAD)[:, 0], small[1]
     cols_a, cols_b = swap(cols_a, cols_b, GRP)
     token_grad = run_tokens(place, tokens, cotangent, gain, grad_normed, cols_a, cols_b)
+    mine, token_grad = lax.optimization_barrier((mine, token_grad))
     other = lax.ppermute(mine, "core", cores)
     qkv_grad, out_grad = run_result(place, mine, other)
-    small = small.reshape(2, C)
-    return out, token_grad, small[1], qkv_grad, small[0].reshape(HEADS, HEAD)[:, 0], out_grad
+    return out, token_grad, gain_grad, qkv_grad, scale_grad, out_grad
 
 
 def solution(mesh):

time: 108 us -> 105 us (0.972)
  starting transfers between devices: 64.3 us -> 62.8 us
    ppermute x1, starting transfers between devices: 7.06 us -> 5.27 us  [body(): other = lax.ppermute(mine, 'core', cores)]
    ppermute x8, waiting for transfers between devices: 0.02 us -> 1.16 us  [the longest x4 1.15 us: swap(): b = lax.ppermute(b, axes, pairs[1])]
    pallas_call x10 -> x11, Pallas kernels: 18.3 us -> 17.4 us  [call(): pl.pallas_call(fn, out_shape=tuple((jax.ShapeDtypeStruct(s, d) for s, d i...]
  transfers between devices with their start and end apart: 13 -> 13, of which waited for: 4 -> 4; matrix products, arithmetic and copies ran while one was open for 1% -> 1% of each run, Pallas kernels for 7% -> 6%
where the time goes in v5:
time: 105 us
  starting transfers between devices  62.8 us (60%)
  waiting for transfers between devices  17.5 us (17%)
  Pallas kernels  17.4 us (17%)
  local copies, waits for them, and re-layouts  5.84 us (6%)
    all_to_all x1, starting transfers between devices, body(): parts = lax.all_to_all(parts, SPLIT, 0, 0)  17.6 us
    pallas_call x11, Pallas kernels, call(): pl.pallas_call(fn, out_shape=tuple((jax.ShapeDtypeStruct(s, d) for s, d i...  17.4 us
    ppermute x4, starting transfers between devices, swap(): return (lax.ppermute(a, axes, pairs[0]), b)  13 us
    ppermute x4, starting transfers between devices, swap(): b = lax.ppermute(b, axes, pairs[1])  12 us
    all_to_all x1, waiting for transfers between devices, body(): parts = lax.all_to_all(parts, SPLIT, 0, 0)  10.4 us
    all_to_all x1, starting transfers between devices, body(): mine = lax.all_to_all(copies, SPLIT, 0, 0)  7.35 us
    all_to_all x1, starting transfers between devices, body(): parts = lax.all_to_all(copies, REST, 0, 0)  5.4 us
    ppermute x1, starting transfers between devices, body(): other = lax.ppermute(mine, 'core', cores)  5.27 us
  transfers between devices with their start and end apart: 13, of which 4 were waited for; matrix products, arithmetic and copies ran while one was open for 1% of the time, Pallas kernels for 6%

profile of v5, /device:TPU:1, one launch (start us, length us, event | category | flops | bytes accessed | tf_op | source)
XLA Modules:
  0.0 104.5 jit_solution(12232367952575900779)
XLA Ops:
  0.7 1.1 %constant_dynamic-slice_fusion = (bf16[3,128,256]{2,1,0:T(8,128)(2,1)S(1)}, bf16[3,128,256]{2,1,0:T(8,128)(2,1)S(1)}) fusion(bf16[4,128,256]{2,1,0:T(8,128)(2,1)} %own.7, s32[]{:T(128)S(6)} %select_n.20, s32[]{:T(128)S(6)} %select_n.19), kind=kLoop, calls=%fused_computation.1 | loop fusion | bytes 786440 | tf_op jit(solution)/shard_map/dynamic_slice | solution.py:450
  1.8 4.0 %collective-permute-start.1 = (bf16[3,128,256]{2,1,0:T(8,128)(2,1)S(1)}, bf16[3,128,256]{2,1,0:T(8,128)(2,1)S(1)}, u32[]{:S(2)}, u32[]{:S(2)}) collective-permute-start(bf16[3,128,256]{2,1,0:T(8,128)(2,1)S(1)} %get-tuple-element.96), channel_id=1, source_target_pairs={{0,4},{8,12},{16,20},{24,28},{32,36},{40,44},{48,52},{56,60},{64,6... | collective-permute-start | bytes 589832 | tf_op jit(solution)/shard_map/ppermute | solution.py:437
  5.9 0.7 collective-permute-start
  6.6 0.6 copy-done.8
  7.5 0.7 copy-done.5
  8.1 0.9 copy-done.2
  9.1 1.6 %shard_map.110 = (bf16[4,128,256]{2,1,0:T(8,128)(2,1)S(1)}, bf16[4,128,256]{2,1,0:T(8,128)(2,1)S(1)}, bf16[4,128,256]{2,1,0:T(8,128)(2,1)S(1)}, f32[4,128,256]{2...) custom-call(s32[5]{0:T(128)S(1)} %stack.23.place, ...), custom_call_target="tpu_custom_call" | custom-call | flops 3000000000 | bytes 1000000 | tf_op jit(solution)/shard_map/pallas_call | solution.py:382
  11.3 4.2 %collective-permute-start.2 = (bf16[10,8,256]{2,1,0:T(8,128)(2,1)S(1)}, bf16[10,8,256]{2,1,0:T(8,128)(2,1)S(1)}, u32[]{:S(2)}, u32[]{:S(2)}) collective-permute-start(bf16[10,8,256]{2,1,0:T(8,128)(2,1)S(1)} %get-tuple-element.51), channel_id=1, source_target_pairs={{1,2},{2,1},{5,6},{6,5},{9,10},{10,9},{13,14},{14,13},{17,18},{18,... | collective-permute-start | bytes 122888 | tf_op jit(solution)/shard_map/ppermute | solution.py:438
  15.4 4.0 %collective-permute-start.3 = (bf16[10,8,256]{2,1,0:T(8,128)(2,1)S(1)}, bf16[10,8,256]{2,1,0:T(8,128)(2,1)S(1)}, u32[]{:S(2)}, u32[]{:S(2)}) collective-permute-start(bf16[10,8,256]{2,1,0:T(8,128)(2,1)S(1)} %get-tuple-element.52), channel_id=1, source_target_pairs={{0,1},{2,3},{1,0},{3,2},{4,5},{6,7},{5,4},{7,6},{8,9},{10,11},{9,8... | collective-permute-start | bytes 122888 | tf_op jit(solution)/shard_map/ppermute | solution.py:437
  20.3 7.2 %shard_map.113 = (f32[33,32,128]{2,1,0:T(8,128)S(1)}, bf16[33,32,128]{2,1,0:T(8,128)(2,1)S(1)}, bf16[4,128,256]{2,1,0:T(8,128)(2,1)S(1)}, bf16[4,128,256]{2,1,0:...) custom-call(s32[5]{0:T(128)S(1)} %stack.23.place, ...), custom_call_target="tpu_custom_call" | custom-call | flops 8999999488 | bytes 1000000 | tf_op jit(solution)/shard_map/pallas_call | solution.py:382
  27.6 2.2 %collective-permute-start.4 = (bf16[33,32,128]{2,1,0:T(8,128)(2,1)S(1)}, bf16[33,32,128]{2,1,0:T(8,128)(2,1)S(1)}, u32[]{:S(2)}, u32[]{:S(2)}) collective-permute-start(bf16[33,32,128]{2,1,0:T(8,128)(2,1)S(1)} %get-tuple-element.71), channel_id=1, source_target_pairs={{0,1},{1,0},{2,3},{3,2},{4,5},{5,4},{6,7},{7,6},{8,9},{9,8},{10,11... | collective-permute-start | bytes 811016 | tf_op jit(solution)/shard_map/ppermute | solution.py:461
  29.7 1.3 %collective-permute-done.4.received = bf16[33,32,128]{2,1,0:T(8,128)(2,1)S(1)} collective-permute-done((bf16[33,32,128]{2,1,0:T(8,128)(2,1)S(1)}, bf16[33,32,128]{2,1,0:T(8,128)(2,1)S(1)}, u32[]{:S(2)}, u32[]{:S(2)}) %collective-permute-start.4) | collective-permute-done | bytes 270368 | tf_op jit(solution)/shard_map/ppermute | solution.py:461
  31.0 0.8 shard_map.114
  31.8 17.6 %all-to-all-start = ((bf16[32,40,128]{2,1,0:T(8,128)(2,1)}), bf16[32,40,128]{2,1,0:T(8,128)(2,1)S(1)}, u32[]{:S(2)}, u32[]{:S(2)}) async-start(bf16[32,40,128]{2,1,0:T(8,128)(2,1)} %shard_map.114), calls=%async_computation | async-start | bytes 655360 | tf_op jit(solution)/shard_map/all_to_all | solution.py:465
  49.4 0.7 collective-permute-start.5
  50.1 2.1 %collective-permute-start.6 = (bf16[3,144,256]{2,1,0:T(8,128)(2,1)S(1)}, bf16[3,144,256]{2,1,0:T(8,128)(2,1)S(1)}, u32[]{:S(2)}, u32[]{:S(2)}) collective-permute-start(bf16[3,144,256]{2,1,0:T(8,128)(2,1)S(1)} %get-tuple-element.81), channel_id=1, source_target_pairs={{0,4},{8,12},{16,20},{24,28},{32,36},{40,44},{48,52},{56,60},{64,6... | collective-permute-start | bytes 663560 | tf_op jit(solution)/shard_map/ppermute | solution.py:437
  52.2 10.4 %all-to-all-done.parts = bf16[32,40,128]{2,1,0:T(8,128)(2,1)S(1)} async-done(((bf16[32,40,128]{2,1,0:T(8,128)(2,1)}), bf16[32,40,128]{2,1,0:T(8,128)(2,1)S(1)}, u32[]{:S(2)}, u32[]{:S(2)}) %all-to-all-start) | async-done | bytes 327712 | tf_op jit(solution)/shard_map/all_to_all | solution.py:465
  62.6 0.7 shard_map.115
  63.3 5.4 %all-to-all-start.1 = ((bf16[8,40,128]{2,1,0:T(8,128)(2,1)}), bf16[8,40,128]{2,1,0:T(8,128)(2,1)S(1)}, u32[]{:S(2)}, u32[]{:S(2)}) async-start(bf16[8,40,128]{2,1,0:T(8,128)(2,1)} %shard_map.115), calls=%async_computation.1 | async-start | bytes 163840 | tf_op jit(solution)/shard_map/all_to_all | solution.py:469
  68.7 0.9 copy-done.7
  69.7 1.8 %shard_map.116 = (bf16[4,128,256]{2,1,0:T(8,128)(2,1)}, f32[4,128,256]{2,1,0:T(8,128)S(1)}, bf16[4,8,256]{2,1,0:T(8,128)(2,1)S(1)}, bf16[4,8,256]{2,1,0:T(8,128)(2,1)S(1)}) custom-call(s32[5]{0:T(128)S(1)} %stack.23.place, bf16[4,128,256]{2,1,0:T(8,128)(2,1)S(1)} %copy-done, bf16[256,768]{1,0:T(8,128)(2,1)S(1)} %copy-done.1, bf16[256,256]{1,0:T(8,128)(2,1)S(1)} %copy-done.4, ...), custom_call_target="tpu_custom_call" | custom-call | flops 3000000000 | bytes 1000000 | tf_op jit(solution)/shard_map/pallas_call | solution.py:382
  71.5 4.6 %all-to-all-done.1.parts = bf16[8,40,128]{2,1,0:T(8,128)(2,1)S(1)} async-done(((bf16[8,40,128]{2,1,0:T(8,128)(2,1)}), bf16[8,40,128]{2,1,0:T(8,128)(2,1)S(1)}, u32[]{:S(2)}, u32[]{:S(2)}) %all-to-all-start.1) | async-done | bytes 81952 | tf_op jit(solution)/shard_map/all_to_all | solution.py:469
  76.1 0.7 shard_map.117
  76.8 7.4 %all-to-all-start.2 = ((bf16[32,32,128]{2,1,0:T(8,128)(2,1)}), bf16[32,32,128]{2,1,0:T(8,128)(2,1)S(1)}, u32[]{:S(2)}, u32[]{:S(2)}) async-start(bf16[32,32,128]{2,1,0:T(8,128)(2,1)} %get-tuple-element.87), calls=%async_computation.2 | async-start | bytes 524288 | tf_op jit(solution)/shard_map/all_to_all | solution.py:475
  84.2 7.5 %collective-permute-start.7 = (bf16[4,8,256]{2,1,0:T(8,128)(2,1)S(1)}, bf16[4,8,256]{2,1,0:T(8,128)(2,1)S(1)}, u32[]{:S(2)}, u32[]{:S(2)}) collective-permute-start(bf16[4,8,256]{2,1,0:T(8,128)(2,1)S(1)} %get-tuple-element.89), channel_id=1, source_target_pairs={{1,2},{2,1},{5,6},{6,5},{9,10},{10,9},{13,14},{14,13},{17,18},{18,... | collective-permute-start | bytes 49160 | tf_op jit(solution)/shard_map/ppermute | solution.py:438
  91.7 1.9 %collective-permute-start.8 = (bf16[4,8,256]{2,1,0:T(8,128)(2,1)S(1)}, bf16[4,8,256]{2,1,0:T(8,128)(2,1)S(1)}, u32[]{:S(2)}, u32[]{:S(2)}) collective-permute-start(bf16[4,8,256]{2,1,0:T(8,128)(2,1)S(1)} %get-tuple-element.90), channel_id=1, source_target_pairs={{0,1},{2,3},{1,0},{3,2},{4,5},{6,7},{5,4},{7,6},{8,9},{10,11},{9,8... | collective-permute-start | bytes 49160 | tf_op jit(solution)/shard_map/ppermute | solution.py:437
  93.6 1.1 %collective-permute-done.8.from_b = bf16[4,8,256]{2,1,0:T(8,128)(2,1)S(1)} collective-permute-done((bf16[4,8,256]{2,1,0:T(8,128)(2,1)S(1)}, bf16[4,8,256]{2,1,0:T(8,128)(2,1)S(1)}, u32[]{:S(2)}, u32[]{:S(2)}) %collective-permute-start.8) | collective-permute-done | bytes 16416 | tf_op jit(solution)/shard_map/ppermute | solution.py:437
  94.8 1.6 %shard_map.118 = f32[4,128,256]{2,1,0:T(8,128)} custom-call(s32[5]{0:T(128)S(1)} %stack.23.place, bf16[4,128,256]{2,1,0:T(8,128)(2,1)S(1)} %copy-done, bf16[4,128,256]{2,1,0:T(8,128)(2,1)S(1)} %copy-done.3, f32[1,256]{1,0:T(1,128)S(1)} %bitcast.14, f32[4,128,256]{2,1,0:T(8,128)S(1)} %get-tuple-element.88.grad_normed, ...), custom_call_target="tpu_custom_call" | custom-call | flops 2000000000 | bytes 1000000 | tf_op jit(solution)/shard_map/pallas_call | solution.py:382
  96.4 5.3 %collective-permute-start.9 = (bf16[32,32,128]{2,1,0:T(8,128)(2,1)S(1)}, bf16[32,32,128]{2,1,0:T(8,128)(2,1)S(1)}, u32[]{:S(2)}, u32[]{:S(2)}) collective-permute-start(bf16[32,32,128]{2,1,0:T(8,128)(2,1)S(1)} %all-to-all-done.2.mine), channel_id=1, source_target_pairs={{0,1},{1,0},{2,3},{3,2},{4,5},{5,4},{6,7},{7,6},{8,9},{9,8},{10,11... | collective-permute-start | bytes 786440 | tf_op jit(solution)/shard_map/ppermute | solution.py:481
  101.7 0.6 fusion
  102.3 0.6 copy.13
  102.9 1.6 %shard_map.119 = (f32[256,768]{1,0:T(8,128)}, f32[256,256]{1,0:T(8,128)}) custom-call(s32[5]{0:T(128)S(1)} %stack.23.place, bf16[32,32,128]{2,1,0:T(8,128)(2,1)S(1)} %all-to-all-done.2.mine, bf16[32,32,128]{2,1,0:T(8,128)(2,1)S(1)} %collective-permute-done.9.other), custom_call_target="tpu_custom_call" | custom-call | flops 1000000000 | bytes 1000000 | tf_op jit(solution)/shard_map/pallas_call | solution.py:382
  (31 shorter events, 1.8 us)
Async XLA Ops:
  0.7 6.8 %copy-start = (bf16[4,128,256]{2,1,0:T(8,128)(2,1)S(1)}, bf16[4,128,256]{2,1,0:T(8,128)(2,1)}, u32[]{:S(2)}) copy-start(bf16[4,128,256]{2,1,0:T(8,128)(2,1)} %own.7) | copy-start | bytes 786436
  0.7 6.8 %copy-start.1 = (bf16[256,768]{1,0:T(8,128)(2,1)S(1)}, bf16[256,768]{1,0:T(8,128)(2,1)}, u32[]{:S(2)}) copy-start(bf16[256,768]{1,0:T(8,128)(2,1)} %wqkv.9) | copy-start | bytes 1179652
  0.7 6.8 %copy-start.4 = (bf16[256,256]{1,0:T(8,128)(2,1)S(1)}, bf16[256,256]{1,0:T(8,128)(2,1)}, u32[]{:S(2)}) copy-start(bf16[256,256]{1,0:T(8,128)(2,1)} %wo.3) | copy-start | bytes 393220
  1.8 8.9 %collective-permute-start.1 = (bf16[3,128,256]{2,1,0:T(8,128)(2,1)S(1)}, bf16[3,128,256]{2,1,0:T(8,128)(2,1)S(1)}, u32[]{:S(2)}, u32[]{:S(2)}) collective-permute-start(bf16[3,128,256]{2,1,0:T(8,128)(2,1)S(1)} %get-tuple-element.96), channel_id=1, source_target_pairs={{0,4},{8,12},{16,20},{24,28},{32,36},{40,44},{48,52},{56,60},{64,6... | collective-permute-start | bytes 589832 | tf_op jit(solution)/shard_map/ppermute | solution.py:437
  5.9 4.8 %collective-permute-start = (bf16[3,128,256]{2,1,0:T(8,128)(2,1)S(1)}, bf16[3,128,256]{2,1,0:T(8,128)(2,1)S(1)}, u32[]{:S(2)}, u32[]{:S(2)}) collective-permute-start(bf16[3,128,256]{2,1,0:T(8,128)(2,1)S(1)} %get-tuple-element.97), channel_id=1, source_target_pairs={{4,8},{12,16},{20,24},{28,32},{36,40},{44,48},{52,56},{60,64},{68,... | collective-permute-start | bytes 589832 | tf_op jit(solution)/shard_map/ppermute | solution.py:438
  6.5 0.7 copy-start.8
  7.4 0.7 copy-start.5
  8.1 0.9 copy-start.2
  11.3 9.1 %collective-permute-start.2 = (bf16[10,8,256]{2,1,0:T(8,128)(2,1)S(1)}, bf16[10,8,256]{2,1,0:T(8,128)(2,1)S(1)}, u32[]{:S(2)}, u32[]{:S(2)}) collective-permute-start(bf16[10,8,256]{2,1,0:T(8,128)(2,1)S(1)} %get-tuple-element.51), channel_id=1, source_target_pairs={{1,2},{2,1},{5,6},{6,5},{9,10},{10,9},{13,14},{14,13},{17,18},{18,... | collective-permute-start | bytes 122888 | tf_op jit(solution)/shard_map/ppermute | solution.py:438
  15.4 4.9 %collective-permute-start.3 = (bf16[10,8,256]{2,1,0:T(8,128)(2,1)S(1)}, bf16[10,8,256]{2,1,0:T(8,128)(2,1)S(1)}, u32[]{:S(2)}, u32[]{:S(2)}) collective-permute-start(bf16[10,8,256]{2,1,0:T(8,128)(2,1)S(1)} %get-tuple-element.52), channel_id=1, source_target_pairs={{0,1},{2,3},{1,0},{3,2},{4,5},{6,7},{5,4},{7,6},{8,9},{10,11},{9,8... | collective-permute-start | bytes 122888 | tf_op jit(solution)/shard_map/ppermute | solution.py:437
  27.5 4.2 %copy-start.6 = (bf16[4,128,256]{2,1,0:T(8,128)(2,1)}, bf16[4,128,256]{2,1,0:T(8,128)(2,1)S(1)}, u32[]{:S(2)}) copy-start(bf16[4,128,256]{2,1,0:T(8,128)(2,1)S(1)} %get-tuple-element.78.g_q) | copy-start | bytes 786436
  27.6 3.4 %collective-permute-start.4 = (bf16[33,32,128]{2,1,0:T(8,128)(2,1)S(1)}, bf16[33,32,128]{2,1,0:T(8,128)(2,1)S(1)}, u32[]{:S(2)}, u32[]{:S(2)}) collective-permute-start(bf16[33,32,128]{2,1,0:T(8,128)(2,1)S(1)} %get-tuple-element.71), channel_id=1, source_target_pairs={{0,1},{1,0},{2,3},{3,2},{4,5},{5,4},{6,7},{7,6},{8,9},{9,8},{10,11... | collective-permute-start | bytes 811016 | tf_op jit(solution)/shard_map/ppermute | solution.py:461
  31.8 30.8 %all-to-all-start = ((bf16[32,40,128]{2,1,0:T(8,128)(2,1)}), bf16[32,40,128]{2,1,0:T(8,128)(2,1)S(1)}, u32[]{:S(2)}, u32[]{:S(2)}) async-start(bf16[32,40,128]{2,1,0:T(8,128)(2,1)} %shard_map.114), calls=%async_computation | async-start | bytes 655360 | tf_op jit(solution)/shard_map/all_to_all | solution.py:465
  49.4 19.3 %collective-permute-start.5 = (bf16[3,144,256]{2,1,0:T(8,128)(2,1)S(1)}, bf16[3,144,256]{2,1,0:T(8,128)(2,1)S(1)}, u32[]{:S(2)}, u32[]{:S(2)}) collective-permute-start(bf16[3,144,256]{2,1,0:T(8,128)(2,1)S(1)} %get-tuple-element.80), channel_id=1, source_target_pairs={{4,8},{12,16},{20,24},{28,32},{36,40},{44,48},{52,56},{60,64},{68,... | collective-permute-start | bytes 663560 | tf_op jit(solution)/shard_map/ppermute | solution.py:438
  50.1 18.6 %collective-permute-start.6 = (bf16[3,144,256]{2,1,0:T(8,128)(2,1)S(1)}, bf16[3,144,256]{2,1,0:T(8,128)(2,1)S(1)}, u32[]{:S(2)}, u32[]{:S(2)}) collective-permute-start(bf16[3,144,256]{2,1,0:T(8,128)(2,1)S(1)} %get-tuple-element.81), channel_id=1, source_target_pairs={{0,4},{8,12},{16,20},{24,28},{32,36},{40,44},{48,52},{56,60},{64,6... | collective-permute-start | bytes 663560 | tf_op jit(solution)/shard_map/ppermute | solution.py:437
  63.3 12.8 %all-to-all-start.1 = ((bf16[8,40,128]{2,1,0:T(8,128)(2,1)}), bf16[8,40,128]{2,1,0:T(8,128)(2,1)S(1)}, u32[]{:S(2)}, u32[]{:S(2)}) async-start(bf16[8,40,128]{2,1,0:T(8,128)(2,1)} %shard_map.115), calls=%async_computation.1 | async-start | bytes 163840 | tf_op jit(solution)/shard_map/all_to_all | solution.py:469
  68.7 1.0 copy-start.7
  76.8 18.0 %copy-start.3 = (bf16[4,128,256]{2,1,0:T(8,128)(2,1)S(1)}, bf16[4,128,256]{2,1,0:T(8,128)(2,1)}, u32[]{:S(2)}) copy-start(bf16[4,128,256]{2,1,0:T(8,128)(2,1)} %cot.5) | copy-start | bytes 786436
  76.8 19.6 %all-to-all-start.2 = ((bf16[32,32,128]{2,1,0:T(8,128)(2,1)}), bf16[32,32,128]{2,1,0:T(8,128)(2,1)S(1)}, u32[]{:S(2)}, u32[]{:S(2)}) async-start(bf16[32,32,128]{2,1,0:T(8,128)(2,1)} %get-tuple-element.87), calls=%async_computation.2 | async-start | bytes 524288 | tf_op jit(solution)/shard_map/all_to_all | solution.py:475
  84.2 9.4 %collective-permute-start.7 = (bf16[4,8,256]{2,1,0:T(8,128)(2,1)S(1)}, bf16[4,8,256]{2,1,0:T(8,128)(2,1)S(1)}, u32[]{:S(2)}, u32[]{:S(2)}) collective-permute-start(bf16[4,8,256]{2,1,0:T(8,128)(2,1)S(1)} %get-tuple-element.89), channel_id=1, source_target_pairs={{1,2},{2,1},{5,6},{6,5},{9,10},{10,9},{13,14},{14,13},{17,18},{18,... | collective-permute-start | bytes 49160 | tf_op jit(solution)/shard_map/ppermute | solution.py:438
  91.7 3.1 %collective-permute-start.8 = (bf16[4,8,256]{2,1,0:T(8,128)(2,1)S(1)}, bf16[4,8,256]{2,1,0:T(8,128)(2,1)S(1)}, u32[]{:S(2)}, u32[]{:S(2)}) collective-permute-start(bf16[4,8,256]{2,1,0:T(8,128)(2,1)S(1)} %get-tuple-element.90), channel_id=1, source_target_pairs={{0,1},{2,3},{1,0},{3,2},{4,5},{6,7},{5,4},{7,6},{8,9},{10,11},{9,8... | collective-permute-start | bytes 49160 | tf_op jit(solution)/shard_map/ppermute | solution.py:437
  96.4 6.5 %collective-permute-start.9 = (bf16[32,32,128]{2,1,0:T(8,128)(2,1)S(1)}, bf16[32,32,128]{2,1,0:T(8,128)(2,1)S(1)}, u32[]{:S(2)}, u32[]{:S(2)}) collective-permute-start(bf16[32,32,128]{2,1,0:T(8,128)(2,1)S(1)} %all-to-all-done.2.mine), channel_id=1, source_target_pairs={{0,1},{1,0},{2,3},{3,2},{4,5},{5,4},{6,7},{7,6},{8,9},{9,8},{10,11... | collective-permute-start | bytes 786440 | tf_op jit(solution)/shard_map/ppermute | solution.py:481

commit v6 on v5

--- a/solution.py
+++ b/solution.py
@@ -239,7 +239,8 @@
     inv_factor = 1.0 / factor[...]
     grad_query = gq[...].reshape(BR * BC, C)
     q_f = q_b[...].reshape(BR * BC, C).astype(F32)
-    mean = per_head_mean(grad_query * q_f, ones[...]) * inv_factor
+    high, low = split_bf16(grad_query * q_f)
+    mean = (mm(high, ones[...]) + mm(low, ones[...])) * inv_factor
     scale_sum = jnp.sum(mean, axis=0, keepdims=True)
     g = q_inv[...].reshape(BR * BC, C) * (factor[...] * grad_query - q_f * mean)
     g = g.astype(BF16)
@@ -317,7 +318,7 @@
     token_grad[...] = cot[...].astype(F32) + grad.reshape(OWN)
 
 
-def edge_kernel(place, rows_a, rows_b, own, to_a, to_b, last, first):
+def edge_kernel(place, rows_b, rows_a, own, to_a, to_b, last, first):
     parts = ((rows_a, place[3] * (WIN + BR)), (rows_b, (1 - place[3]) * (WIN + BR)), (own, WIN))
     for ref, at in parts:
         rows = pl.ds(at, ref.shape[0])
@@ -451,7 +452,7 @@
     )
     own = run_own(place, tokens, cotangent, gain, factor, qkv_weight, out_weight)
     edges = [((ER, PAD, C), BF16)] * 2
-    cols_a, cols_b = call(edge_kernel, edges, [((ER, PAD, C), F32)] * 2, 8, 1, place, rows_a, rows_b, tokens)
+    cols_a, cols_b = call(edge_kernel, edges, [((ER, PAD, C), F32)] * 2, 8, 1, place, rows_b, rows_a, tokens)
     cols_a, cols_b = swap(cols_a, cols_b, GRP)
     halo = (*run_halo(rows_a, gain, qkv_weight), *run_halo(rows_b, gain, qkv_weight))
     keep, send, att_b, g_q, g_kv_own, rows_a, rows_b = run_attention(

time: 105 us -> 104 us (level)
  waiting for transfers between devices: 17.5 us -> 16 us
    all_to_all x1, starting transfers between devices: 7.35 us -> 9.99 us  [body(): mine = lax.all_to_all(copies, SPLIT, 0, 0)]
    ppermute x4, starting transfers between devices: 12 us -> 14.5 us  [swap(): b = lax.ppermute(b, axes, pairs[1])]
    all_to_all x1, starting transfers between devices: 17.6 us -> 15.5 us  [body(): parts = lax.all_to_all(parts, SPLIT, 0, 0)]
    all_to_all x1, starting transfers between devices: 5.4 us -> 3.36 us  [body(): parts = lax.all_to_all(copies, REST, 0, 0)]
    all_to_all x1, waiting for transfers between devices: 10.4 us -> 8.7 us  [body(): parts = lax.all_to_all(parts, SPLIT, 0, 0)]
    ppermute x4, starting transfers between devices: 13 us -> 11.7 us  [swap(): return (lax.ppermute(a, axes, pairs[0]), b)]
  transfers between devices with their start and end apart: 13 -> 13, of which waited for: 4 -> 6; matrix products, arithmetic and copies ran while one was open for 1% -> 1% of each run, Pallas kernels for 6% -> 6%
where the time goes in v6:
time: 104 us; the launch traced here: 103 us
  starting transfers between devices  62.7 us (60%)
  Pallas kernels  17.5 us (17%)
  waiting for transfers between devices  16 us (15%)
  local copies, waits for them, and re-layouts  5.84 us (6%)
    pallas_call x11, Pallas kernels, call(): pl.pallas_call(fn, out_shape=tuple((jax.ShapeDtypeStruct(s, d) for s, d i...  17.5 us
    all_to_all x1, starting transfers between devices, body(): parts = lax.all_to_all(parts, SPLIT, 0, 0)  15.5 us
    ppermute x4, starting transfers between devices, swap(): b = lax.ppermute(b, axes, pairs[1])  14.5 us
    ppermute x4, starting transfers between devices, swap(): return (lax.ppermute(a, axes, pairs[0]), b)  11.7 us
    all_to_all x1, starting transfers between devices, body(): mine = lax.all_to_all(copies, SPLIT, 0, 0)  9.99 us
    all_to_all x1, waiting for transfers between devices, body(): parts = lax.all_to_all(parts, SPLIT, 0, 0)  8.7 us
    ppermute x1, starting transfers between devices, body(): other = lax.ppermute(mine, 'core', cores)  5.58 us
    all_to_all x1, waiting for transfers between devices, body(): parts = lax.all_to_all(copies, REST, 0, 0)  4.55 us
  transfers between devices with their start and end apart: 13, of which 6 were waited for; matrix products, arithmetic and copies ran while one was open for 1% of the time, Pallas kernels for 6%

profile of v6, /device:TPU:1, one launch (start us, length us, event | category | flops | bytes accessed | tf_op | source)
XLA Modules:
  0.0 103.0 jit_solution(10666754215374083479)
XLA Ops:
  0.7 1.1 %constant_dynamic-slice_fusion = (bf16[3,128,256]{2,1,0:T(8,128)(2,1)S(1)}, bf16[3,128,256]{2,1,0:T(8,128)(2,1)S(1)}) fusion(bf16[4,128,256]{2,1,0:T(8,128)(2,1)} %own.7, s32[]{:T(128)S(6)} %select_n.20, s32[]{:T(128)S(6)} %select_n.19), kind=kLoop, calls=%fused_computation.1 | loop fusion | bytes 786440 | tf_op jit(solution)/shard_map/dynamic_slice | solution.py:451
  1.8 0.7 collective-permute-start.1
  2.5 6.6 %collective-permute-start = (bf16[3,128,256]{2,1,0:T(8,128)(2,1)S(1)}, bf16[3,128,256]{2,1,0:T(8,128)(2,1)S(1)}, u32[]{:S(2)}, u32[]{:S(2)}) collective-permute-start(bf16[3,128,256]{2,1,0:T(8,128)(2,1)S(1)} %get-tuple-element.97), channel_id=1, source_target_pairs={{0,4},{8,12},{16,20},{24,28},{32,36},{40,44},{48,52},{56,60},{64,6... | collective-permute-start | bytes 589832 | tf_op jit(solution)/shard_map/ppermute | solution.py:438
  9.1 0.6 copy-done.8
  10.0 0.7 copy-done.5
  10.7 0.9 copy-done.2
  11.6 1.6 %shard_map.110 = (bf16[4,128,256]{2,1,0:T(8,128)(2,1)S(1)}, bf16[4,128,256]{2,1,0:T(8,128)(2,1)S(1)}, bf16[4,128,256]{2,1,0:T(8,128)(2,1)S(1)}, f32[4,128,256]{2...) custom-call(s32[5]{0:T(128)S(1)} %stack.23.place, ...), custom_call_target="tpu_custom_call" | custom-call | flops 3000000000 | bytes 1000000 | tf_op jit(solution)/shard_map/pallas_call | solution.py:383
  13.8 4.7 %collective-permute-start.2 = (bf16[10,8,256]{2,1,0:T(8,128)(2,1)S(1)}, bf16[10,8,256]{2,1,0:T(8,128)(2,1)S(1)}, u32[]{:S(2)}, u32[]{:S(2)}) collective-permute-start(bf16[10,8,256]{2,1,0:T(8,128)(2,1)S(1)} %get-tuple-element.51), channel_id=1, source_target_pairs={{1,2},{2,1},{5,6},{6,5},{9,10},{10,9},{13,14},{14,13},{17,18},{18,... | collective-permute-start | bytes 122888 | tf_op jit(solution)/shard_map/ppermute | solution.py:439
  18.5 1.9 %collective-permute-start.3 = (bf16[10,8,256]{2,1,0:T(8,128)(2,1)S(1)}, bf16[10,8,256]{2,1,0:T(8,128)(2,1)S(1)}, u32[]{:S(2)}, u32[]{:S(2)}) collective-permute-start(bf16[10,8,256]{2,1,0:T(8,128)(2,1)S(1)} %get-tuple-element.52), channel_id=1, source_target_pairs={{0,1},{2,3},{1,0},{3,2},{4,5},{6,7},{5,4},{7,6},{8,9},{10,11},{9,8... | collective-permute-start | bytes 122888 | tf_op jit(solution)/shard_map/ppermute | solution.py:438
  21.6 7.3 %shard_map.113 = (f32[33,32,128]{2,1,0:T(8,128)S(1)}, bf16[33,32,128]{2,1,0:T(8,128)(2,1)S(1)}, bf16[4,128,256]{2,1,0:T(8,128)(2,1)S(1)}, bf16[4,128,256]{2,1,0:...) custom-call(s32[5]{0:T(128)S(1)} %stack.23.place, ...), custom_call_target="tpu_custom_call" | custom-call | flops 8999999488 | bytes 1000000 | tf_op jit(solution)/shard_map/pallas_call | solution.py:383
  28.9 2.2 %collective-permute-start.4 = (bf16[33,32,128]{2,1,0:T(8,128)(2,1)S(1)}, bf16[33,32,128]{2,1,0:T(8,128)(2,1)S(1)}, u32[]{:S(2)}, u32[]{:S(2)}) collective-permute-start(bf16[33,32,128]{2,1,0:T(8,128)(2,1)S(1)} %get-tuple-element.71), channel_id=1, source_target_pairs={{0,1},{1,0},{2,3},{3,2},{4,5},{5,4},{6,7},{7,6},{8,9},{9,8},{10,11... | collective-permute-start | bytes 811016 | tf_op jit(solution)/shard_map/ppermute | solution.py:462
  31.1 1.3 %collective-permute-done.4.received = bf16[33,32,128]{2,1,0:T(8,128)(2,1)S(1)} collective-permute-done((bf16[33,32,128]{2,1,0:T(8,128)(2,1)S(1)}, bf16[33,32,128]{2,1,0:T(8,128)(2,1)S(1)}, u32[]{:S(2)}, u32[]{:S(2)}) %collective-permute-start.4) | collective-permute-done | bytes 270368 | tf_op jit(solution)/shard_map/ppermute | solution.py:462
  32.3 0.8 shard_map.114
  33.1 15.5 %all-to-all-start = ((bf16[32,40,128]{2,1,0:T(8,128)(2,1)}), bf16[32,40,128]{2,1,0:T(8,128)(2,1)S(1)}, u32[]{:S(2)}, u32[]{:S(2)}) async-start(bf16[32,40,128]{2,1,0:T(8,128)(2,1)} %shard_map.114), calls=%async_computation | async-start | bytes 655360 | tf_op jit(solution)/shard_map/all_to_all | solution.py:466
  48.6 0.7 collective-permute-start.5
  49.3 4.1 %collective-permute-start.6 = (bf16[3,144,256]{2,1,0:T(8,128)(2,1)S(1)}, bf16[3,144,256]{2,1,0:T(8,128)(2,1)S(1)}, u32[]{:S(2)}, u32[]{:S(2)}) collective-permute-start(bf16[3,144,256]{2,1,0:T(8,128)(2,1)S(1)} %get-tuple-element.81), channel_id=1, source_target_pairs={{0,4},{8,12},{16,20},{24,28},{32,36},{40,44},{48,52},{56,60},{64,6... | collective-permute-start | bytes 663560 | tf_op jit(solution)/shard_map/ppermute | solution.py:438
  53.3 8.7 %all-to-all-done.parts = bf16[32,40,128]{2,1,0:T(8,128)(2,1)S(1)} async-done(((bf16[32,40,128]{2,1,0:T(8,128)(2,1)}), bf16[32,40,128]{2,1,0:T(8,128)(2,1)S(1)}, u32[]{:S(2)}, u32[]{:S(2)}) %all-to-all-start) | async-done | bytes 327712 | tf_op jit(solution)/shard_map/all_to_all | solution.py:466
  62.0 0.7 shard_map.115
  62.7 3.4 %all-to-all-start.1 = ((bf16[8,40,128]{2,1,0:T(8,128)(2,1)}), bf16[8,40,128]{2,1,0:T(8,128)(2,1)S(1)}, u32[]{:S(2)}, u32[]{:S(2)}) async-start(bf16[8,40,128]{2,1,0:T(8,128)(2,1)} %shard_map.115), calls=%async_computation.1 | async-start | bytes 163840 | tf_op jit(solution)/shard_map/all_to_all | solution.py:470
  66.1 0.9 copy-done.7
  67.1 1.8 %shard_map.116 = (bf16[4,128,256]{2,1,0:T(8,128)(2,1)}, f32[4,128,256]{2,1,0:T(8,128)S(1)}, bf16[4,8,256]{2,1,0:T(8,128)(2,1)S(1)}, bf16[4,8,256]{2,1,0:T(8,128)(2,1)S(1)}) custom-call(s32[5]{0:T(128)S(1)} %stack.23.place, bf16[4,128,256]{2,1,0:T(8,128)(2,1)S(1)} %copy-done, bf16[256,768]{1,0:T(8,128)(2,1)S(1)} %copy-done.1, bf16[256,256]{1,0:T(8,128)(2,1)S(1)} %copy-done.4, ...), custom_call_target="tpu_custom_call" | custom-call | flops 3000000000 | bytes 1000000 | tf_op jit(solution)/shard_map/pallas_call | solution.py:383
  68.9 4.6 %all-to-all-done.1.parts = bf16[8,40,128]{2,1,0:T(8,128)(2,1)S(1)} async-done(((bf16[8,40,128]{2,1,0:T(8,128)(2,1)}), bf16[8,40,128]{2,1,0:T(8,128)(2,1)S(1)}, u32[]{:S(2)}, u32[]{:S(2)}) %all-to-all-start.1) | async-done | bytes 81952 | tf_op jit(solution)/shard_map/all_to_all | solution.py:470
  73.4 0.7 shard_map.117
  74.2 10.0 %all-to-all-start.2 = ((bf16[32,32,128]{2,1,0:T(8,128)(2,1)}), bf16[32,32,128]{2,1,0:T(8,128)(2,1)S(1)}, u32[]{:S(2)}, u32[]{:S(2)}) async-start(bf16[32,32,128]{2,1,0:T(8,128)(2,1)} %get-tuple-element.87), calls=%async_computation.2 | async-start | bytes 524288 | tf_op jit(solution)/shard_map/all_to_all | solution.py:476
  84.1 5.7 %collective-permute-start.7 = (bf16[4,8,256]{2,1,0:T(8,128)(2,1)S(1)}, bf16[4,8,256]{2,1,0:T(8,128)(2,1)S(1)}, u32[]{:S(2)}, u32[]{:S(2)}) collective-permute-start(bf16[4,8,256]{2,1,0:T(8,128)(2,1)S(1)} %get-tuple-element.89), channel_id=1, source_target_pairs={{1,2},{2,1},{5,6},{6,5},{9,10},{10,9},{13,14},{14,13},{17,18},{18,... | collective-permute-start | bytes 49160 | tf_op jit(solution)/shard_map/ppermute | solution.py:439
  89.8 1.9 %collective-permute-start.8 = (bf16[4,8,256]{2,1,0:T(8,128)(2,1)S(1)}, bf16[4,8,256]{2,1,0:T(8,128)(2,1)S(1)}, u32[]{:S(2)}, u32[]{:S(2)}) collective-permute-start(bf16[4,8,256]{2,1,0:T(8,128)(2,1)S(1)} %get-tuple-element.90), channel_id=1, source_target_pairs={{0,1},{2,3},{1,0},{3,2},{4,5},{6,7},{5,4},{7,6},{8,9},{10,11},{9,8... | collective-permute-start | bytes 49160 | tf_op jit(solution)/shard_map/ppermute | solution.py:438
  91.7 1.1 %collective-permute-done.8.from_b = bf16[4,8,256]{2,1,0:T(8,128)(2,1)S(1)} collective-permute-done((bf16[4,8,256]{2,1,0:T(8,128)(2,1)S(1)}, bf16[4,8,256]{2,1,0:T(8,128)(2,1)S(1)}, u32[]{:S(2)}, u32[]{:S(2)}) %collective-permute-start.8) | collective-permute-done | bytes 16416 | tf_op jit(solution)/shard_map/ppermute | solution.py:438
  92.9 1.6 %shard_map.118 = f32[4,128,256]{2,1,0:T(8,128)} custom-call(s32[5]{0:T(128)S(1)} %stack.23.place, bf16[4,128,256]{2,1,0:T(8,128)(2,1)S(1)} %copy-done, bf16[4,128,256]{2,1,0:T(8,128)(2,1)S(1)} %copy-done.3, f32[1,256]{1,0:T(1,128)S(1)} %bitcast.14, f32[4,128,256]{2,1,0:T(8,128)S(1)} %get-tuple-element.88.grad_normed, ...), custom_call_target="tpu_custom_call" | custom-call | flops 2000000000 | bytes 1000000 | tf_op jit(solution)/shard_map/pallas_call | solution.py:383
  94.6 5.6 %collective-permute-start.9 = (bf16[32,32,128]{2,1,0:T(8,128)(2,1)S(1)}, bf16[32,32,128]{2,1,0:T(8,128)(2,1)S(1)}, u32[]{:S(2)}, u32[]{:S(2)}) collective-permute-start(bf16[32,32,128]{2,1,0:T(8,128)(2,1)S(1)} %all-to-all-done.2.mine), channel_id=1, source_target_pairs={{0,1},{1,0},{2,3},{3,2},{4,5},{5,4},{6,7},{7,6},{8,9},{9,8},{10,11... | collective-permute-start | bytes 786440 | tf_op jit(solution)/shard_map/ppermute | solution.py:482
  100.1 0.6 fusion
  100.8 0.6 copy.13
  101.4 1.6 %shard_map.119 = (f32[256,768]{1,0:T(8,128)}, f32[256,256]{1,0:T(8,128)}) custom-call(s32[5]{0:T(128)S(1)} %stack.23.place, bf16[32,32,128]{2,1,0:T(8,128)(2,1)S(1)} %all-to-all-done.2.mine, bf16[32,32,128]{2,1,0:T(8,128)(2,1)S(1)} %collective-permute-done.9.other), custom_call_target="tpu_custom_call" | custom-call | flops 1000000000 | bytes 1000000 | tf_op jit(solution)/shard_map/pallas_call | solution.py:383
  (31 shorter events, 2.2 us)
Async XLA Ops:
  0.7 9.3 %copy-start = (bf16[4,128,256]{2,1,0:T(8,128)(2,1)S(1)}, bf16[4,128,256]{2,1,0:T(8,128)(2,1)}, u32[]{:S(2)}) copy-start(bf16[4,128,256]{2,1,0:T(8,128)(2,1)} %own.7) | copy-start | bytes 786436
  0.7 9.3 %copy-start.1 = (bf16[256,768]{1,0:T(8,128)(2,1)S(1)}, bf16[256,768]{1,0:T(8,128)(2,1)}, u32[]{:S(2)}) copy-start(bf16[256,768]{1,0:T(8,128)(2,1)} %wqkv.9) | copy-start | bytes 1179652
  0.7 9.3 %copy-start.4 = (bf16[256,256]{1,0:T(8,128)(2,1)S(1)}, bf16[256,256]{1,0:T(8,128)(2,1)}, u32[]{:S(2)}) copy-start(bf16[256,256]{1,0:T(8,128)(2,1)} %wo.3) | copy-start | bytes 393220
  1.8 11.4 %collective-permute-start.1 = (bf16[3,128,256]{2,1,0:T(8,128)(2,1)S(1)}, bf16[3,128,256]{2,1,0:T(8,128)(2,1)S(1)}, u32[]{:S(2)}, u32[]{:S(2)}) collective-permute-start(bf16[3,128,256]{2,1,0:T(8,128)(2,1)S(1)} %get-tuple-element.96), channel_id=1, source_target_pairs={{4,8},{12,16},{20,24},{28,32},{36,40},{44,48},{52,56},{60,64},{68,... | collective-permute-start | bytes 589832 | tf_op jit(solution)/shard_map/ppermute | solution.py:439
  2.5 10.7 %collective-permute-start = (bf16[3,128,256]{2,1,0:T(8,128)(2,1)S(1)}, bf16[3,128,256]{2,1,0:T(8,128)(2,1)S(1)}, u32[]{:S(2)}, u32[]{:S(2)}) collective-permute-start(bf16[3,128,256]{2,1,0:T(8,128)(2,1)S(1)} %get-tuple-element.97), channel_id=1, source_target_pairs={{0,4},{8,12},{16,20},{24,28},{32,36},{40,44},{48,52},{56,60},{64,6... | collective-permute-start | bytes 589832 | tf_op jit(solution)/shard_map/ppermute | solution.py:438
  9.1 0.7 copy-start.8
  10.0 0.7 copy-start.5
  10.7 0.9 copy-start.2
  13.8 7.5 %collective-permute-start.2 = (bf16[10,8,256]{2,1,0:T(8,128)(2,1)S(1)}, bf16[10,8,256]{2,1,0:T(8,128)(2,1)S(1)}, u32[]{:S(2)}, u32[]{:S(2)}) collective-permute-start(bf16[10,8,256]{2,1,0:T(8,128)(2,1)S(1)} %get-tuple-element.51), channel_id=1, source_target_pairs={{1,2},{2,1},{5,6},{6,5},{9,10},{10,9},{13,14},{14,13},{17,18},{18,... | collective-permute-start | bytes 122888 | tf_op jit(solution)/shard_map/ppermute | solution.py:439
  18.5 3.1 %collective-permute-start.3 = (bf16[10,8,256]{2,1,0:T(8,128)(2,1)S(1)}, bf16[10,8,256]{2,1,0:T(8,128)(2,1)S(1)}, u32[]{:S(2)}, u32[]{:S(2)}) collective-permute-start(bf16[10,8,256]{2,1,0:T(8,128)(2,1)S(1)} %get-tuple-element.52), channel_id=1, source_target_pairs={{0,1},{2,3},{1,0},{3,2},{4,5},{6,7},{5,4},{7,6},{8,9},{10,11},{9,8... | collective-permute-start | bytes 122888 | tf_op jit(solution)/shard_map/ppermute | solution.py:438
  28.9 4.2 %copy-start.6 = (bf16[4,128,256]{2,1,0:T(8,128)(2,1)}, bf16[4,128,256]{2,1,0:T(8,128)(2,1)S(1)}, u32[]{:S(2)}) copy-start(bf16[4,128,256]{2,1,0:T(8,128)(2,1)S(1)} %get-tuple-element.78.g_q) | copy-start | bytes 786436
  28.9 3.4 %collective-permute-start.4 = (bf16[33,32,128]{2,1,0:T(8,128)(2,1)S(1)}, bf16[33,32,128]{2,1,0:T(8,128)(2,1)S(1)}, u32[]{:S(2)}, u32[]{:S(2)}) collective-permute-start(bf16[33,32,128]{2,1,0:T(8,128)(2,1)S(1)} %get-tuple-element.71), channel_id=1, source_target_pairs={{0,1},{1,0},{2,3},{3,2},{4,5},{5,4},{6,7},{7,6},{8,9},{9,8},{10,11... | collective-permute-start | bytes 811016 | tf_op jit(solution)/shard_map/ppermute | solution.py:462
  33.1 28.9 %all-to-all-start = ((bf16[32,40,128]{2,1,0:T(8,128)(2,1)}), bf16[32,40,128]{2,1,0:T(8,128)(2,1)S(1)}, u32[]{:S(2)}, u32[]{:S(2)}) async-start(bf16[32,40,128]{2,1,0:T(8,128)(2,1)} %shard_map.114), calls=%async_computation | async-start | bytes 655360 | tf_op jit(solution)/shard_map/all_to_all | solution.py:466
  48.6 17.5 %collective-permute-start.5 = (bf16[3,144,256]{2,1,0:T(8,128)(2,1)S(1)}, bf16[3,144,256]{2,1,0:T(8,128)(2,1)S(1)}, u32[]{:S(2)}, u32[]{:S(2)}) collective-permute-start(bf16[3,144,256]{2,1,0:T(8,128)(2,1)S(1)} %get-tuple-element.80), channel_id=1, source_target_pairs={{4,8},{12,16},{20,24},{28,32},{36,40},{44,48},{52,56},{60,64},{68,... | collective-permute-start | bytes 663560 | tf_op jit(solution)/shard_map/ppermute | solution.py:439
  49.3 16.8 %collective-permute-start.6 = (bf16[3,144,256]{2,1,0:T(8,128)(2,1)S(1)}, bf16[3,144,256]{2,1,0:T(8,128)(2,1)S(1)}, u32[]{:S(2)}, u32[]{:S(2)}) collective-permute-start(bf16[3,144,256]{2,1,0:T(8,128)(2,1)S(1)} %get-tuple-element.81), channel_id=1, source_target_pairs={{0,4},{8,12},{16,20},{24,28},{32,36},{40,44},{48,52},{56,60},{64,6... | collective-permute-start | bytes 663560 | tf_op jit(solution)/shard_map/ppermute | solution.py:438
  62.7 10.7 %all-to-all-start.1 = ((bf16[8,40,128]{2,1,0:T(8,128)(2,1)}), bf16[8,40,128]{2,1,0:T(8,128)(2,1)S(1)}, u32[]{:S(2)}, u32[]{:S(2)}) async-start(bf16[8,40,128]{2,1,0:T(8,128)(2,1)} %shard_map.115), calls=%async_computation.1 | async-start | bytes 163840 | tf_op jit(solution)/shard_map/all_to_all | solution.py:470
  66.1 1.0 copy-start.7
  74.1 18.7 %copy-start.3 = (bf16[4,128,256]{2,1,0:T(8,128)(2,1)S(1)}, bf16[4,128,256]{2,1,0:T(8,128)(2,1)}, u32[]{:S(2)}) copy-start(bf16[4,128,256]{2,1,0:T(8,128)(2,1)} %cot.5) | copy-start | bytes 786436
  74.2 20.4 %all-to-all-start.2 = ((bf16[32,32,128]{2,1,0:T(8,128)(2,1)}), bf16[32,32,128]{2,1,0:T(8,128)(2,1)S(1)}, u32[]{:S(2)}, u32[]{:S(2)}) async-start(bf16[32,32,128]{2,1,0:T(8,128)(2,1)} %get-tuple-element.87), calls=%async_computation.2 | async-start | bytes 524288 | tf_op jit(solution)/shard_map/all_to_all | solution.py:476
  84.1 7.6 %collective-permute-start.7 = (bf16[4,8,256]{2,1,0:T(8,128)(2,1)S(1)}, bf16[4,8,256]{2,1,0:T(8,128)(2,1)S(1)}, u32[]{:S(2)}, u32[]{:S(2)}) collective-permute-start(bf16[4,8,256]{2,1,0:T(8,128)(2,1)S(1)} %get-tuple-element.89), channel_id=1, source_target_pairs={{1,2},{2,1},{5,6},{6,5},{9,10},{10,9},{13,14},{14,13},{17,18},{18,... | collective-permute-start | bytes 49160 | tf_op jit(solution)/shard_map/ppermute | solution.py:439
  89.8 3.1 %collective-permute-start.8 = (bf16[4,8,256]{2,1,0:T(8,128)(2,1)S(1)}, bf16[4,8,256]{2,1,0:T(8,128)(2,1)S(1)}, u32[]{:S(2)}, u32[]{:S(2)}) collective-permute-start(bf16[4,8,256]{2,1,0:T(8,128)(2,1)S(1)} %get-tuple-element.90), channel_id=1, source_target_pairs={{0,1},{2,3},{1,0},{3,2},{4,5},{6,7},{5,4},{7,6},{8,9},{10,11},{9,8... | collective-permute-start | bytes 49160 | tf_op jit(solution)/shard_map/ppermute | solution.py:438
  94.6 6.8 %collective-permute-start.9 = (bf16[32,32,128]{2,1,0:T(8,128)(2,1)S(1)}, bf16[32,32,128]{2,1,0:T(8,128)(2,1)S(1)}, u32[]{:S(2)}, u32[]{:S(2)}) collective-permute-start(bf16[32,32,128]{2,1,0:T(8,128)(2,1)S(1)} %all-to-all-done.2.mine), channel_id=1, source_target_pairs={{0,1},{1,0},{2,3},{3,2},{4,5},{5,4},{6,7},{7,6},{8,9},{9,8},{10,11... | collective-permute-start | bytes 786440 | tf_op jit(solution)/shard_map/ppermute | solution.py:482

commit v7 on v6

--- a/solution.py
+++ b/solution.py
@@ -32,8 +32,8 @@
 AXIS_SIZES = (8, 2, 8, 2, 2)
 ROWS = ("z", "xh", "y")
 GRP = ("xl", "core")
-SPLIT = ("z", "xh", "xl")
-REST = ("y",)
+SPLIT = ("xh", "y", "xl")
+REST = ("z",)
 PARTS = 32
 RESTS = 8
 HALF = 2 * C
@@ -73,7 +73,8 @@
 
 
 def normalise(raw, ones):
-    inv = lax.rsqrt(per_head_mean(raw * raw, ones) + EPS)
+    high, low = split_bf16(raw * raw)
+    inv = lax.rsqrt(mm(high, ones) + mm(low, ones) + EPS)
     return raw * inv, inv
 
 

time: 104 us -> 100 us (0.962)
  starting transfers between devices: 62.7 us -> 60.3 us
  waiting for transfers between devices: 16 us -> 14.7 us
    all_to_all x1, starting transfers between devices: 15.5 us -> 8.52 us  [body(): parts = lax.all_to_all(parts, SPLIT, 0, 0)]
    all_to_all x1, starting transfers between devices: 3.36 us -> 10.1 us  [body(): parts = lax.all_to_all(copies, REST, 0, 0)]
    all_to_all x1, starting transfers between devices: 9.99 us -> 4 us  [body(): mine = lax.all_to_all(copies, SPLIT, 0, 0)]
    ppermute x4, starting transfers between devices: 14.5 us -> 16 us  [swap(): b = lax.ppermute(b, axes, pairs[1])]
    ppermute x4, starting transfers between devices: 11.7 us -> 12.9 us  [swap(): return (lax.ppermute(a, axes, pairs[0]), b)]
    all_to_all x1, waiting for transfers between devices: 8.7 us -> 7.61 us  [body(): parts = lax.all_to_all(parts, SPLIT, 0, 0)]
  transfers between devices with their start and end apart: 13 -> 13, of which waited for: 6 -> 5; matrix products, arithmetic and copies ran while one was open for 1% -> 1% of each run, Pallas kernels for 6% -> 7%
where the time goes in v7:
time: 100 us; the launch traced here: 99.6 us
  starting transfers between devices  60.3 us (60%)
  Pallas kernels  17.8 us (18%)
  waiting for transfers between devices  14.7 us (15%)
  local copies, waits for them, and re-layouts  5.84 us (6%)
    pallas_call x11, Pallas kernels, call(): pl.pallas_call(fn, out_shape=tuple((jax.ShapeDtypeStruct(s, d) for s, d i...  17.8 us
    ppermute x4, starting transfers between devices, swap(): b = lax.ppermute(b, axes, pairs[1])  16 us
    ppermute x4, starting transfers between devices, swap(): return (lax.ppermute(a, axes, pairs[0]), b)  12.9 us
    all_to_all x1, starting transfers between devices, body(): parts = lax.all_to_all(copies, REST, 0, 0)  10.1 us
    all_to_all x1, starting transfers between devices, body(): parts = lax.all_to_all(parts, SPLIT, 0, 0)  8.52 us
    all_to_all x1, waiting for transfers between devices, body(): parts = lax.all_to_all(parts, SPLIT, 0, 0)  7.61 us
    ppermute x1, starting transfers between devices, body(): other = lax.ppermute(mine, 'core', cores)  6.42 us
    all_to_all x1, waiting for transfers between devices, body(): parts = lax.all_to_all(copies, REST, 0, 0)  4.75 us
  transfers between devices with their start and end apart: 13, of which 5 were waited for; matrix products, arithmetic and copies ran while one was open for 1% of the time, Pallas kernels for 7%

profile of v7, /device:TPU:1, one launch (start us, length us, event | category | flops | bytes accessed | tf_op | source)
XLA Modules:
  0.0 99.6 jit_solution(11569460993697498851)
XLA Ops:
  0.7 1.1 %constant_dynamic-slice_fusion = (bf16[3,128,256]{2,1,0:T(8,128)(2,1)S(1)}, bf16[3,128,256]{2,1,0:T(8,128)(2,1)S(1)}) fusion(bf16[4,128,256]{2,1,0:T(8,128)(2,1)} %own.7, s32[]{:T(128)S(6)} %select_n.20, s32[]{:T(128)S(6)} %select_n.19), kind=kLoop, calls=%fused_computation.1 | loop fusion | bytes 786440 | tf_op jit(solution)/shard_map/dynamic_slice | solution.py:452
  1.8 0.7 collective-permute-start.1
  2.5 6.6 %collective-permute-start = (bf16[3,128,256]{2,1,0:T(8,128)(2,1)S(1)}, bf16[3,128,256]{2,1,0:T(8,128)(2,1)S(1)}, u32[]{:S(2)}, u32[]{:S(2)}) collective-permute-start(bf16[3,128,256]{2,1,0:T(8,128)(2,1)S(1)} %get-tuple-element.97), channel_id=1, source_target_pairs={{0,4},{8,12},{16,20},{24,28},{32,36},{40,44},{48,52},{56,60},{64,6... | collective-permute-start | bytes 589832 | tf_op jit(solution)/shard_map/ppermute | solution.py:439
  9.1 0.6 copy-done.8
  10.0 0.7 copy-done.5
  10.7 0.9 copy-done.2
  11.6 1.7 %shard_map.110 = (bf16[4,128,256]{2,1,0:T(8,128)(2,1)S(1)}, bf16[4,128,256]{2,1,0:T(8,128)(2,1)S(1)}, bf16[4,128,256]{2,1,0:T(8,128)(2,1)S(1)}, f32[4,128,256]{2...) custom-call(s32[5]{0:T(128)S(1)} %stack.23.place, ...), custom_call_target="tpu_custom_call" | custom-call | flops 3000000000 | bytes 1000000 | tf_op jit(solution)/shard_map/pallas_call | solution.py:384
  13.9 4.5 %collective-permute-start.2 = (bf16[10,8,256]{2,1,0:T(8,128)(2,1)S(1)}, bf16[10,8,256]{2,1,0:T(8,128)(2,1)S(1)}, u32[]{:S(2)}, u32[]{:S(2)}) collective-permute-start(bf16[10,8,256]{2,1,0:T(8,128)(2,1)S(1)} %get-tuple-element.51), channel_id=1, source_target_pairs={{1,2},{2,1},{5,6},{6,5},{9,10},{10,9},{13,14},{14,13},{17,18},{18,... | collective-permute-start | bytes 122888 | tf_op jit(solution)/shard_map/ppermute | solution.py:440
  18.5 1.9 %collective-permute-start.3 = (bf16[10,8,256]{2,1,0:T(8,128)(2,1)S(1)}, bf16[10,8,256]{2,1,0:T(8,128)(2,1)S(1)}, u32[]{:S(2)}, u32[]{:S(2)}) collective-permute-start(bf16[10,8,256]{2,1,0:T(8,128)(2,1)S(1)} %get-tuple-element.52), channel_id=1, source_target_pairs={{0,1},{2,3},{1,0},{3,2},{4,5},{6,7},{5,4},{7,6},{8,9},{10,11},{9,8... | collective-permute-start | bytes 122888 | tf_op jit(solution)/shard_map/ppermute | solution.py:439
  21.6 7.3 %shard_map.113 = (f32[33,32,128]{2,1,0:T(8,128)S(1)}, bf16[33,32,128]{2,1,0:T(8,128)(2,1)S(1)}, bf16[4,128,256]{2,1,0:T(8,128)(2,1)S(1)}, bf16[4,128,256]{2,1,0:...) custom-call(s32[5]{0:T(128)S(1)} %stack.23.place, ...), custom_call_target="tpu_custom_call" | custom-call | flops 8999999488 | bytes 1000000 | tf_op jit(solution)/shard_map/pallas_call | solution.py:384
  28.9 2.4 %collective-permute-start.4 = (bf16[33,32,128]{2,1,0:T(8,128)(2,1)S(1)}, bf16[33,32,128]{2,1,0:T(8,128)(2,1)S(1)}, u32[]{:S(2)}, u32[]{:S(2)}) collective-permute-start(bf16[33,32,128]{2,1,0:T(8,128)(2,1)S(1)} %get-tuple-element.71), channel_id=1, source_target_pairs={{0,1},{1,0},{2,3},{3,2},{4,5},{5,4},{6,7},{7,6},{8,9},{9,8},{10,11... | collective-permute-start | bytes 811016 | tf_op jit(solution)/shard_map/ppermute | solution.py:463
  31.3 1.2 %collective-permute-done.4.received = bf16[33,32,128]{2,1,0:T(8,128)(2,1)S(1)} collective-permute-done((bf16[33,32,128]{2,1,0:T(8,128)(2,1)S(1)}, bf16[33,32,128]{2,1,0:T(8,128)(2,1)S(1)}, u32[]{:S(2)}, u32[]{:S(2)}) %collective-permute-start.4) | collective-permute-done | bytes 270368 | tf_op jit(solution)/shard_map/ppermute | solution.py:463
  32.4 0.8 shard_map.114
  33.2 8.5 %all-to-all-start = ((bf16[32,40,128]{2,1,0:T(8,128)(2,1)}), bf16[32,40,128]{2,1,0:T(8,128)(2,1)S(1)}, u32[]{:S(2)}, u32[]{:S(2)}) async-start(bf16[32,40,128]{2,1,0:T(8,128)(2,1)} %shard_map.114), calls=%async_computation | async-start | bytes 655360 | tf_op jit(solution)/shard_map/all_to_all | solution.py:467
  41.7 0.7 collective-permute-start.5
  42.4 5.6 %collective-permute-start.6 = (bf16[3,144,256]{2,1,0:T(8,128)(2,1)S(1)}, bf16[3,144,256]{2,1,0:T(8,128)(2,1)S(1)}, u32[]{:S(2)}, u32[]{:S(2)}) collective-permute-start(bf16[3,144,256]{2,1,0:T(8,128)(2,1)S(1)} %get-tuple-element.81), channel_id=1, source_target_pairs={{0,4},{8,12},{16,20},{24,28},{32,36},{40,44},{48,52},{56,60},{64,6... | collective-permute-start | bytes 663560 | tf_op jit(solution)/shard_map/ppermute | solution.py:439
  48.0 7.6 %all-to-all-done.parts = bf16[32,40,128]{2,1,0:T(8,128)(2,1)S(1)} async-done(((bf16[32,40,128]{2,1,0:T(8,128)(2,1)}), bf16[32,40,128]{2,1,0:T(8,128)(2,1)S(1)}, u32[]{:S(2)}, u32[]{:S(2)}) %all-to-all-start) | async-done | bytes 327712 | tf_op jit(solution)/shard_map/all_to_all | solution.py:467
  55.6 0.7 shard_map.115
  56.3 10.1 %all-to-all-start.1 = ((bf16[8,40,128]{2,1,0:T(8,128)(2,1)}), bf16[8,40,128]{2,1,0:T(8,128)(2,1)S(1)}, u32[]{:S(2)}, u32[]{:S(2)}) async-start(bf16[8,40,128]{2,1,0:T(8,128)(2,1)} %shard_map.115), calls=%async_computation.1 | async-start | bytes 163840 | tf_op jit(solution)/shard_map/all_to_all | solution.py:471
  66.4 0.9 copy-done.7
  67.3 1.8 %shard_map.116 = (bf16[4,128,256]{2,1,0:T(8,128)(2,1)}, f32[4,128,256]{2,1,0:T(8,128)S(1)}, bf16[4,8,256]{2,1,0:T(8,128)(2,1)S(1)}, bf16[4,8,256]{2,1,0:T(8,128)(2,1)S(1)}) custom-call(s32[5]{0:T(128)S(1)} %stack.23.place, bf16[4,128,256]{2,1,0:T(8,128)(2,1)S(1)} %copy-done, bf16[256,768]{1,0:T(8,128)(2,1)S(1)} %copy-done.1, bf16[256,256]{1,0:T(8,128)(2,1)S(1)} %copy-done.4, ...), custom_call_target="tpu_custom_call" | custom-call | flops 3000000000 | bytes 1000000 | tf_op jit(solution)/shard_map/pallas_call | solution.py:384
  69.1 4.7 %all-to-all-done.1.parts = bf16[8,40,128]{2,1,0:T(8,128)(2,1)S(1)} async-done(((bf16[8,40,128]{2,1,0:T(8,128)(2,1)}), bf16[8,40,128]{2,1,0:T(8,128)(2,1)S(1)}, u32[]{:S(2)}, u32[]{:S(2)}) %all-to-all-start.1) | async-done | bytes 81952 | tf_op jit(solution)/shard_map/all_to_all | solution.py:471
  73.9 0.7 shard_map.117
  74.6 4.0 %all-to-all-start.2 = ((bf16[32,32,128]{2,1,0:T(8,128)(2,1)}), bf16[32,32,128]{2,1,0:T(8,128)(2,1)S(1)}, u32[]{:S(2)}, u32[]{:S(2)}) async-start(bf16[32,32,128]{2,1,0:T(8,128)(2,1)} %get-tuple-element.87), calls=%async_computation.2 | async-start | bytes 524288 | tf_op jit(solution)/shard_map/all_to_all | solution.py:477
  78.6 7.0 %collective-permute-start.7 = (bf16[4,8,256]{2,1,0:T(8,128)(2,1)S(1)}, bf16[4,8,256]{2,1,0:T(8,128)(2,1)S(1)}, u32[]{:S(2)}, u32[]{:S(2)}) collective-permute-start(bf16[4,8,256]{2,1,0:T(8,128)(2,1)S(1)} %get-tuple-element.89), channel_id=1, source_target_pairs={{1,2},{2,1},{5,6},{6,5},{9,10},{10,9},{13,14},{14,13},{17,18},{18,... | collective-permute-start | bytes 49160 | tf_op jit(solution)/shard_map/ppermute | solution.py:440
  85.7 1.9 %collective-permute-start.8 = (bf16[4,8,256]{2,1,0:T(8,128)(2,1)S(1)}, bf16[4,8,256]{2,1,0:T(8,128)(2,1)S(1)}, u32[]{:S(2)}, u32[]{:S(2)}) collective-permute-start(bf16[4,8,256]{2,1,0:T(8,128)(2,1)S(1)} %get-tuple-element.90), channel_id=1, source_target_pairs={{0,1},{2,3},{1,0},{3,2},{4,5},{6,7},{5,4},{7,6},{8,9},{10,11},{9,8... | collective-permute-start | bytes 49160 | tf_op jit(solution)/shard_map/ppermute | solution.py:439
  87.6 1.1 %collective-permute-done.8.from_b = bf16[4,8,256]{2,1,0:T(8,128)(2,1)S(1)} collective-permute-done((bf16[4,8,256]{2,1,0:T(8,128)(2,1)S(1)}, bf16[4,8,256]{2,1,0:T(8,128)(2,1)S(1)}, u32[]{:S(2)}, u32[]{:S(2)}) %collective-permute-start.8) | collective-permute-done | bytes 16416 | tf_op jit(solution)/shard_map/ppermute | solution.py:439
  88.7 1.6 %shard_map.118 = f32[4,128,256]{2,1,0:T(8,128)} custom-call(s32[5]{0:T(128)S(1)} %stack.23.place, bf16[4,128,256]{2,1,0:T(8,128)(2,1)S(1)} %copy-done, bf16[4,128,256]{2,1,0:T(8,128)(2,1)S(1)} %copy-done.3, f32[1,256]{1,0:T(1,128)S(1)} %bitcast.14, f32[4,128,256]{2,1,0:T(8,128)S(1)} %get-tuple-element.88.grad_normed, ...), custom_call_target="tpu_custom_call" | custom-call | flops 2000000000 | bytes 1000000 | tf_op jit(solution)/shard_map/pallas_call | solution.py:384
  90.3 6.4 %collective-permute-start.9 = (bf16[32,32,128]{2,1,0:T(8,128)(2,1)S(1)}, bf16[32,32,128]{2,1,0:T(8,128)(2,1)S(1)}, u32[]{:S(2)}, u32[]{:S(2)}) collective-permute-start(bf16[32,32,128]{2,1,0:T(8,128)(2,1)S(1)} %all-to-all-done.2.mine), channel_id=1, source_target_pairs={{0,1},{1,0},{2,3},{3,2},{4,5},{5,4},{6,7},{7,6},{8,9},{9,8},{10,11... | collective-permute-start | bytes 786440 | tf_op jit(solution)/shard_map/ppermute | solution.py:483
  96.8 0.6 fusion
  97.4 0.6 copy.13
  98.0 1.6 %shard_map.119 = (f32[256,768]{1,0:T(8,128)}, f32[256,256]{1,0:T(8,128)}) custom-call(s32[5]{0:T(128)S(1)} %stack.23.place, bf16[32,32,128]{2,1,0:T(8,128)(2,1)S(1)} %all-to-all-done.2.mine, bf16[32,32,128]{2,1,0:T(8,128)(2,1)S(1)} %collective-permute-done.9.other), custom_call_target="tpu_custom_call" | custom-call | flops 1000000000 | bytes 1000000 | tf_op jit(solution)/shard_map/pallas_call | solution.py:384
  (31 shorter events, 2.1 us)
Async XLA Ops:
  0.7 9.3 %copy-start = (bf16[4,128,256]{2,1,0:T(8,128)(2,1)S(1)}, bf16[4,128,256]{2,1,0:T(8,128)(2,1)}, u32[]{:S(2)}) copy-start(bf16[4,128,256]{2,1,0:T(8,128)(2,1)} %own.7) | copy-start | bytes 786436
  0.7 9.3 %copy-start.1 = (bf16[256,768]{1,0:T(8,128)(2,1)S(1)}, bf16[256,768]{1,0:T(8,128)(2,1)}, u32[]{:S(2)}) copy-start(bf16[256,768]{1,0:T(8,128)(2,1)} %wqkv.9) | copy-start | bytes 1179652
  0.7 9.3 %copy-start.4 = (bf16[256,256]{1,0:T(8,128)(2,1)S(1)}, bf16[256,256]{1,0:T(8,128)(2,1)}, u32[]{:S(2)}) copy-start(bf16[256,256]{1,0:T(8,128)(2,1)} %wo.3) | copy-start | bytes 393220
  1.8 11.5 %collective-permute-start.1 = (bf16[3,128,256]{2,1,0:T(8,128)(2,1)S(1)}, bf16[3,128,256]{2,1,0:T(8,128)(2,1)S(1)}, u32[]{:S(2)}, u32[]{:S(2)}) collective-permute-start(bf16[3,128,256]{2,1,0:T(8,128)(2,1)S(1)} %get-tuple-element.96), channel_id=1, source_target_pairs={{4,8},{12,16},{20,24},{28,32},{36,40},{44,48},{52,56},{60,64},{68,... | collective-permute-start | bytes 589832 | tf_op jit(solution)/shard_map/ppermute | solution.py:440
  2.5 10.9 %collective-permute-start = (bf16[3,128,256]{2,1,0:T(8,128)(2,1)S(1)}, bf16[3,128,256]{2,1,0:T(8,128)(2,1)S(1)}, u32[]{:S(2)}, u32[]{:S(2)}) collective-permute-start(bf16[3,128,256]{2,1,0:T(8,128)(2,1)S(1)} %get-tuple-element.97), channel_id=1, source_target_pairs={{0,4},{8,12},{16,20},{24,28},{32,36},{40,44},{48,52},{56,60},{64,6... | collective-permute-start | bytes 589832 | tf_op jit(solution)/shard_map/ppermute | solution.py:439
  9.1 0.7 copy-start.8
  10.0 0.7 copy-start.5
  10.7 0.9 copy-start.2
  13.9 7.6 %collective-permute-start.2 = (bf16[10,8,256]{2,1,0:T(8,128)(2,1)S(1)}, bf16[10,8,256]{2,1,0:T(8,128)(2,1)S(1)}, u32[]{:S(2)}, u32[]{:S(2)}) collective-permute-start(bf16[10,8,256]{2,1,0:T(8,128)(2,1)S(1)} %get-tuple-element.51), channel_id=1, source_target_pairs={{1,2},{2,1},{5,6},{6,5},{9,10},{10,9},{13,14},{14,13},{17,18},{18,... | collective-permute-start | bytes 122888 | tf_op jit(solution)/shard_map/ppermute | solution.py:440
  18.5 3.1 %collective-permute-start.3 = (bf16[10,8,256]{2,1,0:T(8,128)(2,1)S(1)}, bf16[10,8,256]{2,1,0:T(8,128)(2,1)S(1)}, u32[]{:S(2)}, u32[]{:S(2)}) collective-permute-start(bf16[10,8,256]{2,1,0:T(8,128)(2,1)S(1)} %get-tuple-element.52), channel_id=1, source_target_pairs={{0,1},{2,3},{1,0},{3,2},{4,5},{6,7},{5,4},{7,6},{8,9},{10,11},{9,8... | collective-permute-start | bytes 122888 | tf_op jit(solution)/shard_map/ppermute | solution.py:439
  28.9 4.3 %copy-start.6 = (bf16[4,128,256]{2,1,0:T(8,128)(2,1)}, bf16[4,128,256]{2,1,0:T(8,128)(2,1)S(1)}, u32[]{:S(2)}) copy-start(bf16[4,128,256]{2,1,0:T(8,128)(2,1)S(1)} %get-tuple-element.78.g_q) | copy-start | bytes 786436
  28.9 3.5 %collective-permute-start.4 = (bf16[33,32,128]{2,1,0:T(8,128)(2,1)S(1)}, bf16[33,32,128]{2,1,0:T(8,128)(2,1)S(1)}, u32[]{:S(2)}, u32[]{:S(2)}) collective-permute-start(bf16[33,32,128]{2,1,0:T(8,128)(2,1)S(1)} %get-tuple-element.71), channel_id=1, source_target_pairs={{0,1},{1,0},{2,3},{3,2},{4,5},{5,4},{6,7},{7,6},{8,9},{9,8},{10,11... | collective-permute-start | bytes 811016 | tf_op jit(solution)/shard_map/ppermute | solution.py:463
  33.2 22.4 %all-to-all-start = ((bf16[32,40,128]{2,1,0:T(8,128)(2,1)}), bf16[32,40,128]{2,1,0:T(8,128)(2,1)S(1)}, u32[]{:S(2)}, u32[]{:S(2)}) async-start(bf16[32,40,128]{2,1,0:T(8,128)(2,1)} %shard_map.114), calls=%async_computation | async-start | bytes 655360 | tf_op jit(solution)/shard_map/all_to_all | solution.py:467
  41.7 24.6 %collective-permute-start.5 = (bf16[3,144,256]{2,1,0:T(8,128)(2,1)S(1)}, bf16[3,144,256]{2,1,0:T(8,128)(2,1)S(1)}, u32[]{:S(2)}, u32[]{:S(2)}) collective-permute-start(bf16[3,144,256]{2,1,0:T(8,128)(2,1)S(1)} %get-tuple-element.80), channel_id=1, source_target_pairs={{4,8},{12,16},{20,24},{28,32},{36,40},{44,48},{52,56},{60,64},{68,... | collective-permute-start | bytes 663560 | tf_op jit(solution)/shard_map/ppermute | solution.py:440
  42.4 24.0 %collective-permute-start.6 = (bf16[3,144,256]{2,1,0:T(8,128)(2,1)S(1)}, bf16[3,144,256]{2,1,0:T(8,128)(2,1)S(1)}, u32[]{:S(2)}, u32[]{:S(2)}) collective-permute-start(bf16[3,144,256]{2,1,0:T(8,128)(2,1)S(1)} %get-tuple-element.81), channel_id=1, source_target_pairs={{0,4},{8,12},{16,20},{24,28},{32,36},{40,44},{48,52},{56,60},{64,6... | collective-permute-start | bytes 663560 | tf_op jit(solution)/shard_map/ppermute | solution.py:439
  56.3 17.6 %all-to-all-start.1 = ((bf16[8,40,128]{2,1,0:T(8,128)(2,1)}), bf16[8,40,128]{2,1,0:T(8,128)(2,1)S(1)}, u32[]{:S(2)}, u32[]{:S(2)}) async-start(bf16[8,40,128]{2,1,0:T(8,128)(2,1)} %shard_map.115), calls=%async_computation.1 | async-start | bytes 163840 | tf_op jit(solution)/shard_map/all_to_all | solution.py:471
  66.4 1.0 copy-start.7
  74.6 14.1 %copy-start.3 = (bf16[4,128,256]{2,1,0:T(8,128)(2,1)S(1)}, bf16[4,128,256]{2,1,0:T(8,128)(2,1)}, u32[]{:S(2)}) copy-start(bf16[4,128,256]{2,1,0:T(8,128)(2,1)} %cot.5) | copy-start | bytes 786436
  74.6 15.7 %all-to-all-start.2 = ((bf16[32,32,128]{2,1,0:T(8,128)(2,1)}), bf16[32,32,128]{2,1,0:T(8,128)(2,1)S(1)}, u32[]{:S(2)}, u32[]{:S(2)}) async-start(bf16[32,32,128]{2,1,0:T(8,128)(2,1)} %get-tuple-element.87), calls=%async_computation.2 | async-start | bytes 524288 | tf_op jit(solution)/shard_map/all_to_all | solution.py:477
  78.6 9.0 %collective-permute-start.7 = (bf16[4,8,256]{2,1,0:T(8,128)(2,1)S(1)}, bf16[4,8,256]{2,1,0:T(8,128)(2,1)S(1)}, u32[]{:S(2)}, u32[]{:S(2)}) collective-permute-start(bf16[4,8,256]{2,1,0:T(8,128)(2,1)S(1)} %get-tuple-element.89), channel_id=1, source_target_pairs={{1,2},{2,1},{5,6},{6,5},{9,10},{10,9},{13,14},{14,13},{17,18},{18,... | collective-permute-start | bytes 49160 | tf_op jit(solution)/shard_map/ppermute | solution.py:440
  85.7 3.1 %collective-permute-start.8 = (bf16[4,8,256]{2,1,0:T(8,128)(2,1)S(1)}, bf16[4,8,256]{2,1,0:T(8,128)(2,1)S(1)}, u32[]{:S(2)}, u32[]{:S(2)}) collective-permute-start(bf16[4,8,256]{2,1,0:T(8,128)(2,1)S(1)} %get-tuple-element.90), channel_id=1, source_target_pairs={{0,1},{2,3},{1,0},{3,2},{4,5},{6,7},{5,4},{7,6},{8,9},{10,11},{9,8... | collective-permute-start | bytes 49160 | tf_op jit(solution)/shard_map/ppermute | solution.py:439
  90.3 7.7 %collective-permute-start.9 = (bf16[32,32,128]{2,1,0:T(8,128)(2,1)S(1)}, bf16[32,32,128]{2,1,0:T(8,128)(2,1)S(1)}, u32[]{:S(2)}, u32[]{:S(2)}) collective-permute-start(bf16[32,32,128]{2,1,0:T(8,128)(2,1)S(1)} %all-to-all-done.2.mine), channel_id=1, source_target_pairs={{0,1},{1,0},{2,3},{3,2},{4,5},{5,4},{6,7},{7,6},{8,9},{9,8},{10,11... | collective-permute-start | bytes 786440 | tf_op jit(solution)/shard_map/ppermute | solution.py:483

commit v8 on v7

--- a/solution.py
+++ b/solution.py
@@ -32,7 +32,7 @@
 AXIS_SIZES = (8, 2, 8, 2, 2)
 ROWS = ("z", "xh", "y")
 GRP = ("xl", "core")
-SPLIT = ("xh", "y", "xl")
+SPLIT = ("xl", "xh", "y")
 REST = ("z",)
 PARTS = 32
 RESTS = 8

time: 100 us -> 98.5 us (0.985)
  waiting for transfers between devices: 14.7 us -> 12.1 us
    all_to_all x1, starting transfers between devices: 4 us -> 6.64 us  [body(): mine = lax.all_to_all(copies, SPLIT, 0, 0)]
    all_to_all x1, waiting for transfers between devices: 7.61 us -> 5.03 us  [body(): parts = lax.all_to_all(parts, SPLIT, 0, 0)]
    ppermute x1, starting transfers between devices: 6.42 us -> 5.17 us  [body(): other = lax.ppermute(mine, 'core', cores)]
  transfers between devices with their start and end apart: 13 -> 13, of which waited for: 5 -> 6; matrix products, arithmetic and copies ran while one was open for 1% -> 2% of each run, Pallas kernels for 7% -> 7%
where the time goes in v8:
time: 98.5 us; the launch traced here: 97.8 us
  starting transfers between devices  61.1 us (62%)
  Pallas kernels  17.8 us (18%)
  waiting for transfers between devices  12.1 us (12%)
  local copies, waits for them, and re-layouts  5.84 us (6%)
    pallas_call x11, Pallas kernels, call(): pl.pallas_call(fn, out_shape=tuple((jax.ShapeDtypeStruct(s, d) for s, d i...  17.8 us
    ppermute x4, starting transfers between devices, swap(): b = lax.ppermute(b, axes, pairs[1])  16 us
    ppermute x4, starting transfers between devices, swap(): return (lax.ppermute(a, axes, pairs[0]), b)  12.4 us
    all_to_all x1, starting transfers between devices, body(): parts = lax.all_to_all(copies, REST, 0, 0)  10.1 us
    all_to_all x1, starting transfers between devices, body(): parts = lax.all_to_all(parts, SPLIT, 0, 0)  8.52 us
    all_to_all x1, starting transfers between devices, body(): mine = lax.all_to_all(copies, SPLIT, 0, 0)  6.64 us
    ppermute x1, starting transfers between devices, body(): other = lax.ppermute(mine, 'core', cores)  5.17 us
    all_to_all x1, waiting for transfers between devices, body(): parts = lax.all_to_all(parts, SPLIT, 0, 0)  5.03 us
  transfers between devices with their start and end apart: 13, of which 6 were waited for; matrix products, arithmetic and copies ran while one was open for 2% of the time, Pallas kernels for 7%

profile of v8, /device:TPU:1, one launch (start us, length us, event | category | flops | bytes accessed | tf_op | source)
XLA Modules:
  0.0 97.8 jit_solution(11532527472730580708)
XLA Ops:
  0.7 1.1 %constant_dynamic-slice_fusion = (bf16[3,128,256]{2,1,0:T(8,128)(2,1)S(1)}, bf16[3,128,256]{2,1,0:T(8,128)(2,1)S(1)}) fusion(bf16[4,128,256]{2,1,0:T(8,128)(2,1)} %own.7, s32[]{:T(128)S(6)} %select_n.20, s32[]{:T(128)S(6)} %select_n.19), kind=kLoop, calls=%fused_computation.1 | loop fusion | bytes 786440 | tf_op jit(solution)/shard_map/dynamic_slice | solution.py:452
  1.8 0.7 collective-permute-start.1
  2.5 6.6 %collective-permute-start = (bf16[3,128,256]{2,1,0:T(8,128)(2,1)S(1)}, bf16[3,128,256]{2,1,0:T(8,128)(2,1)S(1)}, u32[]{:S(2)}, u32[]{:S(2)}) collective-permute-start(bf16[3,128,256]{2,1,0:T(8,128)(2,1)S(1)} %get-tuple-element.97), channel_id=1, source_target_pairs={{0,4},{8,12},{16,20},{24,28},{32,36},{40,44},{48,52},{56,60},{64,6... | collective-permute-start | bytes 589832 | tf_op jit(solution)/shard_map/ppermute | solution.py:439
  9.1 0.6 copy-done.8
  10.0 0.7 copy-done.5
  10.7 0.9 copy-done.2
  11.6 1.7 %shard_map.110 = (bf16[4,128,256]{2,1,0:T(8,128)(2,1)S(1)}, bf16[4,128,256]{2,1,0:T(8,128)(2,1)S(1)}, bf16[4,128,256]{2,1,0:T(8,128)(2,1)S(1)}, f32[4,128,256]{2...) custom-call(s32[5]{0:T(128)S(1)} %stack.23.place, ...), custom_call_target="tpu_custom_call" | custom-call | flops 3000000000 | bytes 1000000 | tf_op jit(solution)/shard_map/pallas_call | solution.py:384
  13.9 4.5 %collective-permute-start.2 = (bf16[10,8,256]{2,1,0:T(8,128)(2,1)S(1)}, bf16[10,8,256]{2,1,0:T(8,128)(2,1)S(1)}, u32[]{:S(2)}, u32[]{:S(2)}) collective-permute-start(bf16[10,8,256]{2,1,0:T(8,128)(2,1)S(1)} %get-tuple-element.51), channel_id=1, source_target_pairs={{1,2},{2,1},{5,6},{6,5},{9,10},{10,9},{13,14},{14,13},{17,18},{18,... | collective-permute-start | bytes 122888 | tf_op jit(solution)/shard_map/ppermute | solution.py:440
  18.5 1.9 %collective-permute-start.3 = (bf16[10,8,256]{2,1,0:T(8,128)(2,1)S(1)}, bf16[10,8,256]{2,1,0:T(8,128)(2,1)S(1)}, u32[]{:S(2)}, u32[]{:S(2)}) collective-permute-start(bf16[10,8,256]{2,1,0:T(8,128)(2,1)S(1)} %get-tuple-element.52), channel_id=1, source_target_pairs={{0,1},{2,3},{1,0},{3,2},{4,5},{6,7},{5,4},{7,6},{8,9},{10,11},{9,8... | collective-permute-start | bytes 122888 | tf_op jit(solution)/shard_map/ppermute | solution.py:439
  21.6 7.3 %shard_map.113 = (f32[33,32,128]{2,1,0:T(8,128)S(1)}, bf16[33,32,128]{2,1,0:T(8,128)(2,1)S(1)}, bf16[4,128,256]{2,1,0:T(8,128)(2,1)S(1)}, bf16[4,128,256]{2,1,0:...) custom-call(s32[5]{0:T(128)S(1)} %stack.23.place, ...), custom_call_target="tpu_custom_call" | custom-call | flops 8999999488 | bytes 1000000 | tf_op jit(solution)/shard_map/pallas_call | solution.py:384
  28.9 2.4 %collective-permute-start.4 = (bf16[33,32,128]{2,1,0:T(8,128)(2,1)S(1)}, bf16[33,32,128]{2,1,0:T(8,128)(2,1)S(1)}, u32[]{:S(2)}, u32[]{:S(2)}) collective-permute-start(bf16[33,32,128]{2,1,0:T(8,128)(2,1)S(1)} %get-tuple-element.71), channel_id=1, source_target_pairs={{0,1},{1,0},{2,3},{3,2},{4,5},{5,4},{6,7},{7,6},{8,9},{9,8},{10,11... | collective-permute-start | bytes 811016 | tf_op jit(solution)/shard_map/ppermute | solution.py:463
  31.3 1.2 %collective-permute-done.4.received = bf16[33,32,128]{2,1,0:T(8,128)(2,1)S(1)} collective-permute-done((bf16[33,32,128]{2,1,0:T(8,128)(2,1)S(1)}, bf16[33,32,128]{2,1,0:T(8,128)(2,1)S(1)}, u32[]{:S(2)}, u32[]{:S(2)}) %collective-permute-start.4) | collective-permute-done | bytes 270368 | tf_op jit(solution)/shard_map/ppermute | solution.py:463
  32.4 0.8 shard_map.114
  33.2 8.5 %all-to-all-start = ((bf16[32,40,128]{2,1,0:T(8,128)(2,1)}), bf16[32,40,128]{2,1,0:T(8,128)(2,1)S(1)}, u32[]{:S(2)}, u32[]{:S(2)}) async-start(bf16[32,40,128]{2,1,0:T(8,128)(2,1)} %shard_map.114), calls=%async_computation | async-start | bytes 655360 | tf_op jit(solution)/shard_map/all_to_all | solution.py:467
  41.7 0.7 collective-permute-start.5
  42.4 5.6 %collective-permute-start.6 = (bf16[3,144,256]{2,1,0:T(8,128)(2,1)S(1)}, bf16[3,144,256]{2,1,0:T(8,128)(2,1)S(1)}, u32[]{:S(2)}, u32[]{:S(2)}) collective-permute-start(bf16[3,144,256]{2,1,0:T(8,128)(2,1)S(1)} %get-tuple-element.81), channel_id=1, source_target_pairs={{0,4},{8,12},{16,20},{24,28},{32,36},{40,44},{48,52},{56,60},{64,6... | collective-permute-start | bytes 663560 | tf_op jit(solution)/shard_map/ppermute | solution.py:439
  48.0 5.0 %all-to-all-done.parts = bf16[32,40,128]{2,1,0:T(8,128)(2,1)S(1)} async-done(((bf16[32,40,128]{2,1,0:T(8,128)(2,1)}), bf16[32,40,128]{2,1,0:T(8,128)(2,1)S(1)}, u32[]{:S(2)}, u32[]{:S(2)}) %all-to-all-start) | async-done | bytes 327712 | tf_op jit(solution)/shard_map/all_to_all | solution.py:467
  53.0 0.7 shard_map.115
  53.7 10.1 %all-to-all-start.1 = ((bf16[8,40,128]{2,1,0:T(8,128)(2,1)}), bf16[8,40,128]{2,1,0:T(8,128)(2,1)S(1)}, u32[]{:S(2)}, u32[]{:S(2)}) async-start(bf16[8,40,128]{2,1,0:T(8,128)(2,1)} %shard_map.115), calls=%async_computation.1 | async-start | bytes 163840 | tf_op jit(solution)/shard_map/all_to_all | solution.py:471
  63.8 0.9 copy-done.7
  64.7 1.8 %shard_map.116 = (bf16[4,128,256]{2,1,0:T(8,128)(2,1)}, f32[4,128,256]{2,1,0:T(8,128)S(1)}, bf16[4,8,256]{2,1,0:T(8,128)(2,1)S(1)}, bf16[4,8,256]{2,1,0:T(8,128)(2,1)S(1)}) custom-call(s32[5]{0:T(128)S(1)} %stack.23.place, bf16[4,128,256]{2,1,0:T(8,128)(2,1)S(1)} %copy-done, bf16[256,768]{1,0:T(8,128)(2,1)S(1)} %copy-done.1, bf16[256,256]{1,0:T(8,128)(2,1)S(1)} %copy-done.4, ...), custom_call_target="tpu_custom_call" | custom-call | flops 3000000000 | bytes 1000000 | tf_op jit(solution)/shard_map/pallas_call | solution.py:384
  66.5 4.6 %all-to-all-done.1.parts = bf16[8,40,128]{2,1,0:T(8,128)(2,1)S(1)} async-done(((bf16[8,40,128]{2,1,0:T(8,128)(2,1)}), bf16[8,40,128]{2,1,0:T(8,128)(2,1)S(1)}, u32[]{:S(2)}, u32[]{:S(2)}) %all-to-all-start.1) | async-done | bytes 81952 | tf_op jit(solution)/shard_map/all_to_all | solution.py:471
  71.2 0.7 shard_map.117
  71.9 6.6 %all-to-all-start.2 = ((bf16[32,32,128]{2,1,0:T(8,128)(2,1)}), bf16[32,32,128]{2,1,0:T(8,128)(2,1)S(1)}, u32[]{:S(2)}, u32[]{:S(2)}) async-start(bf16[32,32,128]{2,1,0:T(8,128)(2,1)} %get-tuple-element.87), calls=%async_computation.2 | async-start | bytes 524288 | tf_op jit(solution)/shard_map/all_to_all | solution.py:477
  78.5 6.5 %collective-permute-start.7 = (bf16[4,8,256]{2,1,0:T(8,128)(2,1)S(1)}, bf16[4,8,256]{2,1,0:T(8,128)(2,1)S(1)}, u32[]{:S(2)}, u32[]{:S(2)}) collective-permute-start(bf16[4,8,256]{2,1,0:T(8,128)(2,1)S(1)} %get-tuple-element.89), channel_id=1, source_target_pairs={{1,2},{2,1},{5,6},{6,5},{9,10},{10,9},{13,14},{14,13},{17,18},{18,... | collective-permute-start | bytes 49160 | tf_op jit(solution)/shard_map/ppermute | solution.py:440
  85.1 1.9 %collective-permute-start.8 = (bf16[4,8,256]{2,1,0:T(8,128)(2,1)S(1)}, bf16[4,8,256]{2,1,0:T(8,128)(2,1)S(1)}, u32[]{:S(2)}, u32[]{:S(2)}) collective-permute-start(bf16[4,8,256]{2,1,0:T(8,128)(2,1)S(1)} %get-tuple-element.90), channel_id=1, source_target_pairs={{0,1},{2,3},{1,0},{3,2},{4,5},{6,7},{5,4},{7,6},{8,9},{10,11},{9,8... | collective-permute-start | bytes 49160 | tf_op jit(solution)/shard_map/ppermute | solution.py:439
  87.1 1.0 %collective-permute-done.8.from_b = bf16[4,8,256]{2,1,0:T(8,128)(2,1)S(1)} collective-permute-done((bf16[4,8,256]{2,1,0:T(8,128)(2,1)S(1)}, bf16[4,8,256]{2,1,0:T(8,128)(2,1)S(1)}, u32[]{:S(2)}, u32[]{:S(2)}) %collective-permute-start.8) | collective-permute-done | bytes 16416 | tf_op jit(solution)/shard_map/ppermute | solution.py:439
  88.1 1.6 %shard_map.118 = f32[4,128,256]{2,1,0:T(8,128)} custom-call(s32[5]{0:T(128)S(1)} %stack.23.place, bf16[4,128,256]{2,1,0:T(8,128)(2,1)S(1)} %copy-done, bf16[4,128,256]{2,1,0:T(8,128)(2,1)S(1)} %copy-done.3, f32[1,256]{1,0:T(1,128)S(1)} %bitcast.14, f32[4,128,256]{2,1,0:T(8,128)S(1)} %get-tuple-element.88.grad_normed, ...), custom_call_target="tpu_custom_call" | custom-call | flops 2000000000 | bytes 1000000 | tf_op jit(solution)/shard_map/pallas_call | solution.py:384
  89.8 5.2 %collective-permute-start.9 = (bf16[32,32,128]{2,1,0:T(8,128)(2,1)S(1)}, bf16[32,32,128]{2,1,0:T(8,128)(2,1)S(1)}, u32[]{:S(2)}, u32[]{:S(2)}) collective-permute-start(bf16[32,32,128]{2,1,0:T(8,128)(2,1)S(1)} %all-to-all-done.2.mine), channel_id=1, source_target_pairs={{0,1},{1,0},{2,3},{3,2},{4,5},{5,4},{6,7},{7,6},{8,9},{9,8},{10,11... | collective-permute-start | bytes 786440 | tf_op jit(solution)/shard_map/ppermute | solution.py:483
  94.9 0.6 fusion
  95.6 0.6 copy.13
  96.2 1.6 %shard_map.119 = (f32[256,768]{1,0:T(8,128)}, f32[256,256]{1,0:T(8,128)}) custom-call(s32[5]{0:T(128)S(1)} %stack.23.place, bf16[32,32,128]{2,1,0:T(8,128)(2,1)S(1)} %all-to-all-done.2.mine, bf16[32,32,128]{2,1,0:T(8,128)(2,1)S(1)} %collective-permute-done.9.other), custom_call_target="tpu_custom_call" | custom-call | flops 1000000000 | bytes 1000000 | tf_op jit(solution)/shard_map/pallas_call | solution.py:384
  (31 shorter events, 2.2 us)
Async XLA Ops:
  0.7 9.3 %copy-start = (bf16[4,128,256]{2,1,0:T(8,128)(2,1)S(1)}, bf16[4,128,256]{2,1,0:T(8,128)(2,1)}, u32[]{:S(2)}) copy-start(bf16[4,128,256]{2,1,0:T(8,128)(2,1)} %own.7) | copy-start | bytes 786436
  0.7 9.3 %copy-start.1 = (bf16[256,768]{1,0:T(8,128)(2,1)S(1)}, bf16[256,768]{1,0:T(8,128)(2,1)}, u32[]{:S(2)}) copy-start(bf16[256,768]{1,0:T(8,128)(2,1)} %wqkv.9) | copy-start | bytes 1179652
  0.7 9.3 %copy-start.4 = (bf16[256,256]{1,0:T(8,128)(2,1)S(1)}, bf16[256,256]{1,0:T(8,128)(2,1)}, u32[]{:S(2)}) copy-start(bf16[256,256]{1,0:T(8,128)(2,1)} %wo.3) | copy-start | bytes 393220
  1.8 11.5 %collective-permute-start.1 = (bf16[3,128,256]{2,1,0:T(8,128)(2,1)S(1)}, bf16[3,128,256]{2,1,0:T(8,128)(2,1)S(1)}, u32[]{:S(2)}, u32[]{:S(2)}) collective-permute-start(bf16[3,128,256]{2,1,0:T(8,128)(2,1)S(1)} %get-tuple-element.96), channel_id=1, source_target_pairs={{4,8},{12,16},{20,24},{28,32},{36,40},{44,48},{52,56},{60,64},{68,... | collective-permute-start | bytes 589832 | tf_op jit(solution)/shard_map/ppermute | solution.py:440
  2.5 10.9 %collective-permute-start = (bf16[3,128,256]{2,1,0:T(8,128)(2,1)S(1)}, bf16[3,128,256]{2,1,0:T(8,128)(2,1)S(1)}, u32[]{:S(2)}, u32[]{:S(2)}) collective-permute-start(bf16[3,128,256]{2,1,0:T(8,128)(2,1)S(1)} %get-tuple-element.97), channel_id=1, source_target_pairs={{0,4},{8,12},{16,20},{24,28},{32,36},{40,44},{48,52},{56,60},{64,6... | collective-permute-start | bytes 589832 | tf_op jit(solution)/shard_map/ppermute | solution.py:439
  9.1 0.7 copy-start.8
  10.0 0.7 copy-start.5
  10.7 0.9 copy-start.2
  13.9 7.6 %collective-permute-start.2 = (bf16[10,8,256]{2,1,0:T(8,128)(2,1)S(1)}, bf16[10,8,256]{2,1,0:T(8,128)(2,1)S(1)}, u32[]{:S(2)}, u32[]{:S(2)}) collective-permute-start(bf16[10,8,256]{2,1,0:T(8,128)(2,1)S(1)} %get-tuple-element.51), channel_id=1, source_target_pairs={{1,2},{2,1},{5,6},{6,5},{9,10},{10,9},{13,14},{14,13},{17,18},{18,... | collective-permute-start | bytes 122888 | tf_op jit(solution)/shard_map/ppermute | solution.py:440
  18.5 3.1 %collective-permute-start.3 = (bf16[10,8,256]{2,1,0:T(8,128)(2,1)S(1)}, bf16[10,8,256]{2,1,0:T(8,128)(2,1)S(1)}, u32[]{:S(2)}, u32[]{:S(2)}) collective-permute-start(bf16[10,8,256]{2,1,0:T(8,128)(2,1)S(1)} %get-tuple-element.52), channel_id=1, source_target_pairs={{0,1},{2,3},{1,0},{3,2},{4,5},{6,7},{5,4},{7,6},{8,9},{10,11},{9,8... | collective-permute-start | bytes 122888 | tf_op jit(solution)/shard_map/ppermute | solution.py:439
  28.9 4.3 %copy-start.6 = (bf16[4,128,256]{2,1,0:T(8,128)(2,1)}, bf16[4,128,256]{2,1,0:T(8,128)(2,1)S(1)}, u32[]{:S(2)}) copy-start(bf16[4,128,256]{2,1,0:T(8,128)(2,1)S(1)} %get-tuple-element.78.g_q) | copy-start | bytes 786436
  28.9 3.5 %collective-permute-start.4 = (bf16[33,32,128]{2,1,0:T(8,128)(2,1)S(1)}, bf16[33,32,128]{2,1,0:T(8,128)(2,1)S(1)}, u32[]{:S(2)}, u32[]{:S(2)}) collective-permute-start(bf16[33,32,128]{2,1,0:T(8,128)(2,1)S(1)} %get-tuple-element.71), channel_id=1, source_target_pairs={{0,1},{1,0},{2,3},{3,2},{4,5},{5,4},{6,7},{7,6},{8,9},{9,8},{10,11... | collective-permute-start | bytes 811016 | tf_op jit(solution)/shard_map/ppermute | solution.py:463
  33.2 19.8 %all-to-all-start = ((bf16[32,40,128]{2,1,0:T(8,128)(2,1)}), bf16[32,40,128]{2,1,0:T(8,128)(2,1)S(1)}, u32[]{:S(2)}, u32[]{:S(2)}) async-start(bf16[32,40,128]{2,1,0:T(8,128)(2,1)} %shard_map.114), calls=%async_computation | async-start | bytes 655360 | tf_op jit(solution)/shard_map/all_to_all | solution.py:467
  41.7 22.0 %collective-permute-start.5 = (bf16[3,144,256]{2,1,0:T(8,128)(2,1)S(1)}, bf16[3,144,256]{2,1,0:T(8,128)(2,1)S(1)}, u32[]{:S(2)}, u32[]{:S(2)}) collective-permute-start(bf16[3,144,256]{2,1,0:T(8,128)(2,1)S(1)} %get-tuple-element.80), channel_id=1, source_target_pairs={{4,8},{12,16},{20,24},{28,32},{36,40},{44,48},{52,56},{60,64},{68,... | collective-permute-start | bytes 663560 | tf_op jit(solution)/shard_map/ppermute | solution.py:440
  42.4 21.3 %collective-permute-start.6 = (bf16[3,144,256]{2,1,0:T(8,128)(2,1)S(1)}, bf16[3,144,256]{2,1,0:T(8,128)(2,1)S(1)}, u32[]{:S(2)}, u32[]{:S(2)}) collective-permute-start(bf16[3,144,256]{2,1,0:T(8,128)(2,1)S(1)} %get-tuple-element.81), channel_id=1, source_target_pairs={{0,4},{8,12},{16,20},{24,28},{32,36},{40,44},{48,52},{56,60},{64,6... | collective-permute-start | bytes 663560 | tf_op jit(solution)/shard_map/ppermute | solution.py:439
  53.7 17.5 %all-to-all-start.1 = ((bf16[8,40,128]{2,1,0:T(8,128)(2,1)}), bf16[8,40,128]{2,1,0:T(8,128)(2,1)S(1)}, u32[]{:S(2)}, u32[]{:S(2)}) async-start(bf16[8,40,128]{2,1,0:T(8,128)(2,1)} %shard_map.115), calls=%async_computation.1 | async-start | bytes 163840 | tf_op jit(solution)/shard_map/all_to_all | solution.py:471
  63.8 1.0 copy-start.7
  71.9 16.3 %copy-start.3 = (bf16[4,128,256]{2,1,0:T(8,128)(2,1)S(1)}, bf16[4,128,256]{2,1,0:T(8,128)(2,1)}, u32[]{:S(2)}) copy-start(bf16[4,128,256]{2,1,0:T(8,128)(2,1)} %cot.5) | copy-start | bytes 786436
  71.9 17.9 %all-to-all-start.2 = ((bf16[32,32,128]{2,1,0:T(8,128)(2,1)}), bf16[32,32,128]{2,1,0:T(8,128)(2,1)S(1)}, u32[]{:S(2)}, u32[]{:S(2)}) async-start(bf16[32,32,128]{2,1,0:T(8,128)(2,1)} %get-tuple-element.87), calls=%async_computation.2 | async-start | bytes 524288 | tf_op jit(solution)/shard_map/all_to_all | solution.py:477
  78.5 8.6 %collective-permute-start.7 = (bf16[4,8,256]{2,1,0:T(8,128)(2,1)S(1)}, bf16[4,8,256]{2,1,0:T(8,128)(2,1)S(1)}, u32[]{:S(2)}, u32[]{:S(2)}) collective-permute-start(bf16[4,8,256]{2,1,0:T(8,128)(2,1)S(1)} %get-tuple-element.89), channel_id=1, source_target_pairs={{1,2},{2,1},{5,6},{6,5},{9,10},{10,9},{13,14},{14,13},{17,18},{18,... | collective-permute-start | bytes 49160 | tf_op jit(solution)/shard_map/ppermute | solution.py:440
  85.1 3.1 %collective-permute-start.8 = (bf16[4,8,256]{2,1,0:T(8,128)(2,1)S(1)}, bf16[4,8,256]{2,1,0:T(8,128)(2,1)S(1)}, u32[]{:S(2)}, u32[]{:S(2)}) collective-permute-start(bf16[4,8,256]{2,1,0:T(8,128)(2,1)S(1)} %get-tuple-element.90), channel_id=1, source_target_pairs={{0,1},{2,3},{1,0},{3,2},{4,5},{6,7},{5,4},{7,6},{8,9},{10,11},{9,8... | collective-permute-start | bytes 49160 | tf_op jit(solution)/shard_map/ppermute | solution.py:439
  89.8 6.4 %collective-permute-start.9 = (bf16[32,32,128]{2,1,0:T(8,128)(2,1)S(1)}, bf16[32,32,128]{2,1,0:T(8,128)(2,1)S(1)}, u32[]{:S(2)}, u32[]{:S(2)}) collective-permute-start(bf16[32,32,128]{2,1,0:T(8,128)(2,1)S(1)} %all-to-all-done.2.mine), channel_id=1, source_target_pairs={{0,1},{1,0},{2,3},{3,2},{4,5},{5,4},{6,7},{7,6},{8,9},{9,8},{10,11... | collective-permute-start | bytes 786440 | tf_op jit(solution)/shard_map/ppermute | solution.py:483

commit v9 on v8

--- a/solution.py
+++ b/solution.py
@@ -32,7 +32,7 @@
 AXIS_SIZES = (8, 2, 8, 2, 2)
 ROWS = ("z", "xh", "y")
 GRP = ("xl", "core")
-SPLIT = ("xl", "xh", "y")
+SPLIT = ("xh", "xl", "y")
 REST = ("z",)
 PARTS = 32
 RESTS = 8
@@ -246,8 +246,14 @@
     g = q_inv[...].reshape(BR * BC, C) * (factor[...] * grad_query - q_f * mean)
     g = g.astype(BF16)
     g_q[...] = g.reshape(BR, BC, C)
-    acc[3 * C :] = mm(att_b[...].reshape(BR * BC, C), cot[...].reshape(BR * BC, C), ((0,), (0,)))
-    acc[:C] = mm(normed_own[...].reshape(BR * BC, C), g, ((0,), (0,)))
+    def put(block, total):
+        parts = slice(block * (C // PART), (block + 1) * (C // PART))
+        for h in (0, 1):
+            acc[parts, h * PART : h * PART + PART] = total[:, h * 128 : h * 128 + 128].reshape(C // PART, PART, 128)
+
+    put(3, mm(att_b[...].reshape(BR * BC, C), cot[...].reshape(BR * BC, C), ((0,), (0,))))
+    acc_q = mm(normed_own[...].reshape(BR * BC, C), g, ((0,), (0,)))
+    put(0, acc_q)
 
     @pl.loop(0, ER // 2, unroll=ER // 2)
     def _(i):
@@ -266,13 +272,13 @@
         ref[...] = mm(g, wqkv[:, C:], ((1,), (1,))).astype(BF16).reshape(WIN, EC, C)
 
     acc_kv = mm(normed_ext[...].reshape(ER * EC, C), g_kv[...].reshape(ER * EC, 2 * C), ((0,), (0,)))
-    acc[C : 2 * C] = acc_kv[:, :C]
-    acc[2 * C : 3 * C] = acc_kv[:, C:]
+    put(1, acc_kv[:, :C])
+    put(2, acc_kv[:, C:])
 
     by_feature = (
-        wqkv[:, :C].astype(F32) * acc[:C]
-        + wqkv[:, C : 2 * C].astype(F32) * acc[C : 2 * C]
-        + wqkv[:, 2 * C :].astype(F32) * acc[2 * C : 3 * C]
+        wqkv[:, :C].astype(F32) * acc_q
+        + wqkv[:, C : 2 * C].astype(F32) * acc_kv[:, :C]
+        + wqkv[:, 2 * C :].astype(F32) * acc_kv[:, C:]
     )
     high, low = split_bf16(by_feature)
     every = jnp.ones((8, C), BF16)
@@ -280,11 +286,7 @@
     gain_sum = gain_sum[0:1] / gain[...]
 
     for ref, half in ((keep, place[2]), (send, 1 - place[2])):
-        for part in range(PARTS):
-            rows = pl.ds(pl.multiple_of(half * HALF + part * PART, PART), PART)
-            for h in (0, 1):
-                piece = acc[rows, h * 128 : h * 128 + 128]
-                ref[part, h * PART : h * PART + PART] = piece.astype(ref.dtype)
+        ref[:PARTS] = acc[pl.ds(half * PARTS, PARTS)].astype(ref.dtype)
     small = [part.astype(F32) for part in split_bf16(jnp.concatenate([scale_sum, gain_sum], axis=0))]
     small = [a[i : i + 1, h * 128 : h * 128 + 128] for a in small for i in (0, 1) for h in (0, 1)]
     small = jnp.concatenate(small + [jnp.zeros((2 * PART - EXTRA, 128), F32)], axis=0)
@@ -363,7 +365,7 @@
             for part in range(C // PART):
                 rows = slice(part * PART, part * PART + PART)
                 for h in (0, 1):
-                    piece = half[block % 2 * (C // PART) + part, h * PART : h * PART + PART].astype(F32) / GRID
+                    piece = half[block % 2 * (C // PART) + part, h * PART : h * PART + PART].astype(F32) * (1.0 / GRID)
                     if block < 3:
                         qkv[rows, block * C + h * 128 : block * C + h * 128 + 128] = piece
                     else:
@@ -413,7 +415,7 @@
     to_rows = ((WIN, EC, C), BF16)
     outs = [(half, F32), (half, BF16), (OWN, BF16), (OWN, BF16), ((BR, EC, 2 * C), BF16), to_rows, to_rows]
     scratch = [(EXT, BF16)] * 4 + [(EXT, F32)] * 2 + [(OWN, F32), ((ER, EC, 2 * C), BF16)]
-    scratch += [((4 * C, C), F32), ONES]
+    scratch += [((2 * PARTS, 2 * PART, 128), F32), ONES]
     return call(attention_kernel, outs, scratch, 28, 9, place, from_a, from_b, cot, gain, factor, wqkv, *own, *halo)
 
 

time: 98.5 us -> 98.2 us (level)
  no operation moved by 1% of the time
where the time goes in v9:
time: 98.2 us; the launch traced here: 97.5 us
  starting transfers between devices  61.8 us (63%)
  Pallas kernels  17.8 us (18%)
  waiting for transfers between devices  11.3 us (12%)
  local copies, waits for them, and re-layouts  5.84 us (6%)
    pallas_call x11, Pallas kernels, call(): pl.pallas_call(fn, out_shape=tuple((jax.ShapeDtypeStruct(s, d) for s, d i...  17.8 us
    ppermute x4, starting transfers between devices, swap(): b = lax.ppermute(b, axes, pairs[1])  16 us
    ppermute x4, starting transfers between devices, swap(): return (lax.ppermute(a, axes, pairs[0]), b)  12.7 us
    all_to_all x1, starting transfers between devices, body(): parts = lax.all_to_all(copies, REST, 0, 0)  10.1 us
    all_to_all x1, starting transfers between devices, body(): parts = lax.all_to_all(parts, SPLIT, 0, 0)  8.53 us
    all_to_all x1, starting transfers between devices, body(): mine = lax.all_to_all(copies, SPLIT, 0, 0)  7.39 us
    ppermute x1, starting transfers between devices, body(): other = lax.ppermute(mine, 'core', cores)  4.79 us
    all_to_all x1, waiting for transfers between devices, body(): parts = lax.all_to_all(copies, REST, 0, 0)  4.64 us
  transfers between devices with their start and end apart: 13, of which 6 were waited for; matrix products, arithmetic and copies ran while one was open for 2% of the time, Pallas kernels for 7%

profile of v9, /device:TPU:1, one launch (start us, length us, event | category | flops | bytes accessed | tf_op | source)
XLA Modules:
  0.0 97.5 jit_solution(14068484853607306219)
XLA Ops:
  0.7 1.1 %constant_dynamic-slice_fusion = (bf16[3,128,256]{2,1,0:T(8,128)(2,1)S(1)}, bf16[3,128,256]{2,1,0:T(8,128)(2,1)S(1)}) fusion(bf16[4,128,256]{2,1,0:T(8,128)(2,1)} %own.7, s32[]{:T(128)S(6)} %select_n.20, s32[]{:T(128)S(6)} %select_n.19), kind=kLoop, calls=%fused_computation.1 | loop fusion | bytes 786440 | tf_op jit(solution)/shard_map/dynamic_slice | solution.py:454
  1.8 0.7 collective-permute-start.1
  2.5 6.6 %collective-permute-start = (bf16[3,128,256]{2,1,0:T(8,128)(2,1)S(1)}, bf16[3,128,256]{2,1,0:T(8,128)(2,1)S(1)}, u32[]{:S(2)}, u32[]{:S(2)}) collective-permute-start(bf16[3,128,256]{2,1,0:T(8,128)(2,1)S(1)} %get-tuple-element.97), channel_id=1, source_target_pairs={{0,4},{8,12},{16,20},{24,28},{32,36},{40,44},{48,52},{56,60},{64,6... | collective-permute-start | bytes 589832 | tf_op jit(solution)/shard_map/ppermute | solution.py:441
  9.1 0.6 copy-done.8
  10.0 0.7 copy-done.5
  10.7 0.9 copy-done.2
  11.6 1.7 %shard_map.110 = (bf16[4,128,256]{2,1,0:T(8,128)(2,1)S(1)}, bf16[4,128,256]{2,1,0:T(8,128)(2,1)S(1)}, bf16[4,128,256]{2,1,0:T(8,128)(2,1)S(1)}, f32[4,128,256]{2...) custom-call(s32[5]{0:T(128)S(1)} %stack.23.place, ...), custom_call_target="tpu_custom_call" | custom-call | flops 3000000000 | bytes 1000000 | tf_op jit(solution)/shard_map/pallas_call | solution.py:386
  13.9 4.5 %collective-permute-start.2 = (bf16[10,8,256]{2,1,0:T(8,128)(2,1)S(1)}, bf16[10,8,256]{2,1,0:T(8,128)(2,1)S(1)}, u32[]{:S(2)}, u32[]{:S(2)}) collective-permute-start(bf16[10,8,256]{2,1,0:T(8,128)(2,1)S(1)} %get-tuple-element.51), channel_id=1, source_target_pairs={{1,2},{2,1},{5,6},{6,5},{9,10},{10,9},{13,14},{14,13},{17,18},{18,... | collective-permute-start | bytes 122888 | tf_op jit(solution)/shard_map/ppermute | solution.py:442
  18.5 1.9 %collective-permute-start.3 = (bf16[10,8,256]{2,1,0:T(8,128)(2,1)S(1)}, bf16[10,8,256]{2,1,0:T(8,128)(2,1)S(1)}, u32[]{:S(2)}, u32[]{:S(2)}) collective-permute-start(bf16[10,8,256]{2,1,0:T(8,128)(2,1)S(1)} %get-tuple-element.52), channel_id=1, source_target_pairs={{0,1},{2,3},{1,0},{3,2},{4,5},{6,7},{5,4},{7,6},{8,9},{10,11},{9,8... | collective-permute-start | bytes 122888 | tf_op jit(solution)/shard_map/ppermute | solution.py:441
  21.6 7.2 %shard_map.113 = (f32[33,32,128]{2,1,0:T(8,128)S(1)}, bf16[33,32,128]{2,1,0:T(8,128)(2,1)S(1)}, bf16[4,128,256]{2,1,0:T(8,128)(2,1)S(1)}, bf16[4,128,256]{2,1,0:...) custom-call(s32[5]{0:T(128)S(1)} %stack.23.place, ...), custom_call_target="tpu_custom_call" | custom-call | flops 8999999488 | bytes 1000000 | tf_op jit(solution)/shard_map/pallas_call | solution.py:386
  28.8 2.4 %collective-permute-start.4 = (bf16[33,32,128]{2,1,0:T(8,128)(2,1)S(1)}, bf16[33,32,128]{2,1,0:T(8,128)(2,1)S(1)}, u32[]{:S(2)}, u32[]{:S(2)}) collective-permute-start(bf16[33,32,128]{2,1,0:T(8,128)(2,1)S(1)} %get-tuple-element.71), channel_id=1, source_target_pairs={{0,1},{1,0},{2,3},{3,2},{4,5},{5,4},{6,7},{7,6},{8,9},{9,8},{10,11... | collective-permute-start | bytes 811016 | tf_op jit(solution)/shard_map/ppermute | solution.py:465
  31.2 1.2 %collective-permute-done.4.received = bf16[33,32,128]{2,1,0:T(8,128)(2,1)S(1)} collective-permute-done((bf16[33,32,128]{2,1,0:T(8,128)(2,1)S(1)}, bf16[33,32,128]{2,1,0:T(8,128)(2,1)S(1)}, u32[]{:S(2)}, u32[]{:S(2)}) %collective-permute-start.4) | collective-permute-done | bytes 270368 | tf_op jit(solution)/shard_map/ppermute | solution.py:465
  32.4 0.8 shard_map.114
  33.1 8.5 %all-to-all-start = ((bf16[32,40,128]{2,1,0:T(8,128)(2,1)}), bf16[32,40,128]{2,1,0:T(8,128)(2,1)S(1)}, u32[]{:S(2)}, u32[]{:S(2)}) async-start(bf16[32,40,128]{2,1,0:T(8,128)(2,1)} %shard_map.114), calls=%async_computation | async-start | bytes 655360 | tf_op jit(solution)/shard_map/all_to_all | solution.py:469
  41.7 0.7 collective-permute-start.5
  42.4 5.6 %collective-permute-start.6 = (bf16[3,144,256]{2,1,0:T(8,128)(2,1)S(1)}, bf16[3,144,256]{2,1,0:T(8,128)(2,1)S(1)}, u32[]{:S(2)}, u32[]{:S(2)}) collective-permute-start(bf16[3,144,256]{2,1,0:T(8,128)(2,1)S(1)} %get-tuple-element.81), channel_id=1, source_target_pairs={{0,4},{8,12},{16,20},{24,28},{32,36},{40,44},{48,52},{56,60},{64,6... | collective-permute-start | bytes 663560 | tf_op jit(solution)/shard_map/ppermute | solution.py:441
  47.9 4.2 %all-to-all-done.parts = bf16[32,40,128]{2,1,0:T(8,128)(2,1)S(1)} async-done(((bf16[32,40,128]{2,1,0:T(8,128)(2,1)}), bf16[32,40,128]{2,1,0:T(8,128)(2,1)S(1)}, u32[]{:S(2)}, u32[]{:S(2)}) %all-to-all-start) | async-done | bytes 327712 | tf_op jit(solution)/shard_map/all_to_all | solution.py:469
  52.1 0.7 shard_map.115
  52.8 10.1 %all-to-all-start.1 = ((bf16[8,40,128]{2,1,0:T(8,128)(2,1)}), bf16[8,40,128]{2,1,0:T(8,128)(2,1)S(1)}, u32[]{:S(2)}, u32[]{:S(2)}) async-start(bf16[8,40,128]{2,1,0:T(8,128)(2,1)} %shard_map.115), calls=%async_computation.1 | async-start | bytes 163840 | tf_op jit(solution)/shard_map/all_to_all | solution.py:473
  62.9 0.9 copy-done.7
  63.9 1.8 %shard_map.116 = (bf16[4,128,256]{2,1,0:T(8,128)(2,1)}, f32[4,128,256]{2,1,0:T(8,128)S(1)}, bf16[4,8,256]{2,1,0:T(8,128)(2,1)S(1)}, bf16[4,8,256]{2,1,0:T(8,128)(2,1)S(1)}) custom-call(s32[5]{0:T(128)S(1)} %stack.23.place, bf16[4,128,256]{2,1,0:T(8,128)(2,1)S(1)} %copy-done, bf16[256,768]{1,0:T(8,128)(2,1)S(1)} %copy-done.1, bf16[256,256]{1,0:T(8,128)(2,1)S(1)} %copy-done.4, ...), custom_call_target="tpu_custom_call" | custom-call | flops 3000000000 | bytes 1000000 | tf_op jit(solution)/shard_map/pallas_call | solution.py:386
  65.7 4.6 %all-to-all-done.1.parts = bf16[8,40,128]{2,1,0:T(8,128)(2,1)S(1)} async-done(((bf16[8,40,128]{2,1,0:T(8,128)(2,1)}), bf16[8,40,128]{2,1,0:T(8,128)(2,1)S(1)}, u32[]{:S(2)}, u32[]{:S(2)}) %all-to-all-start.1) | async-done | bytes 81952 | tf_op jit(solution)/shard_map/all_to_all | solution.py:473
  70.3 0.7 shard_map.117
  71.0 7.4 %all-to-all-start.2 = ((bf16[32,32,128]{2,1,0:T(8,128)(2,1)}), bf16[32,32,128]{2,1,0:T(8,128)(2,1)S(1)}, u32[]{:S(2)}, u32[]{:S(2)}) async-start(bf16[32,32,128]{2,1,0:T(8,128)(2,1)} %get-tuple-element.87), calls=%async_computation.2 | async-start | bytes 524288 | tf_op jit(solution)/shard_map/all_to_all | solution.py:479
  78.4 6.8 %collective-permute-start.7 = (bf16[4,8,256]{2,1,0:T(8,128)(2,1)S(1)}, bf16[4,8,256]{2,1,0:T(8,128)(2,1)S(1)}, u32[]{:S(2)}, u32[]{:S(2)}) collective-permute-start(bf16[4,8,256]{2,1,0:T(8,128)(2,1)S(1)} %get-tuple-element.89), channel_id=1, source_target_pairs={{1,2},{2,1},{5,6},{6,5},{9,10},{10,9},{13,14},{14,13},{17,18},{18,... | collective-permute-start | bytes 49160 | tf_op jit(solution)/shard_map/ppermute | solution.py:442
  85.2 1.9 %collective-permute-start.8 = (bf16[4,8,256]{2,1,0:T(8,128)(2,1)S(1)}, bf16[4,8,256]{2,1,0:T(8,128)(2,1)S(1)}, u32[]{:S(2)}, u32[]{:S(2)}) collective-permute-start(bf16[4,8,256]{2,1,0:T(8,128)(2,1)S(1)} %get-tuple-element.90), channel_id=1, source_target_pairs={{0,1},{2,3},{1,0},{3,2},{4,5},{6,7},{5,4},{7,6},{8,9},{10,11},{9,8... | collective-permute-start | bytes 49160 | tf_op jit(solution)/shard_map/ppermute | solution.py:441
  87.3 1.0 %collective-permute-done.8.from_b = bf16[4,8,256]{2,1,0:T(8,128)(2,1)S(1)} collective-permute-done((bf16[4,8,256]{2,1,0:T(8,128)(2,1)S(1)}, bf16[4,8,256]{2,1,0:T(8,128)(2,1)S(1)}, u32[]{:S(2)}, u32[]{:S(2)}) %collective-permute-start.8) | collective-permute-done | bytes 16416 | tf_op jit(solution)/shard_map/ppermute | solution.py:441
  88.3 1.6 %shard_map.118 = f32[4,128,256]{2,1,0:T(8,128)} custom-call(s32[5]{0:T(128)S(1)} %stack.23.place, bf16[4,128,256]{2,1,0:T(8,128)(2,1)S(1)} %copy-done, bf16[4,128,256]{2,1,0:T(8,128)(2,1)S(1)} %copy-done.3, f32[1,256]{1,0:T(1,128)S(1)} %bitcast.14, f32[4,128,256]{2,1,0:T(8,128)S(1)} %get-tuple-element.88.grad_normed, ...), custom_call_target="tpu_custom_call" | custom-call | flops 2000000000 | bytes 1000000 | tf_op jit(solution)/shard_map/pallas_call | solution.py:386
  89.9 4.8 %collective-permute-start.9 = (bf16[32,32,128]{2,1,0:T(8,128)(2,1)S(1)}, bf16[32,32,128]{2,1,0:T(8,128)(2,1)S(1)}, u32[]{:S(2)}, u32[]{:S(2)}) collective-permute-start(bf16[32,32,128]{2,1,0:T(8,128)(2,1)S(1)} %all-to-all-done.2.mine), channel_id=1, source_target_pairs={{0,1},{1,0},{2,3},{3,2},{4,5},{5,4},{6,7},{7,6},{8,9},{9,8},{10,11... | collective-permute-start | bytes 786440 | tf_op jit(solution)/shard_map/ppermute | solution.py:485
  94.7 0.6 fusion
  95.3 0.6 copy.13
  95.9 1.6 %shard_map.119 = (f32[256,768]{1,0:T(8,128)}, f32[256,256]{1,0:T(8,128)}) custom-call(s32[5]{0:T(128)S(1)} %stack.23.place, bf16[32,32,128]{2,1,0:T(8,128)(2,1)S(1)} %all-to-all-done.2.mine, bf16[32,32,128]{2,1,0:T(8,128)(2,1)S(1)} %collective-permute-done.9.other), custom_call_target="tpu_custom_call" | custom-call | flops 1000000000 | bytes 1000000 | tf_op jit(solution)/shard_map/pallas_call | solution.py:386
  (31 shorter events, 2.3 us)
Async XLA Ops:
  0.7 9.3 %copy-start = (bf16[4,128,256]{2,1,0:T(8,128)(2,1)S(1)}, bf16[4,128,256]{2,1,0:T(8,128)(2,1)}, u32[]{:S(2)}) copy-start(bf16[4,128,256]{2,1,0:T(8,128)(2,1)} %own.7) | copy-start | bytes 786436
  0.7 9.3 %copy-start.1 = (bf16[256,768]{1,0:T(8,128)(2,1)S(1)}, bf16[256,768]{1,0:T(8,128)(2,1)}, u32[]{:S(2)}) copy-start(bf16[256,768]{1,0:T(8,128)(2,1)} %wqkv.9) | copy-start | bytes 1179652
  0.7 9.3 %copy-start.4 = (bf16[256,256]{1,0:T(8,128)(2,1)S(1)}, bf16[256,256]{1,0:T(8,128)(2,1)}, u32[]{:S(2)}) copy-start(bf16[256,256]{1,0:T(8,128)(2,1)} %wo.3) | copy-start | bytes 393220
  1.8 11.5 %collective-permute-start.1 = (bf16[3,128,256]{2,1,0:T(8,128)(2,1)S(1)}, bf16[3,128,256]{2,1,0:T(8,128)(2,1)S(1)}, u32[]{:S(2)}, u32[]{:S(2)}) collective-permute-start(bf16[3,128,256]{2,1,0:T(8,128)(2,1)S(1)} %get-tuple-element.96), channel_id=1, source_target_pairs={{4,8},{12,16},{20,24},{28,32},{36,40},{44,48},{52,56},{60,64},{68,... | collective-permute-start | bytes 589832 | tf_op jit(solution)/shard_map/ppermute | solution.py:442
  2.5 10.9 %collective-permute-start = (bf16[3,128,256]{2,1,0:T(8,128)(2,1)S(1)}, bf16[3,128,256]{2,1,0:T(8,128)(2,1)S(1)}, u32[]{:S(2)}, u32[]{:S(2)}) collective-permute-start(bf16[3,128,256]{2,1,0:T(8,128)(2,1)S(1)} %get-tuple-element.97), channel_id=1, source_target_pairs={{0,4},{8,12},{16,20},{24,28},{32,36},{40,44},{48,52},{56,60},{64,6... | collective-permute-start | bytes 589832 | tf_op jit(solution)/shard_map/ppermute | solution.py:441
  9.1 0.7 copy-start.8
  10.0 0.7 copy-start.5
  10.7 0.9 copy-start.2
  13.9 7.6 %collective-permute-start.2 = (bf16[10,8,256]{2,1,0:T(8,128)(2,1)S(1)}, bf16[10,8,256]{2,1,0:T(8,128)(2,1)S(1)}, u32[]{:S(2)}, u32[]{:S(2)}) collective-permute-start(bf16[10,8,256]{2,1,0:T(8,128)(2,1)S(1)} %get-tuple-element.51), channel_id=1, source_target_pairs={{1,2},{2,1},{5,6},{6,5},{9,10},{10,9},{13,14},{14,13},{17,18},{18,... | collective-permute-start | bytes 122888 | tf_op jit(solution)/shard_map/ppermute | solution.py:442
  18.5 3.1 %collective-permute-start.3 = (bf16[10,8,256]{2,1,0:T(8,128)(2,1)S(1)}, bf16[10,8,256]{2,1,0:T(8,128)(2,1)S(1)}, u32[]{:S(2)}, u32[]{:S(2)}) collective-permute-start(bf16[10,8,256]{2,1,0:T(8,128)(2,1)S(1)} %get-tuple-element.52), channel_id=1, source_target_pairs={{0,1},{2,3},{1,0},{3,2},{4,5},{6,7},{5,4},{7,6},{8,9},{10,11},{9,8... | collective-permute-start | bytes 122888 | tf_op jit(solution)/shard_map/ppermute | solution.py:441
  28.8 4.3 %copy-start.6 = (bf16[4,128,256]{2,1,0:T(8,128)(2,1)}, bf16[4,128,256]{2,1,0:T(8,128)(2,1)S(1)}, u32[]{:S(2)}) copy-start(bf16[4,128,256]{2,1,0:T(8,128)(2,1)S(1)} %get-tuple-element.78.g_q) | copy-start | bytes 786436
  28.8 3.5 %collective-permute-start.4 = (bf16[33,32,128]{2,1,0:T(8,128)(2,1)S(1)}, bf16[33,32,128]{2,1,0:T(8,128)(2,1)S(1)}, u32[]{:S(2)}, u32[]{:S(2)}) collective-permute-start(bf16[33,32,128]{2,1,0:T(8,128)(2,1)S(1)} %get-tuple-element.71), channel_id=1, source_target_pairs={{0,1},{1,0},{2,3},{3,2},{4,5},{5,4},{6,7},{7,6},{8,9},{9,8},{10,11... | collective-permute-start | bytes 811016 | tf_op jit(solution)/shard_map/ppermute | solution.py:465
  33.1 19.0 %all-to-all-start = ((bf16[32,40,128]{2,1,0:T(8,128)(2,1)}), bf16[32,40,128]{2,1,0:T(8,128)(2,1)S(1)}, u32[]{:S(2)}, u32[]{:S(2)}) async-start(bf16[32,40,128]{2,1,0:T(8,128)(2,1)} %shard_map.114), calls=%async_computation | async-start | bytes 655360 | tf_op jit(solution)/shard_map/all_to_all | solution.py:469
  41.7 21.2 %collective-permute-start.5 = (bf16[3,144,256]{2,1,0:T(8,128)(2,1)S(1)}, bf16[3,144,256]{2,1,0:T(8,128)(2,1)S(1)}, u32[]{:S(2)}, u32[]{:S(2)}) collective-permute-start(bf16[3,144,256]{2,1,0:T(8,128)(2,1)S(1)} %get-tuple-element.80), channel_id=1, source_target_pairs={{4,8},{12,16},{20,24},{28,32},{36,40},{44,48},{52,56},{60,64},{68,... | collective-permute-start | bytes 663560 | tf_op jit(solution)/shard_map/ppermute | solution.py:442
  42.4 20.5 %collective-permute-start.6 = (bf16[3,144,256]{2,1,0:T(8,128)(2,1)S(1)}, bf16[3,144,256]{2,1,0:T(8,128)(2,1)S(1)}, u32[]{:S(2)}, u32[]{:S(2)}) collective-permute-start(bf16[3,144,256]{2,1,0:T(8,128)(2,1)S(1)} %get-tuple-element.81), channel_id=1, source_target_pairs={{0,4},{8,12},{16,20},{24,28},{32,36},{40,44},{48,52},{56,60},{64,6... | collective-permute-start | bytes 663560 | tf_op jit(solution)/shard_map/ppermute | solution.py:441
  52.8 17.5 %all-to-all-start.1 = ((bf16[8,40,128]{2,1,0:T(8,128)(2,1)}), bf16[8,40,128]{2,1,0:T(8,128)(2,1)S(1)}, u32[]{:S(2)}, u32[]{:S(2)}) async-start(bf16[8,40,128]{2,1,0:T(8,128)(2,1)} %shard_map.115), calls=%async_computation.1 | async-start | bytes 163840 | tf_op jit(solution)/shard_map/all_to_all | solution.py:473
  62.9 1.0 copy-start.7
  71.0 17.2 %copy-start.3 = (bf16[4,128,256]{2,1,0:T(8,128)(2,1)S(1)}, bf16[4,128,256]{2,1,0:T(8,128)(2,1)}, u32[]{:S(2)}) copy-start(bf16[4,128,256]{2,1,0:T(8,128)(2,1)} %cot.5) | copy-start | bytes 786436
  71.0 18.9 %all-to-all-start.2 = ((bf16[32,32,128]{2,1,0:T(8,128)(2,1)}), bf16[32,32,128]{2,1,0:T(8,128)(2,1)S(1)}, u32[]{:S(2)}, u32[]{:S(2)}) async-start(bf16[32,32,128]{2,1,0:T(8,128)(2,1)} %get-tuple-element.87), calls=%async_computation.2 | async-start | bytes 524288 | tf_op jit(solution)/shard_map/all_to_all | solution.py:479
  78.4 8.8 %collective-permute-start.7 = (bf16[4,8,256]{2,1,0:T(8,128)(2,1)S(1)}, bf16[4,8,256]{2,1,0:T(8,128)(2,1)S(1)}, u32[]{:S(2)}, u32[]{:S(2)}) collective-permute-start(bf16[4,8,256]{2,1,0:T(8,128)(2,1)S(1)} %get-tuple-element.89), channel_id=1, source_target_pairs={{1,2},{2,1},{5,6},{6,5},{9,10},{10,9},{13,14},{14,13},{17,18},{18,... | collective-permute-start | bytes 49160 | tf_op jit(solution)/shard_map/ppermute | solution.py:442
  85.2 3.1 %collective-permute-start.8 = (bf16[4,8,256]{2,1,0:T(8,128)(2,1)S(1)}, bf16[4,8,256]{2,1,0:T(8,128)(2,1)S(1)}, u32[]{:S(2)}, u32[]{:S(2)}) collective-permute-start(bf16[4,8,256]{2,1,0:T(8,128)(2,1)S(1)} %get-tuple-element.90), channel_id=1, source_target_pairs={{0,1},{2,3},{1,0},{3,2},{4,5},{6,7},{5,4},{7,6},{8,9},{10,11},{9,8... | collective-permute-start | bytes 49160 | tf_op jit(solution)/shard_map/ppermute | solution.py:441
  89.9 6.0 %collective-permute-start.9 = (bf16[32,32,128]{2,1,0:T(8,128)(2,1)S(1)}, bf16[32,32,128]{2,1,0:T(8,128)(2,1)S(1)}, u32[]{:S(2)}, u32[]{:S(2)}) collective-permute-start(bf16[32,32,128]{2,1,0:T(8,128)(2,1)S(1)} %all-to-all-done.2.mine), channel_id=1, source_target_pairs={{0,1},{1,0},{2,3},{3,2},{4,5},{5,4},{6,7},{7,6},{8,9},{9,8},{10,11... | collective-permute-start | bytes 786440 | tf_op jit(solution)/shard_map/ppermute | solution.py:485
